TPU v7x, 32 devices: a whole 2x2x4 slice. The times are simulated.
32 devices in a mesh: groups: 2 (over x), patch: 4 (over y, core), feat: 4 (over z).
Axes of the slice: x: 2, y: 2, z: 4, core: 2. Of those that a mesh axis runs over, the one named last changes fastest.
Arguments:
- node_lat: bfloat16 [8192, 512], P(('groups', 'patch', 'feat')), parts along dimension 0, may hold values from -6 to 6
- edge_lat: bfloat16 [8192, 8, 512], P(('groups', 'patch', 'feat')), parts along dimension 0, may hold values from -6 to 6
- neighbours: int32 [8, 4096], P(None, ('patch', 'feat')), may hold values from 0 to 1280, as said below
- send_rows: int32 [1024], P('patch'), may hold values from 0 to 1023
- coarse_of: int32 [4096], P(('patch', 'feat')), may hold values from 0 to 63
- weight_in: bfloat16 [1536, 512], replicated, may hold values from -0.15625 to 0.15625
- bias_in: float32 [512], replicated, may hold values from -3 to 3
- weight_out: bfloat16 [512, 512], replicated, may hold values from -0.25 to 0.25
- norm_gain: float32 [512], replicated, may hold values from 0.1 to 1.9
- edge_cotangent: bfloat16 [8192, 8, 512], P(('groups', 'patch', 'feat')), parts along dimension 0, may hold values from -6 to 6
- node_cotangent: bfloat16 [8192, 512], P(('groups', 'patch', 'feat')), parts along dimension 0, may hold values from -6 to 6
Outputs:
- edge_new: bfloat16 [8192, 8, 512], P(('groups', 'patch', 'feat')), parts along dimension 0
- node_new: bfloat16 [8192, 512], P(('groups', 'patch', 'feat')), parts along dimension 0
- grad_edge: bfloat16 [8192, 8, 512], P(('groups', 'patch', 'feat')), parts along dimension 0
- grad_node: bfloat16 [8192, 512], P(('groups', 'patch', 'feat')), parts along dimension 0
- grad_weight_in: float32 [3072, 512], P(('groups', 'patch'), 'feat'), parts along dimension 0
- grad_weight_out: float32 [1024, 512], P(('groups', 'patch'), 'feat'), parts along dimension 0
There are 2 independent parts, one for each index of `groups`. A program takes and returns all parts, laid end to end along the dimension named above; an argument that names none is the same for every part. Nothing has to cross between parts.
Inputs may be any that keep to these rules, and one draw needn't show every extreme that they name: `neighbours`: value 1024 + 2 * 128 marks an empty slot; smaller values index a patch's 1024 rows, then the 128 rows from the lower patch, then the 128 rows from the upper patch.
All inputs are finite; a program needn't handle non-finite values.
Results may differ from a plain program's by a relative error of at most 0.0049.
Values may be sent and summed in bfloat16 or wider, within the bound.
No kernel may reach another device: no remote copies, remote signals or barrier semaphores. Data moves between devices by JAX's collectives and lax.ppermute only.
A program may use at most 128 MiB of HBM per device.

v0:
```python
import math

import jax
import jax.numpy as jnp
from jax import lax
from jax.sharding import PartitionSpec as P

COARSE_DEV = 4


LAYER_EPS = 1e-05


def with_halo(shard, sides, width):
    for axis, dim in sides:
        devices, length = (lax.axis_size(axis), shard.shape[dim])
        up = [(i, (i + 1) % devices) for i in range(devices)]
        down = [(j, i) for i, j in up]
        last = lax.slice_in_dim(shard, length - width, length, axis=dim)
        initial = lax.slice_in_dim(shard, 0, width, axis=dim)
        before = lax.ppermute(last, axis, up)
        after = lax.ppermute(initial, axis, down)
        shard = jnp.concatenate([before, shard, after], axis=dim)
    return shard


def swish_terms(preact):
    sigmoid_value = jax.nn.sigmoid(preact)
    return (preact * sigmoid_value, sigmoid_value * (1.0 + preact * (1.0 - sigmoid_value)))


def edge_block(
    own_nodes,
    edge_rows,
    sources,
    live_slots,
    edge_cot,
    node_cot,
    weight_in,
    bias_in,
    weight_out,
    norm_gain,
):
    node_count, degree, latent = edge_rows.shape
    hidden = weight_in.shape[1]
    edge_total = node_count * degree
    flat_edges = edge_rows.reshape(edge_total, latent)
    flat_sources = sources.reshape(edge_total, latent)
    node_term = jnp.dot(own_nodes, weight_in[2 * latent :], preferred_element_type=jnp.float32)
    preact = jnp.dot(flat_edges, weight_in[:latent], preferred_element_type=jnp.float32)
    preact = preact + jnp.dot(
        flat_sources, weight_in[latent : 2 * latent], preferred_element_type=jnp.float32
    )
    preact = preact.reshape(node_count, degree, hidden) + node_term[:, None, :] + bias_in
    activation, slope_term = swish_terms(preact.reshape(edge_total, hidden))
    hidden_act = activation.astype(jnp.bfloat16)
    projected = jnp.dot(hidden_act, weight_out, preferred_element_type=jnp.float32)
    centre = projected - jnp.mean(projected, axis=1, keepdims=True)
    inverse = lax.rsqrt(jnp.mean(centre * centre, axis=1, keepdims=True) + LAYER_EPS)
    normed = centre * inverse
    message = (normed * norm_gain).reshape(node_count, degree, latent)
    edge_cotan = edge_cot.astype(jnp.float32)
    edge_new = (edge_rows.astype(jnp.float32) + message).astype(jnp.bfloat16)
    aggregate = jnp.sum(message * live_slots[:, :, None], axis=1)
    grad_message = edge_cotan + live_slots[:, :, None] * node_cot.astype(jnp.float32)[:, None, :]
    scaled = grad_message.reshape(edge_total, latent) * norm_gain
    grad_projected = inverse * (
        scaled
        - jnp.mean(scaled, axis=1, keepdims=True)
        - normed * jnp.mean(scaled * normed, axis=1, keepdims=True)
    )
    grad_projected = grad_projected.astype(jnp.bfloat16)
    contract_cols = (((1,), (1,)), ((), ()))
    contract_rows = (((0,), (0,)), ((), ()))
    grad_hidden = lax.dot_general(
        grad_projected, weight_out, contract_cols, preferred_element_type=jnp.float32
    )
    grad_preact = (grad_hidden * slope_term).astype(jnp.bfloat16)
    grad_inputs = lax.dot_general(
        grad_preact, weight_in, contract_cols, preferred_element_type=jnp.float32
    )
    grad_edge = (edge_cotan + grad_inputs[:, :latent].reshape(node_count, degree, latent)).astype(
        jnp.bfloat16
    )
    grad_sources = grad_inputs[:, latent : 2 * latent]
    grad_own = jnp.sum(grad_inputs[:, 2 * latent :].reshape(node_count, degree, latent), axis=1)
    preact_sum = jnp.sum(grad_preact.reshape(node_count, degree, hidden), axis=1, dtype=jnp.float32)
    grad_weight_in = jnp.concatenate(
        [
            lax.dot_general(
                flat_edges, grad_preact, contract_rows, preferred_element_type=jnp.float32
            ),
            lax.dot_general(
                flat_sources, grad_preact, contract_rows, preferred_element_type=jnp.float32
            ),
            lax.dot_general(
                own_nodes.astype(jnp.float32),
                preact_sum,
                contract_rows,
                precision=lax.Precision.HIGHEST,
                preferred_element_type=jnp.float32,
            ),
        ],
        axis=0,
    )
    grad_weight_out = lax.dot_general(
        hidden_act, grad_projected, contract_rows, preferred_element_type=jnp.float32
    )
    return (edge_new, aggregate, grad_edge, grad_own, grad_sources, grad_weight_in, grad_weight_out)


def shards(
    node_lat,
    edge_lat,
    neighbours,
    send_rows,
    coarse_of,
    weight_in,
    bias_in,
    weight_out,
    norm_gain,
    edge_cotangent,
    node_cotangent,
):
    node_count, latent = node_lat.shape
    degree = edge_lat.shape[1]
    rim_rows = send_rows.shape[0] // 2
    feat_count = lax.axis_size("feat")
    patch_count = lax.axis_size("patch")
    coarse_total = COARSE_DEV * patch_count * feat_count
    unit_terms = jnp.ones((node_count,), jnp.float32)
    local_sums = (
        jax.ops.segment_sum(node_lat.astype(jnp.float32), coarse_of, coarse_total),
        jax.ops.segment_sum(node_cotangent.astype(jnp.float32), coarse_of, coarse_total),
        jax.ops.segment_sum(unit_terms, coarse_of, coarse_total),
    )
    pooled_sum, spread_sum, counts = lax.psum(
        (local_sums[0], local_sums[1], local_sums[2]), ("patch", "feat")
    )
    divisor = jnp.maximum(counts, 1.0)[:, None]
    pooled = pooled_sum / divisor
    spread = spread_sum / divisor
    patch_table = lax.all_gather(node_lat, "feat", axis=0, tiled=True)
    patch_total = patch_table.shape[0]
    table_rows = patch_total + 2 * rim_rows
    outgoing = patch_table[send_rows]
    padded_rims = with_halo(outgoing, (("patch", 0),), rim_rows)
    received = jnp.concatenate([padded_rims[:rim_rows], padded_rims[3 * rim_rows :]], axis=0)
    blank_row = jnp.zeros((1, latent), node_lat.dtype)
    full_table = jnp.concatenate([patch_table, received, blank_row], axis=0)
    neighbour_ids = neighbours.T
    sources = full_table[neighbour_ids]
    live_slots = (neighbour_ids != table_rows).astype(jnp.float32)
    results = edge_block(
        node_lat,
        edge_lat,
        sources,
        live_slots,
        edge_cotangent,
        node_cotangent,
        weight_in,
        bias_in,
        weight_out,
        norm_gain,
    )
    edge_new, aggregate, grad_edge, grad_own, grad_sources, grad_weight_in, grad_weight_out = (
        results
    )
    table_grad = jax.ops.segment_sum(grad_sources, neighbour_ids.reshape(-1), table_rows + 1)
    patch_grad = table_grad[:patch_total]
    rim_grad = table_grad[patch_total:table_rows]
    padded_grads = with_halo(rim_grad.astype(jnp.bfloat16), (("patch", 0),), rim_rows).astype(
        rim_grad.dtype
    )
    returned = jnp.concatenate([padded_grads[:rim_rows], padded_grads[3 * rim_rows :]], axis=0)
    patch_grad = patch_grad + jax.ops.segment_sum(returned, send_rows, patch_total)
    own_grad = lax.psum_scatter(patch_grad, "feat", scatter_dimension=0, tiled=True)
    node_new = (node_lat.astype(jnp.float32) + aggregate + pooled[coarse_of]).astype(jnp.bfloat16)
    grad_node = (
        node_cotangent.astype(jnp.float32) + grad_own + own_grad + spread[coarse_of]
    ).astype(jnp.bfloat16)
    section_in, section_out = (
        lax.psum_scatter(grad_weight_in, "patch", scatter_dimension=0, tiled=True),
        lax.psum_scatter(grad_weight_out, "patch", scatter_dimension=0, tiled=True),
    )
    reduced_in, reduced_out = (
        lax.psum_scatter(section_in, "feat", scatter_dimension=1, tiled=True),
        lax.psum_scatter(section_out, "feat", scatter_dimension=1, tiled=True),
    )
    grad_scale = 1.0 / math.sqrt(node_count * degree * patch_count * feat_count)
    return (
        edge_new,
        node_new,
        grad_edge,
        grad_node,
        reduced_in * grad_scale,
        reduced_out * grad_scale,
    )


def solution(mesh):
    return jax.shard_map(
        shards,
        mesh=mesh,
        in_specs=(
            P(("groups", "patch", "feat"), None),
            P(("groups", "patch", "feat"), None, None),
            P(None, ("patch", "feat")),
            P("patch"),
            P(("patch", "feat")),
            P(),
            P(),
            P(),
            P(),
            P(("groups", "patch", "feat"), None, None),
            P(("groups", "patch", "feat"), None),
        ),
        out_specs=(
            P(("groups", "patch", "feat"), None, None),
            P(("groups", "patch", "feat"), None),
            P(("groups", "patch", "feat"), None, None),
            P(("groups", "patch", "feat"), None),
            P(("groups", "patch"), "feat"),
            P(("groups", "patch"), "feat"),
        ),
        check_vma=False,
    )
```

profile of v0, /device:TPU:0, one launch (start us, length us, event | category | flops | bytes accessed | tf_op | source)
XLA Modules:
  0.0 263.0 jit_solution(18018908360420039252)
XLA Ops:
  12.3 2.2 fusion.23
  14.5 4.2 %fusion.9 = f32[2048,512]{1,0:T(8,128)} fusion(bf16[256,8,512]{2,1,0:T(8,128)(2,1)S(1)} %copy-done.5, bf16[1536,512]{1,0:T(8,128)(2,1)} %param.16), kind=kOutput, calls=%fused_computation.36 | convolution fusion | flops 1073741824 | bytes 6815744 | tf_op jit(solution)/shard_map/dot_general | solution.py:50
  18.7 22.3 %all-gather.2.cloned.1.call-done = bf16[1024,512]{1,0:T(8,128)(2,1)} async-done(((bf16[256,512]{1,0:T(8,128)(2,1)}), bf16[1024,512]{1,0:T(8,128)(2,1)}) %all-gather.2.cloned.1.call-update) | async-done | bytes 1048592 | tf_op jit(solution)/shard_map/all_gather | solution.py:143
  41.1 2.6 gather_fusion
  45.5 2.6 %collective-permute-done = bf16[128,512]{1,0:T(8,128)(2,1)S(1)} collective-permute-done((bf16[128,512]{1,0:T(8,128)(2,1)S(1)}, bf16[128,512]{1,0:T(8,128)(2,1)S(1)}, u32[]{:S(2)}, u32[]{:S(2)}) %collective-permute-start) | collective-permute-done | bytes 131104 | tf_op jit(solution)/shard_map/ppermute | solution.py:21
  50.1 9.2 %gather_fusion.1 = bf16[2048,512]{1,0:T(8,128)(2,1)} fusion(bf16[1281,512]{1,0:T(8,128)(2,1)S(1)} %maximum_maximum_fusion, s32[2048]{0:T(1024)S(1)} %broadcast_clamp_fusion), kind=kCustom, calls=%fused_computation.1 | custom fusion | bytes 4202496 | tf_op jit(solution)/shard_map/gather | solution.py:152
  59.3 7.0 %multiply_convert_fusion.2 = (bf16[2048,512]{1,0:T(8,128)(2,1)S(1)}, f32[2048,512]{1,0:T(8,128)}) fusion(f32[512]{0:T(512)S(1)} %copy-done.17, f32[256,512]{1,0:T(8,128)} %fusion.23, f32[2048,512]{1,0:T(8,128)} %fusion.9, bf16[2048,512]{1,0:T(8,128)(2,1)} %gather_fusion.1, bf16[1536,512]{1,0:T(8,128)(2,1)} %param.16), kind=kOutput, calls=%fused_computation.30 | convolution fusion | flops 1082130432 | bytes 13633536 | tf_op jit(solution)/shard_map/dot_general | solution.py:51
  70.0 2.2 copy-done.3
  74.2 6.3 %multiply_reduce_fusion.1 = (f32[256,8]{1,0:T(8,128)S(1)}, f32[256,512]{1,0:T(8,128)}, bf16[256,8,512]{2,1,0:T(8,128)(2,1)}) fusion(bf16[256,8,512]{2,1,0:T(8,128)(2,1)S(1)} %copy-done.3, f32[512]{0:T(512)S(1)} %copy-done.15, f32[256,512]{1,0:T(8,128)S(1)} %convert_element_type.57, f32[256,8]{1,0:T(8,128)S(1)} %copy.19, f32[2048]{0:T(1024)S(1)} %add_rsqrt_fusion, ...), kind=kLoop, calls=%fused_computation.28 | loop fusion | flops 13498368 | bytes 11569152 | tf_op jit(solution)/shard_map/reduce_sum | solution.py:69
  80.6 4.0 %multiply_convert_fusion.1 = bf16[2048,512]{1,0:T(8,128)(2,1)S(1)} fusion(bf16[256,8,512]{2,1,0:T(8,128)(2,1)S(1)} %copy-done.3, f32[2048,512]{1,0:T(8,128)} %copy-done.2, f32[2048]{0:T(1024)S(1)} %broadcast_multiply_fusion.3, f32[2048]{0:T(1024)S(1)} %div.37, f32[256,512]{1,0:T(8,128)S(1)} %convert_element_type.57, f32[256,8]{1,0:T(8,128)S(1)} %copy.19, ...), kind=kLoop, calls=%fused_computation.26 | loop fusion | flops 11534336 | bytes 8955904 | tf_op jit(solution)/shard_map/convert_element_type | solution.py:72
  86.0 2.3 fusion.39
  88.5 5.3 %convert_reduce_fusion = (f32[256,512]{1,0:T(8,128)S(1)}, bf16[2048,512]{1,0:T(8,128)(2,1)S(1)}) fusion(f32[2048,512]{1,0:T(8,128)} %get-tuple-element.22, bf16[2048,512]{1,0:T(8,128)(2,1)} %copy-done.13, bf16[512,512]{1,0:T(8,128)(2,1)S(1)} %copy-done), kind=kOutput, calls=%fused_computation.17 | convolution fusion | flops 1085145088 | bytes 9437184 | tf_op jit(solution)/shard_map/dot_general | solution.py:75
  100.6 2.7 %scatter_custom_fusion.4 = f32[64,512]{1,0:T(8,128)} fusion(s32[256]{0:T(256)S(1)} %copy-done.16, bf16[256,512]{1,0:T(8,128)(2,1)S(1)} %copy-done.11, f32[]{:T(128)} %constant.16.clone.1), kind=kCustom, calls=%fused_computation.56 | custom fusion | flops 262144 | bytes 393220 | tf_op jit(solution)/shard_map/scatter-add | solution.py:134
  103.4 2.7 %scatter_custom_fusion = f32[64,512]{1,0:T(8,128)} fusion(s32[256]{0:T(256)S(1)} %copy-done.16, bf16[256,512]{1,0:T(8,128)(2,1)S(1)} %copy-done.8, f32[]{:T(128)} %constant.16.clone.1), kind=kCustom, calls=%fused_computation.42 | custom fusion | flops 262144 | bytes 393220 | tf_op jit(solution)/shard_map/scatter-add | solution.py:133
  106.4 6.9 %reduce-scatter.12.cloned.1.call-done = f32[128,512]{1,0:T(8,128)} async-done(((f32[512,512]{1,0:T(8,128)}), f32[128,512]{1,0:T(8,128)}) %reduce-scatter.12.cloned.1.call-update) | async-done | bytes 262160 | tf_op jit(solution)/shard_map/reduce_scatter | solution.py:184
  113.6 11.0 %fusion.37 = f32[2048,1536]{1,0:T(8,128)} fusion(bf16[2048,512]{1,0:T(8,128)(2,1)} %copy-done.18, bf16[1536,512]{1,0:T(8,128)(2,1)} %param.16), kind=kOutput, calls=%fused_computation.85 | convolution fusion | flops 3221225472 | bytes 16252928 | tf_op jit(solution)/shard_map/dot_general | solution.py:79
  124.6 15.2 %scatter_custom_fusion.2 = f32[1281,512]{1,0:T(8,128)} fusion(s32[2048]{0:T(1024)S(1)} %reshape.129, f32[2048,1536]{1,0:T(8,128)} %fusion.37, f32[]{:T(128)} %constant.16.clone.1), kind=kCustom, calls=%fused_computation.12 | custom fusion | flops 1048576 | bytes 6818304 | tf_op jit(solution)/shard_map/scatter-add | solution.py:169
  145.2 5.3 %collective-permute-done.2 = bf16[128,512]{1,0:T(8,128)(2,1)S(1)} collective-permute-done((bf16[128,512]{1,0:T(8,128)(2,1)S(1)}, bf16[128,512]{1,0:T(8,128)(2,1)S(1)}, u32[]{:S(2)}, u32[]{:S(2)}) %collective-permute-start.2) | collective-permute-done | bytes 131104 | tf_op jit(solution)/shard_map/ppermute | solution.py:21
  150.6 5.1 %scatter_custom_fusion.3 = f32[1024,512]{1,0:T(8,128)} fusion(f32[1024,512]{1,0:T(8,128)} %slice.72, s32[256]{0:T(256)} %param.14, f32[128,512]{1,0:T(8,128)S(1)} %get-tuple-element.16, f32[]{:T(128)} %constant.7, f32[128,512]{1,0:T(8,128)S(1)} %get-tuple-element.15), kind=kCustom, calls=%fused_computation.47 | custom fusion | flops 262144 | bytes 2621952 | tf_op jit(solution)/shard_map/scatter-add | solution.py:176
  155.8 2.3 scatter_custom_fusion.1
  158.1 34.3 %psum.22 = f32[64]{0:T(128)S(1)} all-reduce(f32[64]{0:T(128)S(1)} %scatter_custom_fusion.1), channel_id=1, replica_groups=mesh['groups'=2,'patch'=4,'feat'=4] {'patch','feat'}, use_global_device_ids=true, to_apply=%region_6.0 | all-reduce | flops 64 | bytes 512 | tf_op jit(solution)/shard_map/psum | solution.py:137
  192.4 44.7 %all-reduce.3.cloned.1.call-done = (f32[64,512]{1,0:T(8,128)}, f32[64,512]{1,0:T(8,128)}) async-done(((f32[64,512]{1,0:T(8,128)}, f32[64,512]{1,0:T(8,128)}), (f32[64,512]{1,0:T(8,128)}, f32[64,512]{1,0:T(8,128)})) %all-reduce.3.cloned.1.call-update) | async-done | bytes 262160 | tf_op jit(solution)/shard_map/psum | solution.py:137
  243.8 6.4 %fusion.3 = (f32[256,512]{1,0:T(8,128)}, bf16[256,8,512]{2,1,0:T(8,128)(2,1)}) fusion(f32[2048,1536]{1,0:T(8,128)} %fusion.37, bf16[256,8,512]{2,1,0:T(8,128)(2,1)S(1)} %copy-done.3), kind=kLoop, calls=%fused_computation.15 | loop fusion | flops 4063232 | bytes 13107200 | tf_op jit(solution)/shard_map/reduce_sum | solution.py:86
  251.7 2.2 add_convert_fusion
  (102 shorter events, 37.8 us)
Async XLA Ops:
  8.0 59.8 %copy-start = (bf16[512,512]{1,0:T(8,128)(2,1)S(1)}, bf16[512,512]{1,0:T(8,128)(2,1)}, u32[]{:S(2)}) copy-start(bf16[512,512]{1,0:T(8,128)(2,1)} %param.18) | copy-start | bytes 1572868
  8.0 6.5 %copy-start.5 = (bf16[256,8,512]{2,1,0:T(8,128)(2,1)S(1)}, bf16[256,8,512]{2,1,0:T(8,128)(2,1)}, u32[]{:S(2)}) copy-start(bf16[256,8,512]{2,1,0:T(8,128)(2,1)} %param.12) | copy-start | bytes 6291460
  8.0 33.1 %all-gather.2.cloned.1.call-start = ((), (), s32[]{:S(2)}) async-start(), calls=%async_computation.5 | async-start | bytes 1310720 | tf_op jit(solution)/shard_map/all_gather | solution.py:143
  8.8 104.6 %reduce-scatter.12.cloned.1.call-start = ((), (), s32[]{:S(2)}) async-start(), calls=%async_computation.9 | async-start | bytes 1310720 | tf_op jit(solution)/shard_map/reduce_scatter | solution.py:184
  43.7 4.4 %collective-permute-start = (bf16[128,512]{1,0:T(8,128)(2,1)S(1)}, bf16[128,512]{1,0:T(8,128)(2,1)S(1)}, u32[]{:S(2)}, u32[]{:S(2)}) collective-permute-start(bf16[128,512]{1,0:T(8,128)(2,1)S(1)} %get-tuple-element.17), channel_id=1, source_target_pairs={{0,4},{4,8},{8,12},{12,0},{1,5},{5,9},{9,13},{13,1},{2,6},{6,10},{... | collective-permute-start | bytes 393224 | tf_op jit(solution)/shard_map/ppermute | solution.py:21
  43.8 4.8 %collective-permute-start.1 = (bf16[128,512]{1,0:T(8,128)(2,1)S(1)}, bf16[128,512]{1,0:T(8,128)(2,1)S(1)}, u32[]{:S(2)}, u32[]{:S(2)}) collective-permute-start(bf16[128,512]{1,0:T(8,128)(2,1)S(1)} %get-tuple-element.18), channel_id=1, source_target_pairs={{4,0},{8,4},{12,8},{0,12},{5,1},{9,5},{13,9},{1,13},{6,2},{10,6},{... | collective-permute-start | bytes 393224 | tf_op jit(solution)/shard_map/ppermute | solution.py:22
  50.1 9.2 %copy-start.17 = (f32[512]{0:T(512)S(1)}, f32[512]{0:T(512)}, u32[]{:S(2)}) copy-start(f32[512]{0:T(512)} %param.17) | copy-start | bytes 6148
  69.1 5.1 %copy-start.2 = (f32[2048,512]{1,0:T(8,128)}, f32[2048,512]{1,0:T(8,128)S(1)}, u32[]{:S(2)}) copy-start(f32[2048,512]{1,0:T(8,128)S(1)} %get-tuple-element.24) | copy-start | bytes 12582916
  69.1 3.1 %copy-start.3 = (bf16[256,8,512]{2,1,0:T(8,128)(2,1)S(1)}, bf16[256,8,512]{2,1,0:T(8,128)(2,1)}, u32[]{:S(2)}) copy-start(bf16[256,8,512]{2,1,0:T(8,128)(2,1)} %param.20) | copy-start | bytes 6291460
  69.1 3.1 %copy-start.15 = (f32[512]{0:T(512)S(1)}, f32[512]{0:T(512)}, u32[]{:S(2)}) copy-start(f32[512]{0:T(512)} %param.19) | copy-start | bytes 6148
  80.6 5.4 %copy-start.10 = (bf16[2048,512]{1,0:T(8,128)(2,1)S(1)}, bf16[2048,512]{1,0:T(8,128)(2,1)}, u32[]{:S(2)}) copy-start(bf16[2048,512]{1,0:T(8,128)(2,1)} %copy-done.9) | copy-start | bytes 6291460
  88.3 104.1 %reduce-scatter.8.cloned.1.call-start = ((), (), s32[]{:S(2)}) async-start(), calls=%async_computation.7 | async-start | bytes 3932160 | tf_op jit(solution)/shard_map/reduce_scatter | solution.py:183
  88.5 5.4 %copy-start.8 = (bf16[256,512]{1,0:T(8,128)(2,1)S(1)}, bf16[256,512]{1,0:T(8,128)(2,1)}, u32[]{:S(2)}) copy-start(bf16[256,512]{1,0:T(8,128)(2,1)} %param.11) | copy-start | bytes 786436
  88.5 6.0 %copy-start.12 = (bf16[2048,512]{1,0:T(8,128)(2,1)S(1)}, bf16[2048,512]{1,0:T(8,128)(2,1)}, u32[]{:S(2)}) copy-start(bf16[2048,512]{1,0:T(8,128)(2,1)} %gather_fusion.1) | copy-start | bytes 6291460
  93.9 2.0 copy-start.18
  99.7 6.5 %copy-start.14 = (s32[8,256]{1,0:T(8,128)S(1)}, s32[8,256]{1,0:T(8,128)}, u32[]{:S(2)}) copy-start(s32[8,256]{1,0:T(8,128)} %param.13) | copy-start | bytes 24580
  99.7 137.5 %all-reduce.3.cloned.1.call-start = ((), (), s32[]{:S(2)}) async-start(), calls=%async_computation.11 | async-start | bytes 524288 | tf_op jit(solution)/shard_map/psum | solution.py:137
  106.1 144.1 %reduce-scatter.14.cloned.1.call-start = ((), (), s32[]{:S(2)}) async-start(), calls=%async_computation.10 | async-start | bytes 327680 | tf_op jit(solution)/shard_map/reduce_scatter | solution.py:188
  113.4 138.3 %reduce-scatter.6.cloned.1.call-start = ((), (), s32[]{:S(2)}) async-start(), calls=%async_computation.6 | async-start | bytes 2621440 | tf_op jit(solution)/shard_map/reduce_scatter | solution.py:177
  139.8 3.9 %copy-start.4 = (f32[1281,512]{1,0:T(8,128)S(1)}, f32[1281,512]{1,0:T(8,128)}, u32[]{:S(2)}) copy-start(f32[1281,512]{1,0:T(8,128)} %scatter_custom_fusion.2) | copy-start | bytes 7870468
  141.9 8.6 %collective-permute-start.2 = (bf16[128,512]{1,0:T(8,128)(2,1)S(1)}, bf16[128,512]{1,0:T(8,128)(2,1)S(1)}, u32[]{:S(2)}, u32[]{:S(2)}) collective-permute-start(bf16[128,512]{1,0:T(8,128)(2,1)S(1)} %get-tuple-element.13), channel_id=1, source_target_pairs={{0,4},{4,8},{8,12},{12,0},{1,5},{5,9},{9,13},{13,1},{2,6},{6,10},{... | collective-permute-start | bytes 393224 | tf_op jit(solution)/shard_map/ppermute | solution.py:21
  142.0 8.6 %collective-permute-start.3 = (bf16[128,512]{1,0:T(8,128)(2,1)S(1)}, bf16[128,512]{1,0:T(8,128)(2,1)S(1)}, u32[]{:S(2)}, u32[]{:S(2)}) collective-permute-start(bf16[128,512]{1,0:T(8,128)(2,1)S(1)} %get-tuple-element.14), channel_id=1, source_target_pairs={{4,0},{8,4},{12,8},{0,12},{5,1},{9,5},{13,9},{1,13},{6,2},{10,6},{... | collective-permute-start | bytes 393224 | tf_op jit(solution)/shard_map/ppermute | solution.py:22
  155.7 98.2 %reduce-scatter.10.cloned.1.call-start = ((), (), s32[]{:S(2)}) async-start(), calls=%async_computation.8 | async-start | bytes 983040 | tf_op jit(solution)/shard_map/reduce_scatter | solution.py:187
  243.8 11.8 %copy-start.1 = (bf16[512,512]{1,0:T(8,128)(2,1)S(1)}, bf16[512,512]{1,0:T(8,128)(2,1)}, u32[]{:S(2)}) copy-start(bf16[512,512]{1,0:T(8,128)(2,1)} %param.18) | copy-start | bytes 1572868
  (6 other events, 8.4 us)
Sparse Core Ops, SparseCore 0:
  10.4 30.6 all-gather.1
  88.4 24.8 reduce-scatter.11
  116.0 40.9 reduce-scatter.7
  159.1 19.8 reduce-scatter.13
  181.3 42.8 reduce-scatter.5
  226.3 22.8 reduce-scatter.9
Sparse Core Ops, SparseCore 1:
  106.2 130.9 all-reduce.2
where the time goes:
time: 264 us; the launch traced here: 263 us
  waiting for transfers between devices  83.1 us (31%)
  other arithmetic  64.8 us (25%)
  matrix products  36.7 us (14%)
  blocking collectives  34.3 us (13%)
  local copies, waits for them, and re-layouts  24 us (9%)
  between operations  15.9 us (6%)
  starting transfers between devices  4.26 us (2%)
    psum x1, waiting for transfers between devices, shards(): lax.psum((local_sums[0], local_sums[1], local_sums[2]), ('patch', 'feat'))  44.7 us
    psum x1, blocking collectives, shards(): lax.psum((local_sums[0], local_sums[1], local_sums[2]), ('patch', 'feat'))  34.3 us
    all_gather x1, waiting for transfers between devices, shards(): patch_table = lax.all_gather(node_lat, 'feat', axis=0, tiled=True)  22.3 us
    scatter-add x1, other arithmetic, shards(): jax.ops.segment_sum(grad_sources, neighbour_ids.reshape(-1), table_rows + 1)  15.2 us
    dot_general x1, matrix products, edge_block(): lax.dot_general(grad_preact, weight_in, contract_cols, preferred_element_...  11 us
    gather x1, local copies, waits for them, and re-layouts, shards(): sources = full_table[neighbour_ids]  9.21 us
    ppermute x2, waiting for transfers between devices, with_halo(): before = lax.ppermute(last, axis, up)  7.95 us
    dot_general x1, matrix products, edge_block(): jnp.dot(flat_sources, weight_in[latent:2 * latent], preferred_element_typ...  7.03 us
  transfers between devices with their start and end apart: 11, of which 6 were waited for; matrix products, arithmetic and copies ran while one was open for 30% of the time, Pallas kernels for 0%

commit v1 on v0

v1 whole, which is shorter than its diff:
```python
import math

import jax
import jax.numpy as jnp
from jax import lax
from jax.experimental import pallas as pl
from jax.experimental.pallas import tpu as pltpu
from jax.sharding import PartitionSpec as P

COARSE_DEV = 4
LAYER_EPS = 1e-05
F32 = jnp.float32
BF16 = jnp.bfloat16
VMEM_LIMIT = 56 * 1024 * 1024
COLS = (((1,), (1,)), ((), ()))
ROWS = (((0,), (0,)), ((), ()))


def dot(a, b):
    return jnp.dot(a, b, preferred_element_type=F32)


def params():
    return pltpu.CompilerParams(vmem_limit_bytes=VMEM_LIMIT)


def cost(flops, bytes_accessed):
    return pl.CostEstimate(flops=int(flops), bytes_accessed=int(bytes_accessed), transcendentals=0)


def whole(array):
    zeros = (0,) * array.ndim
    return pl.BlockSpec(array.shape, lambda i: zeros)


def rows(array, block):
    rest = (0,) * (array.ndim - 1)
    return pl.BlockSpec((block,) + array.shape[1:], lambda i: (i,) + rest)


def one_hot(ids, first, count):
    lanes = lax.broadcasted_iota(jnp.int32, (ids.shape[0], count), 1) + first
    return jnp.where(ids == lanes, 1.0, 0.0).astype(BF16)


def base_kernel(degree, edge_ref, node_ref, ids_ref, own_ref, weight_ref, bias_ref, out_ref, table):
    latent = own_ref.shape[1]

    @pl.when(pl.program_id(0) == 0)
    def _():
        table[...] = dot(own_ref[...], weight_ref[latent : 2 * latent]).astype(BF16)

    edges = edge_ref.shape[0]
    term = dot(node_ref[...], weight_ref[2 * latent :]) + bias_ref[...]
    total = dot(edge_ref[...], weight_ref[:latent])
    total = total + dot(one_hot(ids_ref[...], 0, own_ref.shape[0]), table[...])
    hidden = total.shape[1]
    total = total.reshape(edges // degree, degree, hidden) + term[:, None, :]
    out_ref[...] = total.reshape(edges, hidden)


def base_call(edges, nodes, ids, weight_in, bias, block):
    count, latent = edges.shape
    hidden = weight_in.shape[1]
    degree = count // nodes.shape[0]
    return pl.pallas_call(
        lambda *refs: base_kernel(degree, *refs),
        grid=(count // block,),
        in_specs=[
            rows(edges, block),
            rows(nodes, block // degree),
            rows(ids, block),
            whole(nodes),
            whole(weight_in),
            whole(bias),
        ],
        out_specs=pl.BlockSpec((block, hidden), lambda i: (i, 0)),
        out_shape=jax.ShapeDtypeStruct((count, hidden), F32),
        scratch_shapes=[pltpu.VMEM(nodes.shape, BF16)],
        compiler_params=params(),
        cost_estimate=cost(2 * count * hidden * (latent + nodes.shape[0]), count * 3072),
        name="base_terms",
    )(edges, nodes, ids, nodes, weight_in, bias)


def gather_kernel(first, base_ref, ids_ref, piece_ref, weight_ref, out_ref, table):
    latent = piece_ref.shape[1]

    @pl.when(pl.program_id(0) == 0)
    def _():
        table[...] = dot(piece_ref[...], weight_ref[latent : 2 * latent]).astype(BF16)

    hot = one_hot(ids_ref[...], first, piece_ref.shape[0])
    out_ref[...] = base_ref[...] + dot(hot, table[...])


def gather_call(base, ids, piece, weight_in, first, block):
    count, hidden = base.shape
    return pl.pallas_call(
        lambda *refs: gather_kernel(first, *refs),
        grid=(count // block,),
        in_specs=[rows(base, block), rows(ids, block), whole(piece), whole(weight_in)],
        out_specs=rows(base, block),
        out_shape=jax.ShapeDtypeStruct(base.shape, F32),
        scratch_shapes=[pltpu.VMEM((piece.shape[0], hidden), BF16)],
        input_output_aliases={0: 0},
        compiler_params=params(),
        cost_estimate=cost(2 * count * hidden * piece.shape[0], count * 4096),
        name="gather_terms",
    )(base, ids, piece, weight_in)


def select_kernel(ids_ref, table_ref, out_ref):
    hot = one_hot(ids_ref[...], 0, table_ref.shape[0])
    out_ref[...] = dot(hot, table_ref[...]).astype(out_ref.dtype)


def select_call(ids, table):
    return pl.pallas_call(
        select_kernel,
        out_shape=jax.ShapeDtypeStruct((ids.shape[0], table.shape[1]), BF16),
        compiler_params=params(),
        cost_estimate=cost(2 * ids.shape[0] * table.shape[0] * table.shape[1], 1 << 21),
        name="select_rows",
    )(ids, table)


def edge_kernel(
    first,
    degree,
    base_ref,
    ids_ref,
    rim_ref,
    edge_ref,
    cot_ref,
    ncot_ref,
    weight_ref,
    out_w_ref,
    gain_ref,
    new_ref,
    agg_ref,
    hid_ref,
    gproj_ref,
    gpre_ref,
    psum_ref,
    gedge_ref,
    table,
):
    latent = rim_ref.shape[1]

    @pl.when(pl.program_id(0) == 0)
    def _():
        table[...] = dot(rim_ref[...], weight_ref[latent : 2 * latent]).astype(BF16)

    ids = ids_ref[...]
    edges = ids.shape[0]
    nodes = edges // degree
    limit = first + rim_ref.shape[0]
    live = jnp.where(ids < limit, 1.0, 0.0)
    value = base_ref[...] + dot(one_hot(ids, first, rim_ref.shape[0]), table[...])
    sig = jax.nn.sigmoid(value)
    act = value * sig
    slope = sig + act * (1.0 - sig)
    hid = act.astype(BF16)
    hid_ref[...] = hid
    projected = dot(hid, out_w_ref[...])
    centre = projected - jnp.mean(projected, axis=1, keepdims=True)
    inverse = lax.rsqrt(jnp.mean(centre * centre, axis=1, keepdims=True) + LAYER_EPS)
    normed = centre * inverse
    gain = gain_ref[...]
    message = normed * gain
    new_ref[...] = (edge_ref[...].astype(F32) + message).astype(BF16)
    agg_ref[...] = jnp.sum((message * live).reshape(nodes, degree, latent), axis=1)
    ncot = jnp.broadcast_to(ncot_ref[...].astype(F32)[:, None, :], (nodes, degree, latent))
    cot = cot_ref[...].astype(F32)
    scaled = (cot + live * ncot.reshape(edges, latent)) * gain
    mean_a = jnp.mean(scaled, axis=1, keepdims=True)
    mean_b = jnp.mean(scaled * normed, axis=1, keepdims=True)
    gproj = (inverse * (scaled - mean_a - normed * mean_b)).astype(BF16)
    gproj_ref[...] = gproj
    gpre = (lax.dot_general(gproj, out_w_ref[...], COLS, preferred_element_type=F32) * slope).astype(BF16)
    gpre_ref[...] = gpre
    psum_ref[...] = jnp.sum(gpre.astype(F32).reshape(nodes, degree, gpre.shape[1]), axis=1).astype(BF16)
    back = lax.dot_general(gpre, weight_ref[:latent], COLS, preferred_element_type=F32)
    gedge_ref[...] = (cot + back).astype(BF16)


def edge_call(base, ids, rim, edges, cots, ncot, weight_in, weight_out, gain, first, block):
    count, latent = edges.shape
    hidden = weight_in.shape[1]
    degree = count // ncot.shape[0]
    blocks = count // block
    small = block // degree

    def like(width, dtype, size, total):
        return (
            pl.BlockSpec((size, width), lambda i: (i, 0)),
            jax.ShapeDtypeStruct((total, width), dtype),
        )

    outs = [
        like(latent, BF16, block, count),
        like(latent, F32, small, count // degree),
        like(hidden, BF16, block, count),
        like(latent, BF16, block, count),
        like(hidden, BF16, block, count),
        like(hidden, BF16, small, count // degree),
        like(latent, BF16, block, count),
    ]
    return pl.pallas_call(
        lambda *refs: edge_kernel(first, degree, *refs),
        grid=(blocks,),
        in_specs=[
            rows(base, block),
            rows(ids, block),
            whole(rim),
            rows(edges, block),
            rows(cots, block),
            rows(ncot, small),
            whole(weight_in),
            whole(weight_out),
            whole(gain),
        ],
        out_specs=[spec for spec, _ in outs],
        out_shape=[shape for _, shape in outs],
        scratch_shapes=[pltpu.VMEM((rim.shape[0], hidden), BF16)],
        compiler_params=params(),
        cost_estimate=cost(2 * count * hidden * (3 * latent + rim.shape[0]), count * 10000),
        name="edge_block",
    )(base, ids, rim, edges, cots, ncot, weight_in, weight_out, gain)


def scatter_kernel(first, ids_ref, values_ref, out_ref):
    size = out_ref.shape[0]
    start = first + pl.program_id(0) * size
    places = lax.broadcasted_iota(jnp.int32, (size, ids_ref.shape[1]), 0) + start
    hot = jnp.where(places == ids_ref[...], 1.0, 0.0).astype(BF16)
    out_ref[...] = dot(hot, values_ref[...]).astype(out_ref.dtype)


def scatter_call(ids, values, first, count, block, dtype):
    width = values.shape[1]
    return pl.pallas_call(
        lambda *refs: scatter_kernel(first, *refs),
        grid=(count // block,),
        in_specs=[whole(ids), whole(values)],
        out_specs=pl.BlockSpec((block, width), lambda i: (i, 0)),
        out_shape=jax.ShapeDtypeStruct((count, width), dtype),
        compiler_params=params(),
        cost_estimate=cost(2 * count * width * values.shape[0], values.size * 2 + count * width * 4),
        name="scatter_rows",
    )(ids, values)


def scatter_more_kernel(ids_ref, values_ref, start_ref, out_ref):
    size = out_ref.shape[0]
    places = lax.broadcasted_iota(jnp.int32, (size, ids_ref.shape[1]), 0) + pl.program_id(0) * size
    hot = jnp.where(places == ids_ref[...], 1.0, 0.0).astype(BF16)
    out_ref[...] = (start_ref[...] + dot(hot, values_ref[...])).astype(out_ref.dtype)


def scatter_more_call(ids, values, start, block):
    count, width = start.shape
    return pl.pallas_call(
        scatter_more_kernel,
        grid=(count // block,),
        in_specs=[whole(ids), whole(values), rows(start, block)],
        out_specs=rows(start, block),
        out_shape=jax.ShapeDtypeStruct((count, width), BF16),
        compiler_params=params(),
        cost_estimate=cost(2 * count * width * values.shape[0], count * width * 6),
        name="scatter_more",
    )(ids, values, start)


def xor_swap(value, axis, distance):
    size = lax.axis_size(axis)
    return lax.ppermute(value, axis, [(i, i ^ distance) for i in range(size)])


def bits_of(size):
    return [1 << b for b in range(size.bit_length() - 1)]


def all_sum(value, axis):
    for distance in bits_of(lax.axis_size(axis)):
        value = value + xor_swap(value, axis, distance)
    return value


def shards(
    node_lat,
    edge_lat,
    neighbours,
    send_rows,
    coarse_of,
    weight_in,
    bias_in,
    weight_out,
    norm_gain,
    edge_cotangent,
    node_cotangent,
):
    node_count, latent = node_lat.shape
    degree = edge_lat.shape[1]
    edge_count = node_count * degree
    rim_rows = send_rows.shape[0] // 2
    feat_count = lax.axis_size("feat")
    patch_count = lax.axis_size("patch")
    patch_total = feat_count * node_count
    table_rows = patch_total + 2 * rim_rows
    coarse_total = COARSE_DEV * patch_count * feat_count
    feat = lax.axis_index("feat")
    patch = lax.axis_index("patch")
    block = min(512, edge_count)
    ring_up = [(i, (i + 1) % patch_count) for i in range(patch_count)]
    ring_down = [(j, i) for i, j in ring_up]

    def relative(ids):
        moved = ((ids // node_count) ^ feat) * node_count + ids % node_count
        return jnp.where(ids < patch_total, moved, ids)

    flat_edges = edge_lat.reshape(edge_count, latent)
    flat_cots = edge_cotangent.reshape(edge_count, latent)
    ids = relative(neighbours.T.reshape(edge_count))
    ids_col = ids[:, None]
    ids_row = ids[None, :]
    send_rel = relative(send_rows)
    bias = bias_in[None, :]
    gain = norm_gain[None, :]

    if feat_count == 4:
        far = xor_swap(node_lat, "feat", 2)
        near = xor_swap(node_lat, "feat", 1)
        last = xor_swap(far, "feat", 1)
        base = base_call(flat_edges, node_lat, ids_col, weight_in, bias, block)
        middle = jnp.concatenate([near, far], axis=0)
        table = jnp.concatenate([node_lat, near, far, last], axis=0)
        outgoing = select_call(send_rel[:, None], table)
        base = gather_call(base, ids_col, middle, weight_in, node_count, block)
        base = gather_call(base, ids_col, last, weight_in, 3 * node_count, block)
    else:
        table = node_lat
        for distance in bits_of(feat_count):
            table = jnp.concatenate([table, xor_swap(table, "feat", distance)], axis=0)
        outgoing = select_call(send_rel[:, None], table)
        base = base_call(flat_edges, node_lat, ids_col, weight_in, bias, block)
        base = gather_call(base, ids_col, table[node_count:], weight_in, node_count, block)
    from_lower = lax.ppermute(outgoing[rim_rows:], "patch", ring_up)
    from_upper = lax.ppermute(outgoing[:rim_rows], "patch", ring_down)
    rim = jnp.concatenate([from_lower, from_upper], axis=0)

    edge_new, aggregate, hidden_act, grad_proj, grad_pre, pre_sum, grad_edge = edge_call(
        base,
        ids_col,
        rim,
        flat_edges,
        flat_cots,
        node_cotangent,
        weight_in,
        weight_out,
        gain,
        patch_total,
        256,
    )

    rim_sum = scatter_call(ids_row, grad_pre, patch_total, 2 * rim_rows, 2 * rim_rows, BF16)
    back_upper = lax.ppermute(rim_sum[:rim_rows], "patch", ring_down)
    back_lower = lax.ppermute(rim_sum[rim_rows:], "patch", ring_up)
    patch_sum = scatter_call(ids_row, grad_pre, 0, patch_total, 256, F32)
    returned = jnp.concatenate([back_lower, back_upper], axis=0)
    chunks = scatter_more_call(send_rel[None, :], returned, patch_sum, node_count)
    if feat_count == 4:
        piece = [chunks[j * node_count : (j + 1) * node_count] for j in range(4)]
        relay = xor_swap(piece[3], "feat", 1)
        far_sum = (piece[2].astype(F32) + relay.astype(F32)).astype(BF16)
        got_far = xor_swap(far_sum, "feat", 2)
        got_near = xor_swap(piece[1], "feat", 1)
        own_sum = (piece[0].astype(F32) + got_far.astype(F32) + got_near.astype(F32)).astype(BF16)
    else:
        for distance in reversed(bits_of(feat_count)):
            half = distance * node_count
            got = xor_swap(chunks[half:], "feat", distance)
            chunks = (chunks[:half].astype(F32) + got.astype(F32)).astype(BF16)
        own_sum = chunks

    full_table = jnp.concatenate([table, rim], axis=0)
    full_sum = jnp.concatenate([patch_sum.astype(BF16), rim_sum], axis=0)

    def grad_dot(a, b):
        return lax.dot_general(a, b, ROWS, preferred_element_type=F32)

    in_rows = 3 * latent // patch_count
    out_rows = weight_out.shape[0] // patch_count
    hidden = weight_in.shape[1]
    grads_in = jnp.concatenate(
        [grad_dot(flat_edges, grad_pre), grad_dot(full_table, full_sum), grad_dot(node_lat, pre_sum)], axis=0
    )
    grads_out = grad_dot(hidden_act, grad_proj)
    grads = jnp.concatenate(
        [grads_in.reshape(patch_count, in_rows, hidden), grads_out.reshape(patch_count, out_rows, latent)], axis=1
    )
    span = in_rows + out_rows
    for distance in bits_of(patch_count):
        grads = grads.reshape(-1, 2, span, latent)
        bit = (patch // distance) % 2
        mine = lax.dynamic_index_in_dim(grads, bit, 1, keepdims=False)
        other = lax.dynamic_index_in_dim(grads, 1 - bit, 1, keepdims=False).astype(BF16)
        grads = mine + xor_swap(other, "patch", distance).astype(F32)
    width = latent // feat_count
    grads = grads.reshape(span, feat_count, width).transpose(1, 0, 2)
    for distance in bits_of(feat_count):
        grads = grads.reshape(-1, 2, span, width)
        bit = (feat // distance) % 2
        mine = lax.dynamic_index_in_dim(grads, bit, 1, keepdims=False)
        other = lax.dynamic_index_in_dim(grads, 1 - bit, 1, keepdims=False).astype(BF16)
        grads = mine + xor_swap(other, "feat", distance).astype(F32)
    grads = grads.reshape(span, width) * (1.0 / math.sqrt(edge_count * patch_count * feat_count))

    coarse_hot = (coarse_of[None, :] == jnp.arange(coarse_total)[:, None]).astype(BF16)
    counts = jnp.sum(coarse_hot.astype(F32), axis=1)
    sums = dot(coarse_hot, jnp.concatenate([node_lat, node_cotangent], axis=1))
    sums = jnp.concatenate([sums, jnp.broadcast_to(counts[:, None], (coarse_total, 128))], axis=1)
    sums = all_sum(all_sum(sums, "patch"), "feat")
    divisor = jnp.maximum(sums[:, 2 * latent :][:, :1], 1.0)
    means = (sums[:, : 2 * latent] / divisor).astype(BF16)
    spread = lax.dot_general(coarse_hot, means, ROWS, preferred_element_type=F32)

    node_new = (node_lat.astype(F32) + aggregate + spread[:, :latent]).astype(BF16)
    grad_node = node_cotangent.astype(F32) + spread[:, latent:]
    grad_node = grad_node + lax.dot_general(own_sum, weight_in[latent : 2 * latent], COLS, preferred_element_type=F32)
    grad_node = grad_node + lax.dot_general(pre_sum, weight_in[2 * latent :], COLS, preferred_element_type=F32)
    return (
        edge_new.reshape(edge_lat.shape),
        node_new,
        grad_edge.reshape(edge_lat.shape),
        grad_node.astype(BF16),
        grads[:in_rows],
        grads[in_rows:],
    )


def solution(mesh):
    return jax.shard_map(
        shards,
        mesh=mesh,
        in_specs=(
            P(("groups", "patch", "feat"), None),
            P(("groups", "patch", "feat"), None, None),
            P(None, ("patch", "feat")),
            P("patch"),
            P(("patch", "feat")),
            P(),
            P(),
            P(),
            P(),
            P(("groups", "patch", "feat"), None, None),
            P(("groups", "patch", "feat"), None),
        ),
        out_specs=(
            P(("groups", "patch", "feat"), None, None),
            P(("groups", "patch", "feat"), None),
            P(("groups", "patch", "feat"), None, None),
            P(("groups", "patch", "feat"), None),
            P(("groups", "patch"), "feat"),
            P(("groups", "patch"), "feat"),
        ),
        check_vma=False,
    )
```

time: 264 us -> 155 us (0.59)
  Pallas kernels: 0 us -> 51.6 us
  waiting for transfers between devices: 83.1 us -> 35.4 us
  other arithmetic: 64.8 us -> 20.3 us
  blocking collectives: 34.3 us -> 0 us
  matrix products: 36.7 us -> 11.1 us
  between operations: 15.9 us -> 1.03 us
  starting transfers between devices: 4.26 us -> 18.1 us
  local copies, waits for them, and re-layouts: 24 us -> 16.9 us
    pallas_call x0 -> x8, Pallas kernels: none -> 51.6 us  [the longest x1 16.5 us: edge_call(): pl.pallas_call(lambda *refs: edge_kernel(first, degree, *refs), grid=(blo...]
    psum x1 -> x0, waiting for transfers between devices: 44.7 us -> none  [shards(): lax.psum((local_sums[0], local_sums[1], local_sums[2]), ('patch', 'feat'))]
    psum x1 -> x0, blocking collectives: 34.3 us -> none  [shards(): lax.psum((local_sums[0], local_sums[1], local_sums[2]), ('patch', 'feat'))]
    scatter-add x5 -> x0, other arithmetic: 28 us -> none  [the longest x1 15.2 us: shards(): jax.ops.segment_sum(grad_sources, neighbour_ids.reshape(-1), table_rows + 1)]
    ppermute x4 -> x18, waiting for transfers between devices: 8.35 us -> 35.4 us  [the longest x14 32.6 us: xor_swap(): return lax.ppermute(value, axis, [(i, i ^ distance) for i in range(size)])]
    dot_general x10 -> x8, matrix products: 36.7 us -> 11.1 us  [the longest x4 6.98 us: grad_dot(): return lax.dot_general(a, b, ROWS, preferred_element_type=F32)]
    all_gather x1 -> x0, waiting for transfers between devices: 22.3 us -> none  [shards(): patch_table = lax.all_gather(node_lat, 'feat', axis=0, tiled=True)]
    gather x4 -> x0, local copies, waits for them, and re-layouts: 15.3 us -> none  [the longest x1 9.21 us: shards(): sources = full_table[neighbour_ids]]
  transfers between devices with their start and end apart: 11 -> 18, of which waited for: 6 -> 6; matrix products, arithmetic and copies ran while one was open for 30% -> 30% of each run, Pallas kernels for 0% -> 33%
where the time goes in v1:
time: 155 us; the launch traced here: 154 us
  Pallas kernels  51.6 us (33%)
  waiting for transfers between devices  35.4 us (23%)
  other arithmetic  20.3 us (13%)
  starting transfers between devices  18.1 us (12%)
  local copies, waits for them, and re-layouts  16.9 us (11%)
  matrix products  11.1 us (7%)
    ppermute x14, waiting for transfers between devices, xor_swap(): return lax.ppermute(value, axis, [(i, i ^ distance) for i in range(size)])  32.6 us
    ppermute x14, starting transfers between devices, xor_swap(): return lax.ppermute(value, axis, [(i, i ^ distance) for i in range(size)])  17 us
    pallas_call x1, Pallas kernels, edge_call(): pl.pallas_call(lambda *refs: edge_kernel(first, degree, *refs), grid=(blo...  16.5 us
    pallas_call x2, Pallas kernels, gather_call(): pl.pallas_call(lambda *refs: gather_kernel(first, *refs), grid=(count //...  13.3 us
    pallas_call x2, Pallas kernels, scatter_call(): pl.pallas_call(lambda *refs: scatter_kernel(first, *refs), grid=(count //...  8.52 us
    dot_general x4, matrix products, grad_dot(): return lax.dot_general(a, b, ROWS, preferred_element_type=F32)  6.98 us
    pallas_call x1, Pallas kernels, base_call(): pl.pallas_call(lambda *refs: base_kernel(degree, *refs), grid=(count // b...  6.71 us
    concatenate x2, local copies, waits for them, and re-layouts, shards(): jnp.concatenate([grads_in.reshape(patch_count, in_rows, hidden), grads_ou...  4.91 us
  transfers between devices with their start and end apart: 18, of which 6 were waited for; matrix products, arithmetic and copies ran while one was open for 30% of the time, Pallas kernels for 33%

profile of v1, /device:TPU:0, one launch (start us, length us, event | category | flops | bytes accessed | tf_op | source)
XLA Modules:
  0.0 154.4 jit_solution(13492103358870071387)
XLA Ops:
  0.6 4.1 %collective-permute-start.1 = (bf16[256,512]{1,0:T(8,128)(2,1)}, bf16[256,512]{1,0:T(8,128)(2,1)S(1)}, u32[]{:S(2)}, u32[]{:S(2)}) collective-permute-start(bf16[256,512]{1,0:T(8,128)(2,1)} %refs_3_.3), channel_id=1, source_target_pairs={{0,2},{1,3},{2,0},{3,1},{4,6},{5,7},{6,4},{7,5},{8,10},{9,11},{10,... | collective-permute-start | bytes 786440 | tf_op jit(solution)/shard_map/ppermute | solution.py:278
  9.8 2.1 %compare_select_fusion.refs_2_.refs_1_ = s32[2048,1]{1,0:T(8,128)} fusion(s32[2048,1]{1,0:T(8,128)S(1)} %reshape.317, s32[]{:T(128)S(6)} %axis_index.22), kind=kLoop, calls=%fused_computation.5 | loop fusion | flops 49152 | bytes 16388 | tf_op jit(solution)/shard_map/jit(_where)/select_n | solution.py:321
  13.5 6.7 %base_terms.1.refs_0_ = f32[2048,512]{1,0:T(8,128)} custom-call(bf16[2048,512]{1,0:T(8,128)(2,1)} %bitcast.46, bf16[256,512]{1,0:T(8,128)(2,1)} %refs_3_.3, s32[2048,1]{1,0:T(8,128)} %compare_select_fusion.refs_2_.refs_1_, bf16[256,512]{1,0:T(8,128)(2,1)} %refs_3_.3, bf16[1536,512]{1,0:T(8,128)(2,1)} %refs_6_.1, f32[1,512]{1,0:T(1,128)} %bitcast.52), custom_call_target="tpu_custom_call" | custom-call | flops 1610612736 | bytes 6291456 | tf_op jit(solution)/shard_map/base_terms/pallas_call | solution.py:66
  21.5 6.9 %gather_terms.2.refs_0_ = f32[2048,512]{1,0:T(8,128)} custom-call(f32[2048,512]{1,0:T(8,128)} %base_terms.1.refs_0_, s32[2048,1]{1,0:T(8,128)} %compare_select_fusion.refs_2_.refs_1_, bf16[512,512]{1,0:T(8,128)(2,1)} %pad_maximum_fusion.2.refs_2_, bf16[1536,512]{1,0:T(8,128)(2,1)} %refs_6_.1), custom_call_target="tpu_custom_call", output_to_operand_aliasing={{}: (0, {})} | custom-call | flops 1073741824 | bytes 8388608 | tf_op jit(solution)/shard_map/gather_terms/pallas_call | solution.py:99
  31.9 2.5 %select_rows.1 = bf16[256,512]{1,0:T(8,128)(2,1)} custom-call(s32[256,1]{1,0:T(8,128)} %copy.49.ids_ref, bf16[1024,512]{1,0:T(8,128)(2,1)} %pad_maximum_fusion.1.table_ref), custom_call_target="tpu_custom_call" | custom-call | flops 268435456 | bytes 2097152 | tf_op jit(solution)/shard_map/select_rows/pallas_call | solution.py:119
  35.9 6.3 %gather_terms.3.refs_0_ = f32[2048,512]{1,0:T(8,128)} custom-call(f32[2048,512]{1,0:T(8,128)} %gather_terms.2.refs_0_, s32[2048,1]{1,0:T(8,128)} %compare_select_fusion.refs_2_.refs_1_, bf16[256,512]{1,0:T(8,128)(2,1)} %copy-done.6, bf16[1536,512]{1,0:T(8,128)(2,1)} %refs_6_.1), custom_call_target="tpu_custom_call", output_to_operand_aliasing={{}: (0, {})} | custom-call | flops 536870912 | bytes 8388608 | tf_op jit(solution)/shard_map/gather_terms/pallas_call | solution.py:99
  44.0 16.5 %edge_block.1 = (bf16[2048,512]{1,0:T(8,128)(2,1)}, f32[256,512]{1,0:T(8,128)}, bf16[2048,512]{1,0:T(8,128)(2,1)}, bf16[2048,512]{1,0:T(8,128)(2,1)}, bf16[2048,...) custom-call(f32[2048,512]{1,0:T(8,128)} %gather_terms.3.refs_0_, ...), custom_call_target="tpu_custom_call" | custom-call | flops 3758096384 | bytes 20480000 | tf_op jit(solution)/shard_map/edge_block/pallas_call | solution.py:210
  60.5 3.0 %scatter_rows.2 = bf16[256,512]{1,0:T(8,128)(2,1)} custom-call(s32[1,2048]{1,0:T(1,128)} %compare_select_fusion.1.refs_0_, bf16[2048,512]{1,0:T(8,128)(2,1)} %get-tuple-element.16.refs_1_), custom_call_target="tpu_custom_call" | custom-call | flops 536870912 | bytes 2621440 | tf_op jit(solution)/shard_map/scatter_rows/pallas_call | solution.py:243
  63.5 5.5 %scatter_rows.3.start_ref = f32[1024,512]{1,0:T(8,128)} custom-call(s32[1,2048]{1,0:T(1,128)} %compare_select_fusion.1.refs_0_, bf16[2048,512]{1,0:T(8,128)(2,1)} %get-tuple-element.16.refs_1_), custom_call_target="tpu_custom_call" | custom-call | flops 2147483648 | bytes 4194304 | tf_op jit(solution)/shard_map/scatter_rows/pallas_call | solution.py:243
  72.5 1.9 %pad_maximum_fusion = f32[1536,512]{1,0:T(8,128)} fusion(f32[512,512]{1,0:T(8,128)S(1)} %convolution_bitcast_fusion, f32[512,512]{1,0:T(8,128)S(1)} %fusion.5, f32[512,512]{1,0:T(8,128)S(1)} %convolution_bitcast_fusion.1), kind=kLoop, calls=%fused_computation.4 | loop fusion | flops 1572864 | bytes 6291456 | tf_op jit(solution)/shard_map/concatenate | solution.py:396
  74.5 2.4 %copy.51 = f32[2,2,384,512]{2,3,0,1:T(8,128)S(1)} copy(f32[2,2,384,512]{3,2,1,0:T(8,128)} %bitcast.42) | data formatting | bytes 6291456 | tf_op jit(solution)/shard_map/concatenate | solution.py:400
  76.9 4.5 %fusion.43 = f32[512,512]{1,0:T(8,128)} fusion(bf16[2048,512]{1,0:T(8,128)(2,1)} %get-tuple-element.18, bf16[2048,512]{1,0:T(8,128)(2,1)} %get-tuple-element.19), kind=kOutput, calls=%fused_computation.97 | convolution fusion | flops 1073741824 | bytes 5242880 | tf_op jit(solution)/shard_map/dot_general | solution.py:391
  81.4 2.5 %copy.52 = f32[2,2,128,512]{2,3,0,1:T(8,128)} copy(f32[2,2,128,512]{3,2,1,0:T(8,128)} %bitcast.48) | data formatting | bytes 2097152 | tf_op jit(solution)/shard_map/concatenate | solution.py:400
  83.9 2.2 %fusion.13 = bf16[2,512,512]{1,2,0:T(8,128)(2,1)} fusion(s32[]{:T(128)S(6)} %select_n.143, f32[2,2,128,512]{2,3,0,1:T(8,128)} %copy.52, f32[2,2,384,512]{2,3,0,1:T(8,128)S(1)} %copy.51), kind=kLoop, calls=%fused_computation.28 | loop fusion | flops 2097152 | bytes 5242884 | tf_op jit(solution)/shard_map/convert_element_type | solution.py:408
  90.5 2.7 %collective-permute-done.9 = bf16[128,512]{1,0:T(8,128)(2,1)S(1)} collective-permute-done((bf16[128,512]{1,0:T(8,128)(2,1)S(1)}, bf16[128,512]{1,0:T(8,128)(2,1)S(1)}, u32[]{:S(2)}, u32[]{:S(2)}) %collective-permute-start.9) | collective-permute-done | bytes 131104 | tf_op jit(solution)/shard_map/ppermute | solution.py:369
  94.0 4.1 %scatter_more.1 = bf16[1024,512]{1,0:T(8,128)(2,1)} custom-call(s32[1,256]{1,0:T(1,128)} %bitcast.50, bf16[256,512]{1,0:T(8,128)(2,1)} %pad_maximum_fusion.5.values_ref, f32[1024,512]{1,0:T(8,128)} %scatter_rows.3.start_ref), custom_call_target="tpu_custom_call" | custom-call | flops 268435456 | bytes 3145728 | tf_op jit(solution)/shard_map/scatter_more/pallas_call | solution.py:264
  98.1 1.9 %fusion.40 = (bf16[256,512]{1,0:T(8,128)(2,1)}, bf16[256,512]{1,0:T(8,128)(2,1)}) fusion(bf16[1024,512]{1,0:T(8,128)(2,1)} %scatter_more.1), kind=kLoop, calls=%fused_computation.94 | loop fusion | bytes 1048576 | tf_op jit(solution)/shard_map/slice | solution.py:374
  103.0 8.9 %collective-permute-done.11 = bf16[256,512]{1,0:T(8,128)(2,1)} collective-permute-done((bf16[256,512]{1,0:T(8,128)(2,1)}, bf16[256,512]{1,0:T(8,128)(2,1)}, u32[]{:S(2)}, u32[]{:S(2)}) %collective-permute-start.11) | collective-permute-done | bytes 262176 | tf_op jit(solution)/shard_map/ppermute | solution.py:278
  113.7 2.8 %collective-permute-start.12 = (bf16[256,512]{1,0:T(8,128)(2,1)}, bf16[256,512]{1,0:T(8,128)(2,1)}, u32[]{:S(2)}, u32[]{:S(2)}) collective-permute-start(bf16[256,512]{1,0:T(8,128)(2,1)} %add_convert_fusion.1), channel_id=1, source_target_pairs={{0,2},{1,3},{2,0},{3,1},{4,6},{5,7},{6,4},{7,5},{8,10},{9,11},{10,... | collective-permute-start | bytes 786440 | tf_op jit(solution)/shard_map/ppermute | solution.py:278
  116.5 3.6 %collective-permute-done.8 = f32[64,1152]{1,0:T(8,128)} collective-permute-done((f32[64,1152]{1,0:T(8,128)}, f32[64,1152]{1,0:T(8,128)}, u32[]{:S(2)}, u32[]{:S(2)}) %collective-permute-start.8) | collective-permute-done | bytes 294944 | tf_op jit(solution)/shard_map/ppermute | solution.py:278
  125.2 8.9 %collective-permute-done.15 = bf16[1,512,512]{1,2,0:T(8,128)(2,1)S(1)} collective-permute-done((bf16[1,512,512]{1,2,0:T(8,128)(2,1)S(1)}, bf16[1,512,512]{1,2,0:T(8,128)(2,1)S(1)}, u32[]{:S(2)}, u32[]{:S(2)}) %collective-permute-start.15) | collective-permute-done | bytes 524320 | tf_op jit(solution)/shard_map/ppermute | solution.py:278
  135.3 2.5 %copy.53 = f32[4,512,128]{2,1,0:T(8,128)} copy(f32[4,512,128]{1,2,0:T(8,128)} %bitcast.43) | data formatting | bytes 2097152 | tf_op jit(solution)/shard_map/transpose | solution.py:411
  140.6 5.0 %collective-permute-done.16 = bf16[2,512,128]{2,1,0:T(8,128)(2,1)S(1)} collective-permute-done((bf16[2,512,128]{2,1,0:T(8,128)(2,1)S(1)}, bf16[2,512,128]{2,1,0:T(8,128)(2,1)S(1)}, u32[]{:S(2)}, u32[]{:S(2)}) %collective-permute-start.16) | collective-permute-done | bytes 262176 | tf_op jit(solution)/shard_map/ppermute | solution.py:278
  146.9 6.2 %collective-permute-done.17 = bf16[1,512,128]{2,1,0:T(8,128)(2,1)S(1)} collective-permute-done((bf16[1,512,128]{2,1,0:T(8,128)(2,1)S(1)}, bf16[1,512,128]{2,1,0:T(8,128)(2,1)S(1)}, u32[]{:S(2)}, u32[]{:S(2)}) %collective-permute-start.17) | collective-permute-done | bytes 131104 | tf_op jit(solution)/shard_map/ppermute | solution.py:278
  (109 shorter events, 39.6 us)
Async XLA Ops:
  0.6 19.5 %collective-permute-start.1 = (bf16[256,512]{1,0:T(8,128)(2,1)}, bf16[256,512]{1,0:T(8,128)(2,1)S(1)}, u32[]{:S(2)}, u32[]{:S(2)}) collective-permute-start(bf16[256,512]{1,0:T(8,128)(2,1)} %refs_3_.3), channel_id=1, source_target_pairs={{0,2},{1,3},{2,0},{3,1},{4,6},{5,7},{6,4},{7,5},{8,10},{9,11},{10,... | collective-permute-start | bytes 786440 | tf_op jit(solution)/shard_map/ppermute | solution.py:278
  4.7 16.0 %collective-permute-start = (bf16[256,512]{1,0:T(8,128)(2,1)}, bf16[256,512]{1,0:T(8,128)(2,1)S(1)}, u32[]{:S(2)}, u32[]{:S(2)}) collective-permute-start(bf16[256,512]{1,0:T(8,128)(2,1)} %refs_3_.3), channel_id=1, source_target_pairs={{0,1},{1,0},{2,3},{3,2},{4,5},{5,4},{6,7},{7,6},{8,9},{9,8},{10,11... | collective-permute-start | bytes 786440 | tf_op jit(solution)/shard_map/ppermute | solution.py:278
  8.5 20.0 %collective-permute-start.5 = (f32[64,1152]{1,0:T(8,128)S(1)}, f32[64,1152]{1,0:T(8,128)S(1)}, u32[]{:S(2)}, u32[]{:S(2)}) collective-permute-start(f32[64,1152]{1,0:T(8,128)S(1)} %pad_maximum_fusion.3), channel_id=1, source_target_pairs={{0,4},{4,0},{8,12},{12,8},{1,5},{5,1},{9,13},{13,9},{2,6},{6,2},{1... | collective-permute-start | bytes 884744 | tf_op jit(solution)/shard_map/ppermute | solution.py:278
  11.9 8.2 %copy-start.15 = (s32[256]{0:T(256)}, s32[256]{0:T(256)S(1)}, u32[]{:S(2)}) copy-start(s32[256]{0:T(256)S(1)} %compare_select_fusion.5) | copy-start | bytes 3076
  20.2 10.6 %collective-permute-start.2 = (bf16[256,512]{1,0:T(8,128)(2,1)S(1)}, bf16[256,512]{1,0:T(8,128)(2,1)S(1)}, u32[]{:S(2)}, u32[]{:S(2)}) collective-permute-start(bf16[256,512]{1,0:T(8,128)(2,1)S(1)} %collective-permute-done.1), channel_id=1, source_target_pairs={{0,1},{1,0},{2,3},{3,2},{4,5},{5,4},{6,7},{7,6},{8,9},{9,8},{10,11... | collective-permute-start | bytes 786440 | tf_op jit(solution)/shard_map/ppermute | solution.py:278
  29.3 58.5 %collective-permute-start.6 = (f32[64,1152]{1,0:T(8,128)}, f32[64,1152]{1,0:T(8,128)}, u32[]{:S(2)}, u32[]{:S(2)}) collective-permute-start(f32[64,1152]{1,0:T(8,128)} %fusion.39), channel_id=1, source_target_pairs={{0,8},{4,12},{8,0},{12,4},{1,9},{5,13},{9,1},{13,5},{2,10},{6,14},... | collective-permute-start | bytes 884744 | tf_op jit(solution)/shard_map/ppermute | solution.py:278
  35.4 7.9 %collective-permute-start.4 = (bf16[128,512]{1,0:T(8,128)(2,1)S(1)}, bf16[128,512]{1,0:T(8,128)(2,1)S(1)}, u32[]{:S(2)}, u32[]{:S(2)}) collective-permute-start(bf16[128,512]{1,0:T(8,128)(2,1)S(1)} %get-tuple-element.25), channel_id=1, source_target_pairs={{4,0},{8,4},{12,8},{0,12},{5,1},{9,5},{13,9},{1,13},{6,2},{10,6},{... | collective-permute-start | bytes 393224 | tf_op jit(solution)/shard_map/ppermute | solution.py:350
  35.5 7.8 %collective-permute-start.3 = (bf16[128,512]{1,0:T(8,128)(2,1)S(1)}, bf16[128,512]{1,0:T(8,128)(2,1)S(1)}, u32[]{:S(2)}, u32[]{:S(2)}) collective-permute-start(bf16[128,512]{1,0:T(8,128)(2,1)S(1)} %get-tuple-element.24), channel_id=1, source_target_pairs={{0,4},{4,8},{8,12},{12,0},{1,5},{5,9},{9,13},{13,1},{2,6},{6,10},{... | collective-permute-start | bytes 393224 | tf_op jit(solution)/shard_map/ppermute | solution.py:349
  86.1 35.1 %collective-permute-start.14 = (bf16[2,512,512]{1,2,0:T(8,128)(2,1)}, bf16[2,512,512]{1,2,0:T(8,128)(2,1)}, u32[]{:S(2)}, u32[]{:S(2)}) collective-permute-start(bf16[2,512,512]{1,2,0:T(8,128)(2,1)} %fusion.13), channel_id=1, source_target_pairs={{0,4},{4,0},{8,12},{12,8},{1,5},{5,1},{9,13},{13,9},{2,6},{6,2},{1... | collective-permute-start | bytes 3145736 | tf_op jit(solution)/shard_map/ppermute | solution.py:278
  87.3 3.3 %collective-permute-start.10 = (bf16[128,512]{1,0:T(8,128)(2,1)S(1)}, bf16[128,512]{1,0:T(8,128)(2,1)S(1)}, u32[]{:S(2)}, u32[]{:S(2)}) collective-permute-start(bf16[128,512]{1,0:T(8,128)(2,1)S(1)} %get-tuple-element.23), channel_id=1, source_target_pairs={{4,0},{8,4},{12,8},{0,12},{5,1},{9,5},{13,9},{1,13},{6,2},{10,6},{... | collective-permute-start | bytes 393224 | tf_op jit(solution)/shard_map/ppermute | solution.py:368
  87.5 5.8 %collective-permute-start.9 = (bf16[128,512]{1,0:T(8,128)(2,1)S(1)}, bf16[128,512]{1,0:T(8,128)(2,1)S(1)}, u32[]{:S(2)}, u32[]{:S(2)}) collective-permute-start(bf16[128,512]{1,0:T(8,128)(2,1)S(1)} %get-tuple-element.22), channel_id=1, source_target_pairs={{0,4},{4,8},{8,12},{12,0},{1,5},{5,9},{9,13},{13,1},{2,6},{6,10},{... | collective-permute-start | bytes 393224 | tf_op jit(solution)/shard_map/ppermute | solution.py:369
  88.9 12.6 %collective-permute-start.7 = (f32[64,1152]{1,0:T(8,128)S(1)}, f32[64,1152]{1,0:T(8,128)S(1)}, u32[]{:S(2)}, u32[]{:S(2)}) collective-permute-start(f32[64,1152]{1,0:T(8,128)S(1)} %add.169), channel_id=1, source_target_pairs={{0,1},{1,0},{2,3},{3,2},{4,5},{5,4},{6,7},{7,6},{8,9},{9,8},{10,11... | collective-permute-start | bytes 884744 | tf_op jit(solution)/shard_map/ppermute | solution.py:278
  99.9 12.0 %collective-permute-start.11 = (bf16[256,512]{1,0:T(8,128)(2,1)}, bf16[256,512]{1,0:T(8,128)(2,1)}, u32[]{:S(2)}, u32[]{:S(2)}) collective-permute-start(bf16[256,512]{1,0:T(8,128)(2,1)} %get-tuple-element.20), channel_id=1, source_target_pairs={{0,1},{1,0},{2,3},{3,2},{4,5},{5,4},{6,7},{7,6},{8,9},{9,8},{10,11... | collective-permute-start | bytes 786440 | tf_op jit(solution)/shard_map/ppermute | solution.py:278
  102.2 17.8 %collective-permute-start.8 = (f32[64,1152]{1,0:T(8,128)}, f32[64,1152]{1,0:T(8,128)}, u32[]{:S(2)}, u32[]{:S(2)}) collective-permute-start(f32[64,1152]{1,0:T(8,128)} %add.170), channel_id=1, source_target_pairs={{0,2},{1,3},{2,0},{3,1},{4,6},{5,7},{6,4},{7,5},{8,10},{9,11},{10,... | collective-permute-start | bytes 884744 | tf_op jit(solution)/shard_map/ppermute | solution.py:278
  102.6 18.6 %copy-start.3 = (f32[2,2,128,512]{2,3,0,1:T(8,128)S(1)}, f32[2,2,128,512]{2,3,0,1:T(8,128)}, u32[]{:S(2)}) copy-start(f32[2,2,128,512]{2,3,0,1:T(8,128)} %copy.52) | copy-start | bytes 3145732
  102.6 36.5 %collective-permute-start.13 = (bf16[256,512]{1,0:T(8,128)(2,1)}, bf16[256,512]{1,0:T(8,128)(2,1)}, u32[]{:S(2)}, u32[]{:S(2)}) collective-permute-start(bf16[256,512]{1,0:T(8,128)(2,1)} %get-tuple-element.21), channel_id=1, source_target_pairs={{0,1},{1,0},{2,3},{3,2},{4,5},{5,4},{6,7},{7,6},{8,9},{9,8},{10,11... | collective-permute-start | bytes 786440 | tf_op jit(solution)/shard_map/ppermute | solution.py:278
  113.7 25.4 %collective-permute-start.12 = (bf16[256,512]{1,0:T(8,128)(2,1)}, bf16[256,512]{1,0:T(8,128)(2,1)}, u32[]{:S(2)}, u32[]{:S(2)}) collective-permute-start(bf16[256,512]{1,0:T(8,128)(2,1)} %add_convert_fusion.1), channel_id=1, source_target_pairs={{0,2},{1,3},{2,0},{3,1},{4,6},{5,7},{6,4},{7,5},{8,10},{9,11},{10,... | collective-permute-start | bytes 786440 | tf_op jit(solution)/shard_map/ppermute | solution.py:278
  122.8 11.3 %collective-permute-start.15 = (bf16[1,512,512]{1,2,0:T(8,128)(2,1)S(1)}, bf16[1,512,512]{1,2,0:T(8,128)(2,1)S(1)}, u32[]{:S(2)}, u32[]{:S(2)}) collective-permute-start(bf16[1,512,512]{1,2,0:T(8,128)(2,1)S(1)} %dynamic-slice_convert_fusion), channel_id=1, source_target_pairs={{0,8},{4,12},{8,0},{12,4},{1,9},{5,13},{9,1},{13,5},{2,10},{6,14},... | collective-permute-start | bytes 1572872 | tf_op jit(solution)/shard_map/ppermute | solution.py:278
  125.2 13.9 %copy-start = (bf16[1536,512]{1,0:T(8,128)(2,1)S(1)}, bf16[1536,512]{1,0:T(8,128)(2,1)}, u32[]{:S(2)}) copy-start(bf16[1536,512]{1,0:T(8,128)(2,1)} %refs_6_.1) | copy-start | bytes 4718596
  125.2 13.9 %copy-start.14 = (bf16[256,512]{1,0:T(8,128)(2,1)S(1)}, bf16[256,512]{1,0:T(8,128)(2,1)}, u32[]{:S(2)}) copy-start(bf16[256,512]{1,0:T(8,128)(2,1)} %refs_5_.1) | copy-start | bytes 786436
  137.8 7.8 %copy-start.5 = (f32[4,512,128]{2,1,0:T(8,128)S(1)}, f32[4,512,128]{2,1,0:T(8,128)}, u32[]{:S(2)}) copy-start(f32[4,512,128]{2,1,0:T(8,128)} %copy.53) | copy-start | bytes 3145732
  139.0 6.8 %copy-start.12 = (bf16[256,512]{1,0:T(8,128)(2,1)S(1)}, bf16[256,512]{1,0:T(8,128)(2,1)}, u32[]{:S(2)}) copy-start(bf16[256,512]{1,0:T(8,128)(2,1)} %get-tuple-element.17) | copy-start | bytes 786436
  139.0 6.6 %collective-permute-start.16 = (bf16[2,512,128]{2,1,0:T(8,128)(2,1)S(1)}, bf16[2,512,128]{2,1,0:T(8,128)(2,1)S(1)}, u32[]{:S(2)}, u32[]{:S(2)}) collective-permute-start(bf16[2,512,128]{2,1,0:T(8,128)(2,1)S(1)} %fusion.24), channel_id=1, source_target_pairs={{0,1},{1,0},{2,3},{3,2},{4,5},{5,4},{6,7},{7,6},{8,9},{9,8},{10,11... | collective-permute-start | bytes 786440 | tf_op jit(solution)/shard_map/ppermute | solution.py:278
  145.7 7.3 %collective-permute-start.17 = (bf16[1,512,128]{2,1,0:T(8,128)(2,1)S(1)}, bf16[1,512,128]{2,1,0:T(8,128)(2,1)S(1)}, u32[]{:S(2)}, u32[]{:S(2)}) collective-permute-start(bf16[1,512,128]{2,1,0:T(8,128)(2,1)S(1)} %dynamic-slice_convert_fusion.2), channel_id=1, source_target_pairs={{0,2},{1,3},{2,0},{3,1},{4,6},{5,7},{6,4},{7,5},{8,10},{9,11},{10,... | collective-permute-start | bytes 393224 | tf_op jit(solution)/shard_map/ppermute | solution.py:278
  (12 other events, 38.9 us)

commit v2 on v1

v2 whole, which is shorter than its diff:
```python
import math

import jax
import jax.numpy as jnp
from jax import lax
from jax.experimental import pallas as pl
from jax.experimental.pallas import tpu as pltpu
from jax.sharding import PartitionSpec as P

COARSE_DEV = 4
LAYER_EPS = 1e-05
F32 = jnp.float32
BF16 = jnp.bfloat16
VMEM_LIMIT = 24 * 1024 * 1024
COLS = (((1,), (1,)), ((), ()))
ROWS = (((0,), (0,)), ((), ()))


def dot(a, b):
    return jnp.dot(a, b, preferred_element_type=F32)


def params():
    return pltpu.CompilerParams(vmem_limit_bytes=VMEM_LIMIT)


def cost(micros):
    return pl.CostEstimate(flops=int(micros * 1.15e9), bytes_accessed=1 << 20, transcendentals=0)


def whole(array):
    zeros = (0,) * array.ndim
    return pl.BlockSpec(array.shape, lambda i: zeros)


def rows(array, block):
    rest = (0,) * (array.ndim - 1)
    return pl.BlockSpec((block,) + array.shape[1:], lambda i: (i,) + rest)


def one_hot(ids, first, count):
    lanes = lax.broadcasted_iota(jnp.int32, (ids.shape[0], count), 1) + first
    return jnp.where(ids == lanes, 1.0, 0.0).astype(BF16)


def fill_table(table, pieces, weight_ref):
    latent = pieces[0].shape[1]
    at = 0
    for piece in pieces:
        size = piece.shape[0]
        table[at : at + size] = dot(piece[...], weight_ref[latent : 2 * latent]).astype(BF16)
        at += size


def base_kernel(degree, edge_ref, node_ref, ids_ref, weight_ref, bias_ref, after_ref, *refs):
    pieces, (out_ref, table) = refs[:-2], refs[-2:]
    latent = edge_ref.shape[1]

    @pl.when(pl.program_id(0) == 0)
    def _():
        fill_table(table, pieces, weight_ref)

    edges = edge_ref.shape[0]
    term = dot(node_ref[...], weight_ref[2 * latent :]) + bias_ref[...]
    total = dot(edge_ref[...], weight_ref[:latent])
    total = total + dot(one_hot(ids_ref[...], 0, table.shape[0]), table[...])
    hidden = total.shape[1]
    total = total.reshape(edges // degree, degree, hidden) + term[:, None, :]
    out_ref[...] = total.reshape(edges, hidden)


def base_call(edges, nodes, ids, weight_in, bias, after, pieces, block):
    count, latent = edges.shape
    hidden = weight_in.shape[1]
    degree = count // nodes.shape[0]
    size = sum(piece.shape[0] for piece in pieces)
    return pl.pallas_call(
        lambda *refs: base_kernel(degree, *refs),
        grid=(count // block,),
        in_specs=[
            rows(edges, block),
            rows(nodes, block // degree),
            rows(ids, block),
            whole(weight_in),
            whole(bias),
            pl.BlockSpec(memory_space=pl.ANY),
        ]
        + [whole(piece) for piece in pieces],
        out_specs=pl.BlockSpec((block, hidden), lambda i: (i, 0)),
        out_shape=jax.ShapeDtypeStruct((count, hidden), F32),
        scratch_shapes=[pltpu.VMEM((size, hidden), BF16)],
        compiler_params=params(),
        cost_estimate=cost(5),
        name="base_terms",
    )(edges, nodes, ids, weight_in, bias, after, *pieces)


def edge_kernel(
    first,
    degree,
    base_ref,
    ids_ref,
    low_ref,
    high_ref,
    edge_ref,
    cot_ref,
    ncot_ref,
    weight_ref,
    out_w_ref,
    gain_ref,
    mine_ref,
    got_ref,
    new_ref,
    agg_ref,
    hid_ref,
    gproj_ref,
    gpre_ref,
    psum_ref,
    gedge_ref,
    sum_ref,
    table,
):
    latent = low_ref.shape[1]
    half = low_ref.shape[0]

    @pl.when(pl.program_id(0) == 0)
    def _():
        table[:half] = dot(low_ref[...], weight_ref[latent : 2 * latent]).astype(BF16)
        table[half:] = dot(high_ref[...], weight_ref[latent : 2 * latent]).astype(BF16)
        sum_ref[...] = mine_ref[...] + got_ref[...]

    ids = ids_ref[...]
    edges = ids.shape[0]
    nodes = edges // degree
    limit = first + 2 * half
    live = jnp.where(ids < limit, 1.0, 0.0)
    value = base_ref[...] + dot(one_hot(ids, first, 2 * half), table[...])
    sig = jax.nn.sigmoid(value)
    act = value * sig
    slope = sig + act * (1.0 - sig)
    hid = act.astype(BF16)
    hid_ref[...] = hid
    projected = dot(hid, out_w_ref[...])
    centre = projected - jnp.mean(projected, axis=1, keepdims=True)
    inverse = lax.rsqrt(jnp.mean(centre * centre, axis=1, keepdims=True) + LAYER_EPS)
    normed = centre * inverse
    gain = gain_ref[...]
    message = normed * gain
    new_ref[...] = (edge_ref[...].astype(F32) + message).astype(BF16)
    agg_ref[...] = jnp.sum((message * live).reshape(nodes, degree, latent), axis=1)
    ncot = jnp.broadcast_to(ncot_ref[...].astype(F32)[:, None, :], (nodes, degree, latent))
    cot = cot_ref[...].astype(F32)
    scaled = (cot + live * ncot.reshape(edges, latent)) * gain
    mean_a = jnp.mean(scaled, axis=1, keepdims=True)
    mean_b = jnp.mean(scaled * normed, axis=1, keepdims=True)
    gproj = (inverse * (scaled - mean_a - normed * mean_b)).astype(BF16)
    gproj_ref[...] = gproj
    gpre = (lax.dot_general(gproj, out_w_ref[...], COLS, preferred_element_type=F32) * slope).astype(BF16)
    gpre_ref[...] = gpre
    psum_ref[...] = jnp.sum(gpre.astype(F32).reshape(nodes, degree, gpre.shape[1]), axis=1).astype(BF16)
    back = lax.dot_general(gpre, weight_ref[:latent], COLS, preferred_element_type=F32)
    gedge_ref[...] = (cot + back).astype(BF16)


def edge_call(base, ids, low, high, edges, cots, ncot, weight_in, weight_out, gain, mine, got, first, block):
    count, latent = edges.shape
    hidden = weight_in.shape[1]
    degree = count // ncot.shape[0]
    blocks = count // block
    small = block // degree

    def like(width, dtype, size, total):
        return (
            pl.BlockSpec((size, width), lambda i: (i, 0)),
            jax.ShapeDtypeStruct((total, width), dtype),
        )

    outs = [
        like(latent, BF16, block, count),
        like(latent, F32, small, count // degree),
        like(hidden, BF16, block, count),
        like(latent, BF16, block, count),
        like(hidden, BF16, block, count),
        like(hidden, BF16, small, count // degree),
        like(latent, BF16, block, count),
        (whole(mine), jax.ShapeDtypeStruct(mine.shape, F32)),
    ]
    return pl.pallas_call(
        lambda *refs: edge_kernel(first, degree, *refs),
        grid=(blocks,),
        in_specs=[
            rows(base, block),
            rows(ids, block),
            whole(low),
            whole(high),
            rows(edges, block),
            rows(cots, block),
            rows(ncot, small),
            whole(weight_in),
            whole(weight_out),
            whole(gain),
            whole(mine),
            whole(got),
        ],
        out_specs=[spec for spec, _ in outs],
        out_shape=[shape for _, shape in outs],
        scratch_shapes=[pltpu.VMEM((2 * low.shape[0], hidden), BF16)],
        compiler_params=params(),
        cost_estimate=cost(12),
        name="edge_block",
    )(base, ids, low, high, edges, cots, ncot, weight_in, weight_out, gain, mine, got)


def gather_kernel(first, base_ref, ids_ref, *refs):
    pieces, (weight_ref, out_ref, table) = refs[:-3], refs[-3:]

    @pl.when(pl.program_id(0) == 0)
    def _():
        fill_table(table, pieces, weight_ref)

    hot = one_hot(ids_ref[...], first, table.shape[0])
    out_ref[...] = base_ref[...] + dot(hot, table[...])


def gather_call(base, ids, pieces, weight_in, first, block):
    count, hidden = base.shape
    size = sum(piece.shape[0] for piece in pieces)
    return pl.pallas_call(
        lambda *refs: gather_kernel(first, *refs),
        grid=(count // block,),
        in_specs=[rows(base, block), rows(ids, block)] + [whole(piece) for piece in pieces] + [whole(weight_in)],
        out_specs=rows(base, block),
        out_shape=jax.ShapeDtypeStruct(base.shape, F32),
        scratch_shapes=[pltpu.VMEM((size, hidden), BF16)],
        compiler_params=params(),
        cost_estimate=cost(2),
        name="gather_terms",
    )(base, ids, *pieces, weight_in)


def select_kernel(ids_ref, mine_ref, got_ref, after_ref, *refs):
    pieces, (low_ref, high_ref, sum_ref) = refs[:-3], refs[-3:]
    total, at = None, 0
    for piece in pieces:
        term = dot(one_hot(ids_ref[...], at, piece.shape[0]), piece[...])
        total = term if total is None else total + term
        at += piece.shape[0]
    half = low_ref.shape[0]
    low_ref[...] = total[:half].astype(BF16)
    high_ref[...] = total[half:].astype(BF16)
    sum_ref[...] = mine_ref[...] + got_ref[...]


def select_call(ids, mine, got, after, pieces):
    count, width = ids.shape[0], pieces[0].shape[1]
    half = jax.ShapeDtypeStruct((count // 2, width), BF16)
    vmem = pl.BlockSpec(memory_space=pltpu.VMEM)
    return pl.pallas_call(
        select_kernel,
        in_specs=[vmem] * 3 + [pl.BlockSpec(memory_space=pl.ANY)] + [vmem] * len(pieces),
        out_shape=[half, half, jax.ShapeDtypeStruct(mine.shape, F32)],
        compiler_params=params(),
        cost_estimate=cost(0.7),
        name="select_rows",
    )(ids, mine, got, after, *pieces)


def rim_sum_kernel(first, ids_ref, values_ref, low_ref, high_ref):
    half = low_ref.shape[0]
    places = lax.broadcasted_iota(jnp.int32, (2 * half, ids_ref.shape[1]), 0) + first
    hot = jnp.where(places == ids_ref[...], 1.0, 0.0).astype(BF16)
    total = dot(hot, values_ref[...])
    low_ref[...] = total[:half].astype(BF16)
    high_ref[...] = total[half:].astype(BF16)


def rim_sum_call(ids, values, first, count):
    half = jax.ShapeDtypeStruct((count // 2, values.shape[1]), BF16)
    return pl.pallas_call(
        lambda *refs: rim_sum_kernel(first, *refs),
        out_shape=[half, half],
        compiler_params=params(),
        cost_estimate=cost(0.7),
        name="rim_sums",
    )(ids, values)


def patch_sum_kernel(ids_ref, values_ref, out_ref):
    size = out_ref.shape[0]
    places = lax.broadcasted_iota(jnp.int32, (size, ids_ref.shape[1]), 0) + pl.program_id(0) * size
    hot = jnp.where(places == ids_ref[...], 1.0, 0.0).astype(BF16)
    out_ref[...] = dot(hot, values_ref[...])


def patch_sum_call(ids, values, count, block):
    width = values.shape[1]
    return pl.pallas_call(
        patch_sum_kernel,
        grid=(count // block,),
        in_specs=[whole(ids), whole(values)],
        out_specs=pl.BlockSpec((block, width), lambda i: (i, 0)),
        out_shape=jax.ShapeDtypeStruct((count, width), F32),
        compiler_params=params(),
        cost_estimate=cost(2.8),
        name="patch_sums",
    )(ids, values)


def add_rim_kernel(ids_ref, low_ref, high_ref, start_ref, mine_ref, got_ref, sum_ref, *outs):
    sum_ref[...] = mine_ref[...] + got_ref[...]
    half = low_ref.shape[0]
    size = outs[0].shape[0]
    for j, out in enumerate(outs):
        places = lax.broadcasted_iota(jnp.int32, (size, 2 * half), 0) + j * size
        hot = jnp.where(places == ids_ref[...], 1.0, 0.0).astype(BF16)
        total = start_ref[j * size : (j + 1) * size] + dot(hot[:, :half], low_ref[...])
        total = total + dot(hot[:, half:], high_ref[...])
        out[...] = total.astype(BF16)


def add_rim_call(ids, low, high, start, mine, got, size):
    count, width = start.shape
    piece = jax.ShapeDtypeStruct((size, width), BF16)
    return pl.pallas_call(
        add_rim_kernel,
        out_shape=[jax.ShapeDtypeStruct(mine.shape, F32)] + [piece] * (count // size),
        compiler_params=params(),
        cost_estimate=cost(0.7),
        name="add_rim_sums",
    )(ids, low, high, start, mine, got)


def edge_grads_kernel(edge_ref, gpre_ref, hid_ref, gproj_ref, in_ref, out_ref):
    in_ref[...] = lax.dot_general(edge_ref[...], gpre_ref[...], ROWS, preferred_element_type=F32)
    out_ref[...] = lax.dot_general(hid_ref[...], gproj_ref[...], ROWS, preferred_element_type=F32)


def edge_grads_call(edges, gpre, hid, gproj):
    latent, hidden = edges.shape[1], gpre.shape[1]
    return pl.pallas_call(
        edge_grads_kernel,
        out_shape=[
            jax.ShapeDtypeStruct((latent, hidden), F32),
            jax.ShapeDtypeStruct((hidden, latent), F32),
        ],
        compiler_params=params(),
        cost_estimate=cost(2.4),
        name="edge_grads",
    )(edges, gpre, hid, gproj)


def pack_kernel(pieces, bit_ref, psum_ref, edge_ref, out_ref, *refs):
    tables, sums = refs[:pieces], refs[pieces : 2 * pieces]
    keep_ref, send_ref, total = refs[2 * pieces :]
    latent = tables[0].shape[1]
    grad = None
    for table, part in zip(tables, sums):
        term = lax.dot_general(table[...], part[...], ROWS, preferred_element_type=F32)
        grad = term if grad is None else grad + term
    total[:latent] = edge_ref[...]
    total[latent : 2 * latent] = grad
    total[2 * latent : 3 * latent] = lax.dot_general(
        tables[0][...], psum_ref[...], ROWS, preferred_element_type=F32
    )
    total[3 * latent :] = out_ref[...]
    feats, pairs, span, width = keep_ref.shape
    unit = span // 4
    bit = bit_ref[0]
    for m in range(pairs):
        for slot in range(4):
            for ref, which in ((keep_ref, bit), (send_ref, 1 - bit)):
                patch = 2 * m + which
                row = (patch * 3 + slot) * unit if slot < 3 else 3 * latent + patch * unit
                block = total[pl.ds(pl.multiple_of(row, unit), unit), :]
                for f in range(feats):
                    ref[f, m, slot * unit : (slot + 1) * unit, :] = block[:, f * width : (f + 1) * width].astype(
                        ref.dtype
                    )


def pack_call(bit, psum, edge_grad, out_grad, tables, sums, feats, patches):
    latent, hidden = edge_grad.shape
    shape = (feats, patches // 2, 4 * latent // patches, hidden // feats)
    vmem = pl.BlockSpec(memory_space=pltpu.VMEM)
    return pl.pallas_call(
        lambda *refs: pack_kernel(len(tables), *refs),
        in_specs=[pl.BlockSpec(memory_space=pltpu.SMEM)] + [vmem] * (3 + 2 * len(tables)),
        out_shape=[jax.ShapeDtypeStruct(shape, F32), jax.ShapeDtypeStruct(shape, BF16)],
        scratch_shapes=[pltpu.VMEM((4 * latent, hidden), F32)],
        compiler_params=params(),
        cost_estimate=cost(3.2),
        name="pack_grads",
    )(bit, psum, edge_grad, out_grad, *tables, *sums)


def coarse_sum_kernel(ids_ref, lat_ref, cot_ref, bit_ref, mine_ref, other_ref):
    latent = lat_ref.shape[1]
    half = mine_ref.shape[0]
    for ref, bit in ((mine_ref, bit_ref[0]), (other_ref, 1 - bit_ref[0])):
        places = lax.broadcasted_iota(jnp.int32, (half, ids_ref.shape[1]), 0) + bit * half
        live = jnp.where(places == ids_ref[...], 1.0, 0.0)
        hot = live.astype(BF16)
        ref[:, :latent] = dot(hot, lat_ref[...])
        ref[:, latent : 2 * latent] = dot(hot, cot_ref[...])
        ref[:, 2 * latent :] = jnp.broadcast_to(jnp.sum(live, axis=1, keepdims=True), (half, 128))


def coarse_sum_call(ids, lat, cot, bit, coarse):
    vmem = pl.BlockSpec(memory_space=pltpu.VMEM)
    half = jax.ShapeDtypeStruct((coarse // 2, 2 * lat.shape[1] + 128), F32)
    return pl.pallas_call(
        coarse_sum_kernel,
        in_specs=[vmem, vmem, vmem, pl.BlockSpec(memory_space=pltpu.SMEM)],
        out_shape=[half, half],
        compiler_params=params(),
        cost_estimate=cost(0.3),
        name="coarse_sums",
    )(ids, lat, cot, bit)


def add_split_kernel(bit_ref, keep_ref, got_ref, mine_ref, other_ref):
    bit = bit_ref[0]
    for ref, which in ((mine_ref, bit), (other_ref, 1 - bit)):
        for a in range(keep_ref.shape[0]):
            ref[a] = (keep_ref[a, which] + got_ref[a, which].astype(F32)).astype(ref.dtype)


def add_split_call(bit, keep, got, send_type):
    vmem = pl.BlockSpec(memory_space=pltpu.VMEM)
    shape = keep.shape[:1] + keep.shape[2:]
    return pl.pallas_call(
        add_split_kernel,
        in_specs=[pl.BlockSpec(memory_space=pltpu.SMEM), vmem, vmem],
        out_shape=[jax.ShapeDtypeStruct(shape, F32), jax.ShapeDtypeStruct(shape, send_type)],
        compiler_params=params(),
        cost_estimate=cost(1),
        name="add_split",
    )(bit, keep, got)


def last_grads_kernel(scale, keep_ref, got_ref, in_ref, out_ref):
    rows_in = in_ref.shape[0]
    in_ref[...] = (keep_ref[:rows_in] + got_ref[:rows_in].astype(F32)) * scale
    out_ref[...] = (keep_ref[rows_in:] + got_ref[rows_in:].astype(F32)) * scale


def last_grads_call(scale, keep, got, rows_in):
    span, width = keep.shape
    return pl.pallas_call(
        lambda *refs: last_grads_kernel(scale, *refs),
        out_shape=[
            jax.ShapeDtypeStruct((rows_in, width), F32),
            jax.ShapeDtypeStruct((span - rows_in, width), F32),
        ],
        compiler_params=params(),
        cost_estimate=cost(0.5),
        name="last_grads",
    )(keep, got)


def node_kernel(
    place_ref, ids_ref, lat_ref, cot_ref, agg_ref, psum_ref, weight_ref, *refs
):
    pieces, (new_ref, part_ref, total) = refs[:-3], refs[-3:]
    latent = lat_ref.shape[1]
    for j, piece in enumerate(pieces):
        size = piece.shape[0]
        total[pl.ds(pl.multiple_of(place_ref[j] * size, size), size), :] = piece[...]
    sums = total[...]
    means = sums[:, : 2 * latent] / jnp.maximum(sums[:, 2 * latent : 2 * latent + 1], 1.0)
    places = lax.broadcasted_iota(jnp.int32, (sums.shape[0], ids_ref.shape[1]), 0)
    hot = jnp.where(places == ids_ref[...], 1.0, 0.0).astype(BF16)
    high = means.astype(BF16)
    low = (means - high.astype(F32)).astype(BF16)
    pooled = lax.dot_general(hot, high, ROWS, preferred_element_type=F32)
    pooled = pooled + lax.dot_general(hot, low, ROWS, preferred_element_type=F32)
    new_ref[...] = (lat_ref[...].astype(F32) + agg_ref[...] + pooled[:, :latent]).astype(BF16)
    own = lax.dot_general(psum_ref[...], weight_ref[2 * latent :], COLS, preferred_element_type=F32)
    part_ref[...] = cot_ref[...].astype(F32) + own + pooled[:, latent:]


def node_call(place, ids, lat, cot, agg, psum, weight_in, pieces):
    vmem = pl.BlockSpec(memory_space=pltpu.VMEM)
    coarse = sum(piece.shape[0] for piece in pieces)
    return pl.pallas_call(
        node_kernel,
        in_specs=[pl.BlockSpec(memory_space=pltpu.SMEM)] + [vmem] * (6 + len(pieces)),
        scratch_shapes=[pltpu.VMEM((coarse, pieces[0].shape[1]), F32)],
        out_shape=[jax.ShapeDtypeStruct(lat.shape, BF16), jax.ShapeDtypeStruct(lat.shape, F32)],
        compiler_params=params(),
        cost_estimate=cost(1.1),
        name="node_outputs",
    )(place, ids, lat, cot, agg, psum, weight_in, *pieces)


def grad_node_kernel(part_ref, own_ref, far_ref, near_ref, weight_ref, out_ref):
    latent = part_ref.shape[1]
    total = own_ref[...].astype(F32) + far_ref[...].astype(F32) + near_ref[...].astype(F32)
    back = lax.dot_general(
        total.astype(BF16), weight_ref[latent : 2 * latent], COLS, preferred_element_type=F32
    )
    out_ref[...] = (part_ref[...] + back).astype(BF16)


def grad_node_call(part, own, far, near, weight_in):
    return pl.pallas_call(
        grad_node_kernel,
        out_shape=jax.ShapeDtypeStruct(part.shape, BF16),
        compiler_params=params(),
        cost_estimate=cost(8),
        name="grad_node",
    )(part, own, far, near, weight_in)


def xor_swap(value, axis, distance):
    size = lax.axis_size(axis)
    return lax.ppermute(value, axis, [(i, i ^ distance) for i in range(size)])


def bits_of(size):
    return [1 << b for b in range(size.bit_length() - 1)]


def split(value, dim, bit):
    mine = lax.dynamic_index_in_dim(value, bit, dim, keepdims=False)
    other = lax.dynamic_index_in_dim(value, 1 - bit, dim, keepdims=False)
    return mine, other


def coarse_reduce(sums, other, patch):
    width = sums.shape[1]
    bits = bits_of(lax.axis_size("patch"))
    sums = sums + xor_swap(other, "patch", 1)
    for distance in bits[1:]:
        mine, other = split(sums.reshape(2, -1, width), 0, (patch // distance) % 2)
        sums = mine + xor_swap(other, "patch", distance)
    for distance in bits_of(lax.axis_size("feat")):
        sums = sums + xor_swap(sums, "feat", distance)
    for distance in reversed(bits):
        got = xor_swap(sums, "patch", distance)
        first = (patch // distance) % 2 == 0
        sums = jnp.concatenate([jnp.where(first, sums, got), jnp.where(first, got, sums)], axis=0)
    return sums


def shards(
    node_lat,
    edge_lat,
    neighbours,
    send_rows,
    coarse_of,
    weight_in,
    bias_in,
    weight_out,
    norm_gain,
    edge_cotangent,
    node_cotangent,
):
    node_count, latent = node_lat.shape
    degree = edge_lat.shape[1]
    edge_count = node_count * degree
    rim_rows = send_rows.shape[0] // 2
    feat_count = lax.axis_size("feat")
    patch_count = lax.axis_size("patch")
    patch_total = feat_count * node_count
    coarse_total = COARSE_DEV * patch_count * feat_count
    feat = lax.axis_index("feat")
    patch = lax.axis_index("patch")
    block = min(512, edge_count)
    ring_up = [(i, (i + 1) % patch_count) for i in range(patch_count)]
    ring_down = [(j, i) for i, j in ring_up]

    def relative(ids):
        moved = ((ids // node_count) ^ feat) * node_count + ids % node_count
        return jnp.where(ids < patch_total, moved, ids)

    flat_edges = edge_lat.reshape(edge_count, latent)
    flat_cots = edge_cotangent.reshape(edge_count, latent)
    ids = relative(neighbours).T.reshape(edge_count)
    ids_col = ids[:, None]
    ids_row = ids[None, :]
    send_rel = relative(send_rows)
    bias = bias_in[None, :]
    gain = norm_gain[None, :]
    coarse_row = coarse_of[None, :]

    core_bit = (patch % 2).astype(jnp.int32).reshape(1)
    whole_step = feat_count == 4 and patch_count == 4

    if feat_count == 4:
        far = xor_swap(node_lat, "feat", 2)
        near = xor_swap(node_lat, "feat", 1)
        last = xor_swap(far, "feat", 1)
        pieces = [node_lat, near, far, last]
    else:
        pieces = [node_lat]
        for distance in bits_of(feat_count):
            pieces = pieces + [xor_swap(piece, "feat", distance) for piece in pieces]

    coarse, coarse_other = coarse_sum_call(coarse_row, node_lat, node_cotangent, core_bit, coarse_total)
    if whole_step:
        got = xor_swap(coarse_other, "patch", 1)
        high_bit = (patch // 2).astype(jnp.int32).reshape(1)
        halves = (1, 2, coarse.shape[0] // 2, coarse.shape[1])
        coarse, coarse_other = add_split_call(high_bit, coarse.reshape(halves), got.reshape(halves), F32)
        coarse, coarse_other = coarse[0], coarse_other[0]
        got = xor_swap(coarse_other, "patch", 2)
    else:
        coarse = coarse_reduce(coarse, coarse_other, patch)
        got = jnp.zeros_like(coarse)
    base = base_call(flat_edges, node_lat, ids_col, weight_in, bias, coarse, pieces[:-1], block)
    to_lower, to_upper, coarse = select_call(send_rel[:, None], coarse, got, base, pieces)
    from_lower = lax.ppermute(to_upper, "patch", ring_up)
    from_upper = lax.ppermute(to_lower, "patch", ring_down)
    got = xor_swap(coarse, "feat", 1) if whole_step else jnp.zeros_like(coarse)
    base = gather_call(base, ids_col, pieces[-1:], weight_in, patch_total - node_count, block)

    edge_new, aggregate, hidden_act, grad_proj, grad_pre, pre_sum, grad_edge, coarse = edge_call(
        base,
        ids_col,
        from_lower,
        from_upper,
        flat_edges,
        flat_cots,
        node_cotangent,
        weight_in,
        weight_out,
        gain,
        coarse,
        got,
        patch_total,
        block,
    )

    rim_low, rim_high = rim_sum_call(ids_row, grad_pre, patch_total, 2 * rim_rows)
    back_upper = lax.ppermute(rim_low, "patch", ring_down)
    back_lower = lax.ppermute(rim_high, "patch", ring_up)
    got = xor_swap(coarse, "feat", 2) if whole_step else jnp.zeros_like(coarse)
    patch_sum = patch_sum_call(ids_row, grad_pre, patch_total, node_count)
    edge_grad, out_grad = edge_grads_call(flat_edges, grad_pre, hidden_act, grad_proj)
    coarse, *sums = add_rim_call(send_rel[None, :], back_lower, back_upper, patch_sum, coarse, got, node_count)
    if feat_count == 4:
        relay = xor_swap(sums[3], "feat", 1)
        far_sum = (sums[2].astype(F32) + relay.astype(F32)).astype(BF16)
        got_far = xor_swap(far_sum, "feat", 2)
        got_near = xor_swap(sums[1], "feat", 1)
        own = [sums[0], got_far, got_near]
    else:
        parts = sums
        for distance in reversed(bits_of(feat_count)):
            got = [xor_swap(part, "feat", distance) for part in parts[distance:]]
            parts = [(a.astype(F32) + b.astype(F32)).astype(BF16) for a, b in zip(parts[:distance], got)]
        own = [parts[0], jnp.zeros_like(parts[0]), jnp.zeros_like(parts[0])]

    keep, send = pack_call(core_bit, pre_sum, edge_grad, out_grad, pieces, sums, feat_count, patch_count)
    span, width = keep.shape[2:]
    steps = [("patch", d) for d in bits_of(patch_count)[1:]] + [("feat", d) for d in bits_of(feat_count)]
    got = xor_swap(send, "patch", 1)
    for axis, distance in steps:
        index = patch if axis == "patch" else feat
        bit = ((index // distance) % 2).astype(jnp.int32).reshape(1)
        shape = (-1, 2, span, width)
        keep, send = add_split_call(bit, keep.reshape(shape), got.reshape(shape), BF16)
        got = xor_swap(send, axis, distance)
    scale = 1.0 / math.sqrt(edge_count * patch_count * feat_count)
    in_rows = 3 * latent // patch_count
    grads_in, grads_out = last_grads_call(scale, keep.reshape(span, width), got.reshape(span, width), in_rows)

    if whole_step:
        parts = [coarse] + [xor_swap(coarse, "patch", j) for j in range(1, 4)]
        place = jnp.stack([((patch ^ j) % 2) * 2 + (patch ^ j) // 2 for j in range(4)]).astype(jnp.int32)
    else:
        parts, place = [coarse], jnp.zeros((1,), jnp.int32)
    node_new, part = node_call(
        place, coarse_row, node_lat, node_cotangent, aggregate, pre_sum, weight_in, parts
    )
    grad_node = grad_node_call(part, *own, weight_in)
    return (
        edge_new.reshape(edge_lat.shape),
        node_new,
        grad_edge.reshape(edge_lat.shape),
        grad_node,
        grads_in,
        grads_out,
    )


def solution(mesh):
    return jax.shard_map(
        shards,
        mesh=mesh,
        in_specs=(
            P(("groups", "patch", "feat"), None),
            P(("groups", "patch", "feat"), None, None),
            P(None, ("patch", "feat")),
            P("patch"),
            P(("patch", "feat")),
            P(),
            P(),
            P(),
            P(),
            P(("groups", "patch", "feat"), None, None),
            P(("groups", "patch", "feat"), None),
        ),
        out_specs=(
            P(("groups", "patch", "feat"), None, None),
            P(("groups", "patch", "feat"), None),
            P(("groups", "patch", "feat"), None, None),
            P(("groups", "patch", "feat"), None),
            P(("groups", "patch"), "feat"),
            P(("groups", "patch"), "feat"),
        ),
        check_vma=False,
    )
```

time: 155 us -> 110 us (0.71)
  other arithmetic: 20.3 us -> 2.53 us
  Pallas kernels: 51.6 us -> 35.3 us
  matrix products: 11.1 us -> 0 us
  starting transfers between devices: 18.1 us -> 23.2 us
  local copies, waits for them, and re-layouts: 16.9 us -> 13.6 us
  waiting for transfers between devices: 35.4 us -> 33.7 us
    pallas_call x2 -> x1, Pallas kernels: 13.3 us -> 1.7 us  [gather_call(): pl.pallas_call(lambda *refs: gather_kernel(first, *refs), grid=(count //...]
    dot_general x8 -> x0, matrix products: 11.1 us -> none  [the longest x4 6.98 us: grad_dot(): return lax.dot_general(a, b, ROWS, preferred_element_type=F32)]
    unnamed x41 -> x60, local copies, waits for them, and re-layouts: 1.89 us -> 13 us
    add x7 -> x0, other arithmetic: 6.4 us -> none  [the longest x4 3.66 us: all_sum(): value = value + xor_swap(value, axis, distance)]
    concatenate x6 -> x0, other arithmetic: 5.29 us -> none  [the longest x1 1.94 us: shards(): jnp.concatenate([grad_dot(flat_edges, grad_pre), grad_dot(full_table, ful...]
    concatenate x3 -> x0, local copies, waits for them, and re-layouts: 4.92 us -> none  [the longest x2 4.91 us: shards(): jnp.concatenate([grads_in.reshape(patch_count, in_rows, hidden), grads_ou...]
    pallas_call x1, Pallas kernels: 16.5 us -> 12 us  [edge_call(): pl.pallas_call(lambda *refs: edge_kernel(first, degree, *refs), grid=(blo...]
    slice x5 -> x0, local copies, waits for them, and re-layouts: 4.19 us -> none  [the longest x1 1.86 us: shards(): piece = [chunks[j * node_count:(j + 1) * node_count] for j in range(4)]]
  transfers between devices with their start and end apart: 18 -> 21, of which waited for: 6 -> 11; matrix products, arithmetic and copies ran while one was open for 30% -> 3% of each run, Pallas kernels for 33% -> 11%
where the time goes in v2:
time: 110 us; the launch traced here: 109 us
  Pallas kernels  35.3 us (32%)
  waiting for transfers between devices  33.7 us (31%)
  starting transfers between devices  23.2 us (21%)
  local copies, waits for them, and re-layouts  13.6 us (12%)
  other arithmetic  2.53 us (2%)
    ppermute x17, waiting for transfers between devices, xor_swap(): return lax.ppermute(value, axis, [(i, i ^ distance) for i in range(size)])  31.8 us
    ppermute x17, starting transfers between devices, xor_swap(): return lax.ppermute(value, axis, [(i, i ^ distance) for i in range(size)])  19.6 us
    unnamed x60, local copies, waits for them, and re-layouts  13 us
    pallas_call x1, Pallas kernels, edge_call(): pl.pallas_call(lambda *refs: edge_kernel(first, degree, *refs), grid=(blo...  12 us
    pallas_call x1, Pallas kernels, base_call(): pl.pallas_call(lambda *refs: base_kernel(degree, *refs), grid=(count // b...  4.74 us
    pallas_call x1, Pallas kernels, pack_call(): pl.pallas_call(lambda *refs: pack_kernel(len(tables), *refs), in_specs=[p...  3.31 us
    pallas_call x1, Pallas kernels, patch_sum_call(): pl.pallas_call(patch_sum_kernel, grid=(count // block,), in_specs=[whole(...  2.85 us
    pallas_call x1, Pallas kernels, edge_grads_call(): pl.pallas_call(edge_grads_kernel, out_shape=[jax.ShapeDtypeStruct((latent...  2.35 us
  transfers between devices with their start and end apart: 21, of which 11 were waited for; matrix products, arithmetic and copies ran while one was open for 3% of the time, Pallas kernels for 11%

profile of v2, /device:TPU:0, one launch (start us, length us, event | category | flops | bytes accessed | tf_op | source)
XLA Modules:
  0.0 109.3 jit_solution(17007582991037908401)
XLA Ops:
  0.6 4.1 %collective-permute-start.2 = (bf16[256,512]{1,0:T(8,128)(2,1)}, bf16[256,512]{1,0:T(8,128)(2,1)S(1)}, u32[]{:S(2)}, u32[]{:S(2)}) collective-permute-start(bf16[256,512]{1,0:T(8,128)(2,1)} %refs_4_.1), channel_id=1, source_target_pairs={{0,2},{1,3},{2,0},{3,1},{4,6},{5,7},{6,4},{7,5},{8,10},{9,11},{10,... | collective-permute-start | bytes 786440 | tf_op jit(solution)/shard_map/ppermute | solution.py:517
  4.7 1.6 %collective-permute-start.1 = (bf16[256,512]{1,0:T(8,128)(2,1)}, bf16[256,512]{1,0:T(8,128)(2,1)S(1)}, u32[]{:S(2)}, u32[]{:S(2)}) collective-permute-start(bf16[256,512]{1,0:T(8,128)(2,1)} %refs_4_.1), channel_id=1, source_target_pairs={{0,1},{1,0},{2,3},{3,2},{4,5},{5,4},{6,7},{7,6},{8,9},{9,8},{10,11... | collective-permute-start | bytes 786440 | tf_op jit(solution)/shard_map/ppermute | solution.py:517
  13.3 1.6 %collective-permute-start.4 = (f32[16,1152]{1,0:T(8,128)S(1)}, f32[16,1152]{1,0:T(8,128)S(1)}, u32[]{:S(2)}, u32[]{:S(2)}) collective-permute-start(f32[16,1152]{1,0:T(8,128)S(1)} %bitcast.42), channel_id=1, source_target_pairs={{0,8},{4,12},{8,0},{12,4},{1,9},{5,13},{9,1},{13,5},{2,10},{6,14},... | collective-permute-start | bytes 221192 | tf_op jit(solution)/shard_map/ppermute | solution.py:517
  14.9 2.1 %collective-permute-done.2.refs_8_.refs_2_.refs_6_ = bf16[256,512]{1,0:T(8,128)(2,1)S(1)} collective-permute-done((bf16[256,512]{1,0:T(8,128)(2,1)}, bf16[256,512]{1,0:T(8,128)(2,1)S(1)}, u32[]{:S(2)}, u32[]{:S(2)}) %collective-permute-start.2) | collective-permute-done | bytes 262176 | tf_op jit(solution)/shard_map/ppermute | solution.py:517
  17.7 4.7 %base_terms.1.refs_0_.after_ref = f32[2048,512]{1,0:T(8,128)S(1)} custom-call(bf16[2048,512]{1,0:T(8,128)(2,1)S(1)} %bitcast.35, bf16[256,512]{1,0:T(8,128)(2,1)S(1)} %copy-done.2, s32[2048,1]{1,0:T(8,128)S(1)} %broadcast_in_dim_reshape.8.refs_2_.refs_1_, bf16[1536,512]{1,0:T(8,128)(2,1)S(1)} %copy-done, f32[1,512]{1,0:T(1,128)S(1)} %bitcast.43, ...), custom_call_target="tpu_custom_call" | custom-call | flops 5750000128 | bytes 1048576 | tf_op jit(solution)/shard_map/base_terms/pallas_call | solution.py:77
  22.5 1.9 %collective-permute-done.3.refs_2_.refs_3_.refs_7_ = bf16[256,512]{1,0:T(8,128)(2,1)S(1)} collective-permute-done((bf16[256,512]{1,0:T(8,128)(2,1)S(1)}, bf16[256,512]{1,0:T(8,128)(2,1)S(1)}, u32[]{:S(2)}, u32[]{:S(2)}) %collective-permute-start.3) | collective-permute-done | bytes 262176 | tf_op jit(solution)/shard_map/ppermute | solution.py:517
  24.9 1.6 %collective-permute-start.7 = (f32[16,1152]{1,0:T(8,128)S(1)}, f32[16,1152]{1,0:T(8,128)S(1)}, u32[]{:S(2)}, u32[]{:S(2)}) collective-permute-start(f32[16,1152]{1,0:T(8,128)S(1)} %get-tuple-element.48.refs_10_), channel_id=1, source_target_pairs={{0,1},{1,0},{2,3},{3,2},{4,5},{5,4},{6,7},{7,6},{8,9},{9,8},{10,11... | collective-permute-start | bytes 221192 | tf_op jit(solution)/shard_map/ppermute | solution.py:517
  26.5 1.8 %collective-permute-start.6 = (bf16[128,512]{1,0:T(8,128)(2,1)S(1)}, bf16[128,512]{1,0:T(8,128)(2,1)S(1)}, u32[]{:S(2)}, u32[]{:S(2)}) collective-permute-start(bf16[128,512]{1,0:T(8,128)(2,1)S(1)} %get-tuple-element.47), channel_id=1, source_target_pairs={{4,0},{8,4},{12,8},{0,12},{5,1},{9,5},{13,9},{1,13},{6,2},{10,6},{... | collective-permute-start | bytes 393224 | tf_op jit(solution)/shard_map/ppermute | solution.py:614
  28.3 1.7 %gather_terms.1.refs_0_ = f32[2048,512]{1,0:T(8,128)S(1)} custom-call(f32[2048,512]{1,0:T(8,128)S(1)} %base_terms.1.refs_0_.after_ref, s32[2048,1]{1,0:T(8,128)S(1)} %broadcast_in_dim_reshape.8.refs_2_.refs_1_, bf16[256,512]{1,0:T(8,128)(2,1)S(1)} %collective-permute-done.3.refs_2_.refs_3_.refs_7_, bf16[1536,512]{1,0:T(8,128)(2,1)S(1)} %copy-done), custom_call_target="tpu_custom_call" | custom-call | flops 2300000000 | bytes 1048576 | tf_op jit(solution)/shard_map/gather_terms/pallas_call | solution.py:228
  31.3 12.0 %edge_block.1 = (bf16[2048,512]{1,0:T(8,128)(2,1)}, f32[256,512]{1,0:T(8,128)S(1)}, bf16[2048,512]{1,0:T(8,128)(2,1)S(1)}, bf16[2048,512]{1,0:T(8,128)(2,1)S(1)}...) custom-call(f32[2048,512]{1,0:T(8,128)S(1)} %gather_terms.1.refs_0_,, ...), custom_call_target="tpu_custom_call" | custom-call | flops 13799999488 | bytes 1048576 | tf_op jit(solution)/shard_map/edge_block/pallas_call | solution.py:188
  44.1 2.8 %patch_sums.1.start_ref = f32[1024,512]{1,0:T(8,128)S(1)} custom-call(s32[1,2048]{1,0:T(1,128)S(1)} %broadcast_in_dim_reshape.7.refs_0_.ids_ref, bf16[2048,512]{1,0:T(8,128)(2,1)S(1)} %get-tuple-element.52.refs_1_.values_ref.gpre_ref), custom_call_target="tpu_custom_call" | custom-call | flops 3220000000 | bytes 1048576 | tf_op jit(solution)/shard_map/patch_sums/pallas_call | solution.py:297
  46.9 3.3 %collective-permute-start.10 = (f32[16,1152]{1,0:T(8,128)S(1)}, f32[16,1152]{1,0:T(8,128)S(1)}, u32[]{:S(2)}, u32[]{:S(2)}) collective-permute-start(f32[16,1152]{1,0:T(8,128)S(1)} %get-tuple-element.55.mine_ref), channel_id=1, source_target_pairs={{0,2},{1,3},{2,0},{3,1},{4,6},{5,7},{6,4},{7,5},{8,10},{9,11},{10,... | collective-permute-start | bytes 221192 | tf_op jit(solution)/shard_map/ppermute | solution.py:517
  52.0 2.3 %edge_grads.1 = (f32[512,512]{1,0:T(8,128)S(1)}, f32[512,512]{1,0:T(8,128)S(1)}) custom-call(bf16[2048,512]{1,0:T(8,128)(2,1)S(1)} %bitcast.37, bf16[2048,512]{1,0:T(8,128)(2,1)S(1)} %get-tuple-element.52.refs_1_.values_ref.gpre_ref, bf16[2048,512]{1,0:T(8,128)(2,1)S(1)} %get-tuple-element.64.hid_ref, bf16[2048,512]{1,0:T(8,128)(2,1)S(1)} %get-tuple-element.65.gproj_ref), custom_call_target="tpu_custom_call" | custom-call | flops 2760000000 | bytes 1048576 | tf_op jit(solution)/shard_map/edge_grads/pallas_call | solution.py:340
  55.2 1.4 %add_rim_sums.1 = (f32[16,1152]{1,0:T(8,128)}, bf16[256,512]{1,0:T(8,128)(2,1)S(1)}, bf16[256,512]{1,0:T(8,128)(2,1)}, bf16[256,512]{1,0:T(8,128)(2,1)S(1)}, bf16[256,512]{1,0:T(8,128)(2,1)}) custom-call(s32[1,256]{1,0:T(1,128)S(1)} %bitcast.33, bf16[128,512]{1,0:T(8,128)(2,1)S(1)} %collective-permute-done.8.low_ref, ...), custom_call_target="tpu_custom_call" | custom-call | flops 805000000 | bytes 1048576 | tf_op jit(solution)/shard_map/add_rim_sums/pallas_call | solution.py:324
  56.7 3.3 %pack_grads.1 = (f32[4,2,512,128]{3,2,1,0:T(8,128)S(1)}, bf16[4,2,512,128]{3,2,1,0:T(8,128)(2,1)}) custom-call(s32[1]{0:T(128)} %bitcast.5.bit_ref.refs_0_, bf16[256,512]{1,0:T(8,128)(2,1)S(1)} %get-tuple-element.51.psum_ref.refs_1_, f32[512,512]{1,0:T(8,128)S(1)} %get-tuple-element.66.refs_2_, f32[512,512]{1,0:T(8,128)S(1)} %get-tuple-element.67.refs_3_, ...), custom_call_target="tpu_custom_call" | custom-call | flops 3680000000 | bytes 1048576 | tf_op jit(solution)/shard_map/pack_grads/pallas_call | solution.py:385
  62.5 2.6 %collective-permute-done.17.got_ref = bf16[4,2,512,128]{3,2,1,0:T(8,128)(2,1)} collective-permute-done((bf16[4,2,512,128]{3,2,1,0:T(8,128)(2,1)}, bf16[4,2,512,128]{3,2,1,0:T(8,128)(2,1)}, u32[]{:S(2)}, u32[]{:S(2)}) %collective-permute-start.17) | collective-permute-done | bytes 1048608 | tf_op jit(solution)/shard_map/ppermute | solution.py:517
  65.2 1.6 %copy-done.22 = f32[4,2,512,128]{3,2,1,0:T(8,128)S(1)} copy-done((f32[4,2,512,128]{3,2,1,0:T(8,128)S(1)}, f32[4,2,512,128]{3,2,1,0:T(8,128)}, u32[]{:S(2)}) %copy-start.22) | copy-done | bytes 2097176
  66.7 1.4 %add_split.5 = (f32[4,512,128]{2,1,0:T(8,128)S(1)}, bf16[4,512,128]{2,1,0:T(8,128)(2,1)S(1)}) custom-call(s32[1]{0:T(128)} %bitcast.22.bit_ref, f32[4,2,512,128]{3,2,1,0:T(8,128)S(1)} %copy-done.22, bf16[4,2,512,128]{3,2,1,0:T(8,128)(2,1)} %collective-permute-done.17.got_ref), custom_call_target="tpu_custom_call" | custom-call | flops 1150000000 | bytes 1048576 | tf_op jit(solution)/shard_map/add_split/pallas_call | solution.py:431
  72.4 11.5 %collective-permute-done.18 = bf16[4,512,128]{2,1,0:T(8,128)(2,1)S(1)} collective-permute-done((bf16[4,512,128]{2,1,0:T(8,128)(2,1)S(1)}, bf16[4,512,128]{2,1,0:T(8,128)(2,1)S(1)}, u32[]{:S(2)}, u32[]{:S(2)}) %collective-permute-start.18) | collective-permute-done | bytes 524320 | tf_op jit(solution)/shard_map/ppermute | solution.py:517
  85.6 1.8 %collective-permute-start.19 = (bf16[2,512,128]{2,1,0:T(8,128)(2,1)S(1)}, bf16[2,512,128]{2,1,0:T(8,128)(2,1)S(1)}, u32[]{:S(2)}, u32[]{:S(2)}) collective-permute-start(bf16[2,512,128]{2,1,0:T(8,128)(2,1)S(1)} %get-tuple-element.73), channel_id=1, source_target_pairs={{0,1},{1,0},{2,3},{3,2},{4,5},{5,4},{6,7},{7,6},{8,9},{9,8},{10,11... | collective-permute-start | bytes 786440 | tf_op jit(solution)/shard_map/ppermute | solution.py:517
  87.4 1.7 %add_convert_fusion = bf16[256,512]{1,0:T(8,128)(2,1)} fusion(bf16[256,512]{1,0:T(8,128)(2,1)} %collective-permute-done.14, bf16[256,512]{1,0:T(8,128)(2,1)S(1)} %get-tuple-element.61.refs_10_), kind=kLoop, calls=%fused_computation | loop fusion | flops 524288 | bytes 786432 | tf_op jit(solution)/shard_map/convert_element_type | solution.py:644
  91.3 2.2 %node_outputs.1 = (bf16[256,512]{1,0:T(8,128)(2,1)}, f32[256,512]{1,0:T(8,128)S(1)}) custom-call(s32[4]{0:T(128)S(1)} %pad_add_fusion.place_ref, s32[1,256]{1,0:T(1,128)S(1)} %bitcast.46, bf16[256,512]{1,0:T(8,128)(2,1)S(1)} %copy-done.2, bf16[256,512]{1,0:T(8,128)(2,1)S(1)} %copy-done.8, f32[256,512]{1,0:T(8,128)S(1)} %copy-done.26, ...), custom_call_target="tpu_custom_call" | custom-call | flops 1264999936 | bytes 1048576 | tf_op jit(solution)/shard_map/node_outputs/pallas_call | solution.py:485
  93.5 8.8 %collective-permute-done.19 = bf16[2,512,128]{2,1,0:T(8,128)(2,1)S(1)} collective-permute-done((bf16[2,512,128]{2,1,0:T(8,128)(2,1)S(1)}, bf16[2,512,128]{2,1,0:T(8,128)(2,1)S(1)}, u32[]{:S(2)}, u32[]{:S(2)}) %collective-permute-start.19) | collective-permute-done | bytes 262176 | tf_op jit(solution)/shard_map/ppermute | solution.py:517
  104.3 4.4 %collective-permute-done.20 = bf16[1,512,128]{2,1,0:T(8,128)(2,1)S(1)} collective-permute-done((bf16[1,512,128]{2,1,0:T(8,128)(2,1)S(1)}, bf16[1,512,128]{2,1,0:T(8,128)(2,1)S(1)}, u32[]{:S(2)}, u32[]{:S(2)}) %collective-permute-start.20) | collective-permute-done | bytes 131104 | tf_op jit(solution)/shard_map/ppermute | solution.py:517
  (103 shorter events, 26.0 us)
Async XLA Ops:
  0.6 10.0 %copy-start.29 = (s32[256]{0:T(256)S(1)}, s32[256]{0:T(256)}, u32[]{:S(2)}) copy-start(s32[256]{0:T(256)} %param.14) | copy-start | bytes 3076
  0.6 16.3 %collective-permute-start.2 = (bf16[256,512]{1,0:T(8,128)(2,1)}, bf16[256,512]{1,0:T(8,128)(2,1)S(1)}, u32[]{:S(2)}, u32[]{:S(2)}) collective-permute-start(bf16[256,512]{1,0:T(8,128)(2,1)} %refs_4_.1), channel_id=1, source_target_pairs={{0,2},{1,3},{2,0},{3,1},{4,6},{5,7},{6,4},{7,5},{8,10},{9,11},{10,... | collective-permute-start | bytes 786440 | tf_op jit(solution)/shard_map/ppermute | solution.py:517
  4.7 13.0 %collective-permute-start.1 = (bf16[256,512]{1,0:T(8,128)(2,1)}, bf16[256,512]{1,0:T(8,128)(2,1)S(1)}, u32[]{:S(2)}, u32[]{:S(2)}) collective-permute-start(bf16[256,512]{1,0:T(8,128)(2,1)} %refs_4_.1), channel_id=1, source_target_pairs={{0,1},{1,0},{2,3},{3,2},{4,5},{5,4},{6,7},{7,6},{8,9},{9,8},{10,11... | collective-permute-start | bytes 786440 | tf_op jit(solution)/shard_map/ppermute | solution.py:517
  9.2 1.6 %collective-permute-start = (f32[32,1152]{1,0:T(8,128)S(1)}, f32[32,1152]{1,0:T(8,128)S(1)}, u32[]{:S(2)}, u32[]{:S(2)}) collective-permute-start(f32[32,1152]{1,0:T(8,128)S(1)} %get-tuple-element.43), channel_id=1, source_target_pairs={{0,4},{4,0},{8,12},{12,8},{1,5},{5,1},{9,13},{13,9},{2,6},{6,2},{1... | collective-permute-start | bytes 442376 | tf_op jit(solution)/shard_map/ppermute | solution.py:517
  13.3 9.2 %collective-permute-start.4 = (f32[16,1152]{1,0:T(8,128)S(1)}, f32[16,1152]{1,0:T(8,128)S(1)}, u32[]{:S(2)}, u32[]{:S(2)}) collective-permute-start(f32[16,1152]{1,0:T(8,128)S(1)} %bitcast.42), channel_id=1, source_target_pairs={{0,8},{4,12},{8,0},{12,4},{1,9},{5,13},{9,1},{13,5},{2,10},{6,14},... | collective-permute-start | bytes 221192 | tf_op jit(solution)/shard_map/ppermute | solution.py:517
  17.0 7.4 %collective-permute-start.3 = (bf16[256,512]{1,0:T(8,128)(2,1)S(1)}, bf16[256,512]{1,0:T(8,128)(2,1)S(1)}, u32[]{:S(2)}, u32[]{:S(2)}) collective-permute-start(bf16[256,512]{1,0:T(8,128)(2,1)S(1)} %collective-permute-done.2.refs_8_.refs_2_.refs_6_), channel_id=1, source_target_pairs={{0,1},{1,0},{2,3},{3,2},{4,5},{5,4},{6,7},{7,6},{8,9},{9,8},{10,11... | collective-permute-start | bytes 786440 | tf_op jit(solution)/shard_map/ppermute | solution.py:517
  24.9 5.1 %collective-permute-start.7 = (f32[16,1152]{1,0:T(8,128)S(1)}, f32[16,1152]{1,0:T(8,128)S(1)}, u32[]{:S(2)}, u32[]{:S(2)}) collective-permute-start(f32[16,1152]{1,0:T(8,128)S(1)} %get-tuple-element.48.refs_10_), channel_id=1, source_target_pairs={{0,1},{1,0},{2,3},{3,2},{4,5},{5,4},{6,7},{7,6},{8,9},{9,8},{10,11... | collective-permute-start | bytes 221192 | tf_op jit(solution)/shard_map/ppermute | solution.py:517
  26.5 4.4 %collective-permute-start.5 = (bf16[128,512]{1,0:T(8,128)(2,1)S(1)}, bf16[128,512]{1,0:T(8,128)(2,1)S(1)}, u32[]{:S(2)}, u32[]{:S(2)}) collective-permute-start(bf16[128,512]{1,0:T(8,128)(2,1)S(1)} %get-tuple-element.46), channel_id=1, source_target_pairs={{0,4},{4,8},{8,12},{12,0},{1,5},{5,9},{9,13},{13,1},{2,6},{6,10},{... | collective-permute-start | bytes 393224 | tf_op jit(solution)/shard_map/ppermute | solution.py:613
  26.5 4.8 %collective-permute-start.6 = (bf16[128,512]{1,0:T(8,128)(2,1)S(1)}, bf16[128,512]{1,0:T(8,128)(2,1)S(1)}, u32[]{:S(2)}, u32[]{:S(2)}) collective-permute-start(bf16[128,512]{1,0:T(8,128)(2,1)S(1)} %get-tuple-element.47), channel_id=1, source_target_pairs={{4,0},{8,4},{12,8},{0,12},{5,1},{9,5},{13,9},{1,13},{6,2},{10,6},{... | collective-permute-start | bytes 393224 | tf_op jit(solution)/shard_map/ppermute | solution.py:614
  43.4 13.3 %copy-start.27 = (bf16[256,512]{1,0:T(8,128)(2,1)}, bf16[256,512]{1,0:T(8,128)(2,1)S(1)}, u32[]{:S(2)}) copy-start(bf16[256,512]{1,0:T(8,128)(2,1)S(1)} %get-tuple-element.51.psum_ref.refs_1_) | copy-start | bytes 786436
  46.9 7.7 %collective-permute-start.10 = (f32[16,1152]{1,0:T(8,128)S(1)}, f32[16,1152]{1,0:T(8,128)S(1)}, u32[]{:S(2)}, u32[]{:S(2)}) collective-permute-start(f32[16,1152]{1,0:T(8,128)S(1)} %get-tuple-element.55.mine_ref), channel_id=1, source_target_pairs={{0,2},{1,3},{2,0},{3,1},{4,6},{5,7},{6,4},{7,5},{8,10},{9,11},{10,... | collective-permute-start | bytes 221192 | tf_op jit(solution)/shard_map/ppermute | solution.py:517
  50.3 4.4 %collective-permute-start.8 = (bf16[128,512]{1,0:T(8,128)(2,1)S(1)}, bf16[128,512]{1,0:T(8,128)(2,1)S(1)}, u32[]{:S(2)}, u32[]{:S(2)}) collective-permute-start(bf16[128,512]{1,0:T(8,128)(2,1)S(1)} %get-tuple-element.53), channel_id=1, source_target_pairs={{0,4},{4,8},{8,12},{12,0},{1,5},{5,9},{9,13},{13,1},{2,6},{6,10},{... | collective-permute-start | bytes 393224 | tf_op jit(solution)/shard_map/ppermute | solution.py:637
  51.2 4.0 %collective-permute-start.9 = (bf16[128,512]{1,0:T(8,128)(2,1)S(1)}, bf16[128,512]{1,0:T(8,128)(2,1)S(1)}, u32[]{:S(2)}, u32[]{:S(2)}) collective-permute-start(bf16[128,512]{1,0:T(8,128)(2,1)S(1)} %get-tuple-element.54), channel_id=1, source_target_pairs={{4,0},{8,4},{12,8},{0,12},{5,1},{9,5},{13,9},{1,13},{6,2},{10,6},{... | collective-permute-start | bytes 393224 | tf_op jit(solution)/shard_map/ppermute | solution.py:636
  61.3 3.8 %collective-permute-start.17 = (bf16[4,2,512,128]{3,2,1,0:T(8,128)(2,1)}, bf16[4,2,512,128]{3,2,1,0:T(8,128)(2,1)}, u32[]{:S(2)}, u32[]{:S(2)}) collective-permute-start(bf16[4,2,512,128]{3,2,1,0:T(8,128)(2,1)} %get-tuple-element.69), channel_id=1, source_target_pairs={{0,4},{4,0},{8,12},{12,8},{1,5},{5,1},{9,13},{13,9},{2,6},{6,2},{1... | collective-permute-start | bytes 3145736 | tf_op jit(solution)/shard_map/ppermute | solution.py:517
  69.2 14.8 %collective-permute-start.18 = (bf16[4,512,128]{2,1,0:T(8,128)(2,1)S(1)}, bf16[4,512,128]{2,1,0:T(8,128)(2,1)S(1)}, u32[]{:S(2)}, u32[]{:S(2)}) collective-permute-start(bf16[4,512,128]{2,1,0:T(8,128)(2,1)S(1)} %get-tuple-element.71), channel_id=1, source_target_pairs={{0,8},{4,12},{8,0},{12,4},{1,9},{5,13},{9,1},{13,5},{2,10},{6,14},... | collective-permute-start | bytes 1572872 | tf_op jit(solution)/shard_map/ppermute | solution.py:517
  70.3 15.3 %collective-permute-start.14 = (bf16[256,512]{1,0:T(8,128)(2,1)}, bf16[256,512]{1,0:T(8,128)(2,1)}, u32[]{:S(2)}, u32[]{:S(2)}) collective-permute-start(bf16[256,512]{1,0:T(8,128)(2,1)} %get-tuple-element.62.refs_11_), channel_id=1, source_target_pairs={{0,1},{1,0},{2,3},{3,2},{4,5},{5,4},{6,7},{7,6},{8,9},{9,8},{10,11... | collective-permute-start | bytes 786440 | tf_op jit(solution)/shard_map/ppermute | solution.py:517
  70.6 18.5 %collective-permute-start.13 = (f32[16,1152]{1,0:T(8,128)}, f32[16,1152]{1,0:T(8,128)S(1)}, u32[]{:S(2)}, u32[]{:S(2)}) collective-permute-start(f32[16,1152]{1,0:T(8,128)} %get-tuple-element.56.refs_0_), channel_id=1, source_target_pairs={{0,12},{4,8},{8,4},{12,0},{1,13},{5,9},{9,5},{13,1},{2,14},{6,10},... | collective-permute-start | bytes 221192 | tf_op jit(solution)/shard_map/ppermute | solution.py:517
  70.9 18.3 %collective-permute-start.12 = (f32[16,1152]{1,0:T(8,128)}, f32[16,1152]{1,0:T(8,128)}, u32[]{:S(2)}, u32[]{:S(2)}) collective-permute-start(f32[16,1152]{1,0:T(8,128)} %get-tuple-element.56.refs_0_), channel_id=1, source_target_pairs={{0,8},{4,12},{8,0},{12,4},{1,9},{5,13},{9,1},{13,5},{2,10},{6,14},... | collective-permute-start | bytes 221192 | tf_op jit(solution)/shard_map/ppermute | solution.py:517
  72.0 17.2 %collective-permute-start.11 = (f32[16,1152]{1,0:T(8,128)}, f32[16,1152]{1,0:T(8,128)}, u32[]{:S(2)}, u32[]{:S(2)}) collective-permute-start(f32[16,1152]{1,0:T(8,128)} %get-tuple-element.56.refs_0_), channel_id=1, source_target_pairs={{0,4},{4,0},{8,12},{12,8},{1,5},{5,1},{9,13},{13,9},{2,6},{6,2},{1... | collective-permute-start | bytes 221192 | tf_op jit(solution)/shard_map/ppermute | solution.py:517
  83.9 18.5 %collective-permute-start.16 = (bf16[256,512]{1,0:T(8,128)(2,1)}, bf16[256,512]{1,0:T(8,128)(2,1)S(1)}, u32[]{:S(2)}, u32[]{:S(2)}) collective-permute-start(bf16[256,512]{1,0:T(8,128)(2,1)} %get-tuple-element.63.refs_9_), channel_id=1, source_target_pairs={{0,1},{1,0},{2,3},{3,2},{4,5},{5,4},{6,7},{7,6},{8,9},{9,8},{10,11... | collective-permute-start | bytes 786440 | tf_op jit(solution)/shard_map/ppermute | solution.py:517
  85.6 16.7 %collective-permute-start.19 = (bf16[2,512,128]{2,1,0:T(8,128)(2,1)S(1)}, bf16[2,512,128]{2,1,0:T(8,128)(2,1)S(1)}, u32[]{:S(2)}, u32[]{:S(2)}) collective-permute-start(bf16[2,512,128]{2,1,0:T(8,128)(2,1)S(1)} %get-tuple-element.73), channel_id=1, source_target_pairs={{0,1},{1,0},{2,3},{3,2},{4,5},{5,4},{6,7},{7,6},{8,9},{9,8},{10,11... | collective-permute-start | bytes 786440 | tf_op jit(solution)/shard_map/ppermute | solution.py:517
  89.1 13.5 %collective-permute-start.15 = (bf16[256,512]{1,0:T(8,128)(2,1)}, bf16[256,512]{1,0:T(8,128)(2,1)S(1)}, u32[]{:S(2)}, u32[]{:S(2)}) collective-permute-start(bf16[256,512]{1,0:T(8,128)(2,1)} %add_convert_fusion), channel_id=1, source_target_pairs={{0,2},{1,3},{2,0},{3,1},{4,6},{5,7},{6,4},{7,5},{8,10},{9,11},{10,... | collective-permute-start | bytes 786440 | tf_op jit(solution)/shard_map/ppermute | solution.py:517
  91.3 11.0 %copy-start.18 = (f32[2,512,128]{2,1,0:T(8,128)S(1)}, f32[2,512,128]{2,1,0:T(8,128)}, u32[]{:S(2)}) copy-start(f32[2,512,128]{2,1,0:T(8,128)} %copy-done.17) | copy-start | bytes 1572868
  102.3 6.3 %collective-permute-start.20 = (bf16[1,512,128]{2,1,0:T(8,128)(2,1)S(1)}, bf16[1,512,128]{2,1,0:T(8,128)(2,1)S(1)}, u32[]{:S(2)}, u32[]{:S(2)}) collective-permute-start(bf16[1,512,128]{2,1,0:T(8,128)(2,1)S(1)} %get-tuple-element.75), channel_id=1, source_target_pairs={{0,2},{1,3},{2,0},{3,1},{4,6},{5,7},{6,4},{7,5},{8,10},{9,11},{10,... | collective-permute-start | bytes 393224 | tf_op jit(solution)/shard_map/ppermute | solution.py:517
  (27 other events, 70.7 us)

commit v3 on v2

--- a/solution.py
+++ b/solution.py
@@ -28,6 +28,47 @@
     return pl.CostEstimate(flops=int(micros * 1.15e9), bytes_accessed=1 << 20, transcendentals=0)
 
 
+class Order:
+    token = None
+
+
+def launch(kernel, out_shape, in_specs=None, out_specs=None, grid=None, **settings):
+    outs = list(out_shape) if isinstance(out_shape, (list, tuple)) else [out_shape]
+    mark = jax.ShapeDtypeStruct((8, 128), F32)
+
+    def call(*args):
+        count = len(args)
+        late = [] if Order.token is None else [Order.token]
+        vmem = pl.BlockSpec(memory_space=pltpu.VMEM)
+        specs = list(in_specs or [vmem] * count) + [pl.BlockSpec(memory_space=pl.ANY)] * len(late)
+        end = count + len(late) + len(outs)
+
+        def body(*refs):
+            refs[end][...] = jnp.zeros((8, 128), F32)
+            kernel(*refs[:count], *refs[count + len(late) : end], *refs[end + 1 :])
+
+        if grid is None:
+            places, more = [vmem] * (len(outs) + 1), {}
+        else:
+            places = list(out_specs) if isinstance(out_specs, (list, tuple)) else [out_specs]
+            places, more = places + [pl.BlockSpec((8, 128), lambda i: (0, 0))], {"grid": grid}
+        results = pl.pallas_call(
+            body, out_shape=outs + [mark], in_specs=specs, out_specs=places, **more, **settings
+        )(*args, *late)
+        Order.token = results[-1]
+        return results[:-1] if isinstance(out_shape, (list, tuple)) else results[0]
+
+    return call
+
+
+def streamed(array):
+    return pltpu.with_memory_space_constraint(array, pltpu.HBM)
+
+
+def held(array):
+    return pltpu.with_memory_space_constraint(array, pltpu.VMEM)
+
+
 def whole(array):
     zeros = (0,) * array.ndim
     return pl.BlockSpec(array.shape, lambda i: zeros)
@@ -52,7 +93,7 @@
         at += size
 
 
-def base_kernel(degree, edge_ref, node_ref, ids_ref, weight_ref, bias_ref, after_ref, *refs):
+def base_kernel(degree, edge_ref, node_ref, ids_ref, weight_ref, bias_ref, *refs):
     pieces, (out_ref, table) = refs[:-2], refs[-2:]
     latent = edge_ref.shape[1]
 
@@ -69,12 +110,12 @@
     out_ref[...] = total.reshape(edges, hidden)
 
 
-def base_call(edges, nodes, ids, weight_in, bias, after, pieces, block):
+def base_call(edges, nodes, ids, weight_in, bias, pieces, block):
     count, latent = edges.shape
     hidden = weight_in.shape[1]
     degree = count // nodes.shape[0]
     size = sum(piece.shape[0] for piece in pieces)
-    return pl.pallas_call(
+    return launch(
         lambda *refs: base_kernel(degree, *refs),
         grid=(count // block,),
         in_specs=[
@@ -83,16 +124,15 @@
             rows(ids, block),
             whole(weight_in),
             whole(bias),
-            pl.BlockSpec(memory_space=pl.ANY),
         ]
         + [whole(piece) for piece in pieces],
         out_specs=pl.BlockSpec((block, hidden), lambda i: (i, 0)),
         out_shape=jax.ShapeDtypeStruct((count, hidden), F32),
         scratch_shapes=[pltpu.VMEM((size, hidden), BF16)],
         compiler_params=params(),
-        cost_estimate=cost(5),
+        cost_estimate=cost(15),
         name="base_terms",
-    )(edges, nodes, ids, weight_in, bias, after, *pieces)
+    )(streamed(edges), nodes, ids, weight_in, bias, *pieces)
 
 
 def edge_kernel(
@@ -100,6 +140,7 @@
     degree,
     base_ref,
     ids_ref,
+    last_ref,
     low_ref,
     high_ref,
     edge_ref,
@@ -108,8 +149,6 @@
     weight_ref,
     out_w_ref,
     gain_ref,
-    mine_ref,
-    got_ref,
     new_ref,
     agg_ref,
     hid_ref,
@@ -117,24 +156,20 @@
     gpre_ref,
     psum_ref,
     gedge_ref,
-    sum_ref,
     table,
 ):
     latent = low_ref.shape[1]
-    half = low_ref.shape[0]
 
     @pl.when(pl.program_id(0) == 0)
     def _():
-        table[:half] = dot(low_ref[...], weight_ref[latent : 2 * latent]).astype(BF16)
-        table[half:] = dot(high_ref[...], weight_ref[latent : 2 * latent]).astype(BF16)
-        sum_ref[...] = mine_ref[...] + got_ref[...]
+        fill_table(table, (last_ref, low_ref, high_ref), weight_ref)
 
     ids = ids_ref[...]
     edges = ids.shape[0]
     nodes = edges // degree
-    limit = first + 2 * half
+    limit = first + table.shape[0]
     live = jnp.where(ids < limit, 1.0, 0.0)
-    value = base_ref[...] + dot(one_hot(ids, first, 2 * half), table[...])
+    value = base_ref[...] + dot(one_hot(ids, first, table.shape[0]), table[...])
     sig = jax.nn.sigmoid(value)
     act = value * sig
     slope = sig + act * (1.0 - sig)
@@ -162,7 +197,7 @@
     gedge_ref[...] = (cot + back).astype(BF16)
 
 
-def edge_call(base, ids, low, high, edges, cots, ncot, weight_in, weight_out, gain, mine, got, first, block):
+def edge_call(base, ids, last, low, high, edges, cots, ncot, weight_in, weight_out, gain, first, block):
     count, latent = edges.shape
     hidden = weight_in.shape[1]
     degree = count // ncot.shape[0]
@@ -183,14 +218,14 @@
         like(hidden, BF16, block, count),
         like(hidden, BF16, small, count // degree),
         like(latent, BF16, block, count),
-        (whole(mine), jax.ShapeDtypeStruct(mine.shape, F32)),
     ]
-    return pl.pallas_call(
+    return launch(
         lambda *refs: edge_kernel(first, degree, *refs),
         grid=(blocks,),
         in_specs=[
             rows(base, block),
             rows(ids, block),
+            whole(last),
             whole(low),
             whole(high),
             rows(edges, block),
@@ -199,47 +234,18 @@
             whole(weight_in),
             whole(weight_out),
             whole(gain),
-            whole(mine),
-            whole(got),
         ],
         out_specs=[spec for spec, _ in outs],
         out_shape=[shape for _, shape in outs],
-        scratch_shapes=[pltpu.VMEM((2 * low.shape[0], hidden), BF16)],
-        compiler_params=params(),
-        cost_estimate=cost(12),
+        scratch_shapes=[pltpu.VMEM((last.shape[0] + 2 * low.shape[0], hidden), BF16)],
+        compiler_params=params(),
+        cost_estimate=cost(36),
         name="edge_block",
-    )(base, ids, low, high, edges, cots, ncot, weight_in, weight_out, gain, mine, got)
-
-
-def gather_kernel(first, base_ref, ids_ref, *refs):
-    pieces, (weight_ref, out_ref, table) = refs[:-3], refs[-3:]
-
-    @pl.when(pl.program_id(0) == 0)
-    def _():
-        fill_table(table, pieces, weight_ref)
-
-    hot = one_hot(ids_ref[...], first, table.shape[0])
-    out_ref[...] = base_ref[...] + dot(hot, table[...])
-
-
-def gather_call(base, ids, pieces, weight_in, first, block):
-    count, hidden = base.shape
-    size = sum(piece.shape[0] for piece in pieces)
-    return pl.pallas_call(
-        lambda *refs: gather_kernel(first, *refs),
-        grid=(count // block,),
-        in_specs=[rows(base, block), rows(ids, block)] + [whole(piece) for piece in pieces] + [whole(weight_in)],
-        out_specs=rows(base, block),
-        out_shape=jax.ShapeDtypeStruct(base.shape, F32),
-        scratch_shapes=[pltpu.VMEM((size, hidden), BF16)],
-        compiler_params=params(),
-        cost_estimate=cost(2),
-        name="gather_terms",
-    )(base, ids, *pieces, weight_in)
-
-
-def select_kernel(ids_ref, mine_ref, got_ref, after_ref, *refs):
-    pieces, (low_ref, high_ref, sum_ref) = refs[:-3], refs[-3:]
+    )(streamed(base), ids, last, low, high, streamed(edges), streamed(cots), ncot, weight_in, weight_out, gain)
+
+
+def select_kernel(ids_ref, *refs):
+    pieces, (low_ref, high_ref) = refs[:-2], refs[-2:]
     total, at = None, 0
     for piece in pieces:
         term = dot(one_hot(ids_ref[...], at, piece.shape[0]), piece[...])
@@ -248,21 +254,18 @@
     half = low_ref.shape[0]
     low_ref[...] = total[:half].astype(BF16)
     high_ref[...] = total[half:].astype(BF16)
-    sum_ref[...] = mine_ref[...] + got_ref[...]
-
-
-def select_call(ids, mine, got, after, pieces):
+
+
+def select_call(ids, pieces):
     count, width = ids.shape[0], pieces[0].shape[1]
     half = jax.ShapeDtypeStruct((count // 2, width), BF16)
-    vmem = pl.BlockSpec(memory_space=pltpu.VMEM)
-    return pl.pallas_call(
+    return launch(
         select_kernel,
-        in_specs=[vmem] * 3 + [pl.BlockSpec(memory_space=pl.ANY)] + [vmem] * len(pieces),
-        out_shape=[half, half, jax.ShapeDtypeStruct(mine.shape, F32)],
-        compiler_params=params(),
-        cost_estimate=cost(0.7),
+        out_shape=[half, half],
+        compiler_params=params(),
+        cost_estimate=cost(2),
         name="select_rows",
-    )(ids, mine, got, after, *pieces)
+    )(ids, *pieces)
 
 
 def rim_sum_kernel(first, ids_ref, values_ref, low_ref, high_ref):
@@ -276,11 +279,11 @@
 
 def rim_sum_call(ids, values, first, count):
     half = jax.ShapeDtypeStruct((count // 2, values.shape[1]), BF16)
-    return pl.pallas_call(
+    return launch(
         lambda *refs: rim_sum_kernel(first, *refs),
         out_shape=[half, half],
         compiler_params=params(),
-        cost_estimate=cost(0.7),
+        cost_estimate=cost(2.4),
         name="rim_sums",
     )(ids, values)
 
@@ -294,38 +297,49 @@
 
 def patch_sum_call(ids, values, count, block):
     width = values.shape[1]
-    return pl.pallas_call(
+    return launch(
         patch_sum_kernel,
         grid=(count // block,),
         in_specs=[whole(ids), whole(values)],
         out_specs=pl.BlockSpec((block, width), lambda i: (i, 0)),
         out_shape=jax.ShapeDtypeStruct((count, width), F32),
         compiler_params=params(),
-        cost_estimate=cost(2.8),
+        cost_estimate=cost(0.5),
         name="patch_sums",
     )(ids, values)
 
 
-def add_rim_kernel(ids_ref, low_ref, high_ref, start_ref, mine_ref, got_ref, sum_ref, *outs):
-    sum_ref[...] = mine_ref[...] + got_ref[...]
+def add_rim_kernel(ids_ref, low_ref, high_ref, start_ref, mine_ref, got_ref, *outs):
     half = low_ref.shape[0]
     size = outs[0].shape[0]
+    latent = start_ref.shape[1]
+    coarse = mine_ref[...] + got_ref[...]
+    few = coarse.shape[0]
+    counts = coarse[:, 2 * latent :]
+    high = jnp.floor(counts * (1.0 / 64.0))
     for j, out in enumerate(outs):
         places = lax.broadcasted_iota(jnp.int32, (size, 2 * half), 0) + j * size
         hot = jnp.where(places == ids_ref[...], 1.0, 0.0).astype(BF16)
         total = start_ref[j * size : (j + 1) * size] + dot(hot[:, :half], low_ref[...])
         total = total + dot(hot[:, half:], high_ref[...])
-        out[...] = total.astype(BF16)
-
-
-def add_rim_call(ids, low, high, start, mine, got, size):
+        out[:size] = total.astype(BF16)
+        if out.shape[0] > size:
+            out[size : size + few] = coarse[:, :latent].astype(BF16)
+            out[size + few : size + 2 * few] = coarse[:, latent : 2 * latent].astype(BF16)
+            out[size + 2 * few :] = jnp.zeros((few, latent), BF16)
+            out[size + 2 * few :, :128] = high.astype(BF16)
+            out[size + 2 * few :, 128:256] = (counts - 64.0 * high).astype(BF16)
+
+
+def add_rim_call(ids, low, high, start, mine, got, size, extended):
     count, width = start.shape
-    piece = jax.ShapeDtypeStruct((size, width), BF16)
-    return pl.pallas_call(
+    pieces = count // size
+    extra = [3 * mine.shape[0] if extended and j == pieces - 1 else 0 for j in range(pieces)]
+    return launch(
         add_rim_kernel,
-        out_shape=[jax.ShapeDtypeStruct(mine.shape, F32)] + [piece] * (count // size),
-        compiler_params=params(),
-        cost_estimate=cost(0.7),
+        out_shape=[jax.ShapeDtypeStruct((size + more, width), BF16) for more in extra],
+        compiler_params=params(),
+        cost_estimate=cost(15.0),
         name="add_rim_sums",
     )(ids, low, high, start, mine, got)
 
@@ -337,25 +351,27 @@
 
 def edge_grads_call(edges, gpre, hid, gproj):
     latent, hidden = edges.shape[1], gpre.shape[1]
-    return pl.pallas_call(
+    return launch(
         edge_grads_kernel,
         out_shape=[
             jax.ShapeDtypeStruct((latent, hidden), F32),
             jax.ShapeDtypeStruct((hidden, latent), F32),
         ],
         compiler_params=params(),
-        cost_estimate=cost(2.4),
+        cost_estimate=cost(0.5),
         name="edge_grads",
     )(edges, gpre, hid, gproj)
 
 
-def pack_kernel(pieces, bit_ref, psum_ref, edge_ref, out_ref, *refs):
-    tables, sums = refs[:pieces], refs[pieces : 2 * pieces]
-    keep_ref, send_ref, total = refs[2 * pieces :]
+def pack_kernel(pieces, bit_ref, psum_ref, edge_ref, out_ref, patch_ref, low_ref, high_ref, *refs):
+    tables = refs[:pieces]
+    keep_ref, send_ref, total = refs[pieces:]
     latent = tables[0].shape[1]
+    size = tables[0].shape[0]
+    parts = [patch_ref[j * size : (j + 1) * size].astype(BF16) for j in range(pieces - 2)]
     grad = None
-    for table, part in zip(tables, sums):
-        term = lax.dot_general(table[...], part[...], ROWS, preferred_element_type=F32)
+    for table, part in zip(tables, parts + [low_ref[...], high_ref[...]]):
+        term = lax.dot_general(table[...], part, ROWS, preferred_element_type=F32)
         grad = term if grad is None else grad + term
     total[:latent] = edge_ref[...]
     total[latent : 2 * latent] = grad
@@ -378,19 +394,19 @@
                     )
 
 
-def pack_call(bit, psum, edge_grad, out_grad, tables, sums, feats, patches):
+def pack_call(bit, psum, edge_grad, out_grad, patch_sum, low, high, tables, feats, patches):
     latent, hidden = edge_grad.shape
     shape = (feats, patches // 2, 4 * latent // patches, hidden // feats)
     vmem = pl.BlockSpec(memory_space=pltpu.VMEM)
-    return pl.pallas_call(
+    return launch(
         lambda *refs: pack_kernel(len(tables), *refs),
-        in_specs=[pl.BlockSpec(memory_space=pltpu.SMEM)] + [vmem] * (3 + 2 * len(tables)),
+        in_specs=[pl.BlockSpec(memory_space=pltpu.SMEM)] + [vmem] * (6 + len(tables)),
         out_shape=[jax.ShapeDtypeStruct(shape, F32), jax.ShapeDtypeStruct(shape, BF16)],
         scratch_shapes=[pltpu.VMEM((4 * latent, hidden), F32)],
         compiler_params=params(),
-        cost_estimate=cost(3.2),
+        cost_estimate=cost(0.5),
         name="pack_grads",
-    )(bit, psum, edge_grad, out_grad, *tables, *sums)
+    )(bit, psum, edge_grad, out_grad, patch_sum, low, high, *tables)
 
 
 def coarse_sum_kernel(ids_ref, lat_ref, cot_ref, bit_ref, mine_ref, other_ref):
@@ -408,14 +424,48 @@
 def coarse_sum_call(ids, lat, cot, bit, coarse):
     vmem = pl.BlockSpec(memory_space=pltpu.VMEM)
     half = jax.ShapeDtypeStruct((coarse // 2, 2 * lat.shape[1] + 128), F32)
-    return pl.pallas_call(
+    return launch(
         coarse_sum_kernel,
         in_specs=[vmem, vmem, vmem, pl.BlockSpec(memory_space=pltpu.SMEM)],
         out_shape=[half, half],
         compiler_params=params(),
-        cost_estimate=cost(0.3),
+        cost_estimate=cost(1),
         name="coarse_sums",
     )(ids, lat, cot, bit)
+
+
+def add_pair_kernel(a_ref, b_ref, out_ref):
+    out_ref[...] = (a_ref[...].astype(F32) + b_ref[...].astype(F32)).astype(out_ref.dtype)
+
+
+def add_pair_call(a, b):
+    return launch(
+        add_pair_kernel,
+        out_shape=jax.ShapeDtypeStruct(a.shape, a.dtype),
+        compiler_params=params(),
+        cost_estimate=cost(1.0),
+        name="add_pair",
+    )(a, b)
+
+
+def far_sum_kernel(own_ref, sent_ref, got_ref, far_ref, coarse_ref):
+    size = own_ref.shape[0]
+    far_ref[...] = (own_ref[...].astype(F32) + got_ref[:size].astype(F32)).astype(BF16)
+    coarse_ref[...] = sent_ref[size:].astype(F32) + got_ref[size:].astype(F32)
+
+
+def far_sum_call(own, sent, got):
+    size, width = own.shape
+    return launch(
+        far_sum_kernel,
+        out_shape=[
+            jax.ShapeDtypeStruct((size, width), BF16),
+            jax.ShapeDtypeStruct((sent.shape[0] - size, width), F32),
+        ],
+        compiler_params=params(),
+        cost_estimate=cost(1.0),
+        name="far_sum",
+    )(own, sent, got)
 
 
 def add_split_kernel(bit_ref, keep_ref, got_ref, mine_ref, other_ref):
@@ -428,12 +478,12 @@
 def add_split_call(bit, keep, got, send_type):
     vmem = pl.BlockSpec(memory_space=pltpu.VMEM)
     shape = keep.shape[:1] + keep.shape[2:]
-    return pl.pallas_call(
+    return launch(
         add_split_kernel,
         in_specs=[pl.BlockSpec(memory_space=pltpu.SMEM), vmem, vmem],
         out_shape=[jax.ShapeDtypeStruct(shape, F32), jax.ShapeDtypeStruct(shape, send_type)],
         compiler_params=params(),
-        cost_estimate=cost(1),
+        cost_estimate=cost(1.0),
         name="add_split",
     )(bit, keep, got)
 
@@ -446,26 +496,27 @@
 
 def last_grads_call(scale, keep, got, rows_in):
     span, width = keep.shape
-    return pl.pallas_call(
+    return launch(
         lambda *refs: last_grads_kernel(scale, *refs),
         out_shape=[
             jax.ShapeDtypeStruct((rows_in, width), F32),
             jax.ShapeDtypeStruct((span - rows_in, width), F32),
         ],
         compiler_params=params(),
-        cost_estimate=cost(0.5),
+        cost_estimate=cost(1.5),
         name="last_grads",
     )(keep, got)
 
 
-def node_kernel(
-    place_ref, ids_ref, lat_ref, cot_ref, agg_ref, psum_ref, weight_ref, *refs
-):
-    pieces, (new_ref, part_ref, total) = refs[:-3], refs[-3:]
+def node_kernel(place_ref, ids_ref, lat_ref, cot_ref, agg_ref, back_ref, *refs):
+    pieces, (new_ref, grad_ref, total) = refs[:-3], refs[-3:]
     latent = lat_ref.shape[1]
     for j, piece in enumerate(pieces):
-        size = piece.shape[0]
-        total[pl.ds(pl.multiple_of(place_ref[j] * size, size), size), :] = piece[...]
+        size = piece.shape[0] // 3
+        here = pl.ds(pl.multiple_of(place_ref[j] * size, size), size)
+        total[here, :latent] = piece[:size]
+        total[here, latent : 2 * latent] = piece[size : 2 * size]
+        total[here, 2 * latent :] = 64.0 * piece[2 * size :, :128] + piece[2 * size :, 128:256]
     sums = total[...]
     means = sums[:, : 2 * latent] / jnp.maximum(sums[:, 2 * latent : 2 * latent + 1], 1.0)
     places = lax.broadcasted_iota(jnp.int32, (sums.shape[0], ids_ref.shape[1]), 0)
@@ -475,41 +526,42 @@
     pooled = lax.dot_general(hot, high, ROWS, preferred_element_type=F32)
     pooled = pooled + lax.dot_general(hot, low, ROWS, preferred_element_type=F32)
     new_ref[...] = (lat_ref[...].astype(F32) + agg_ref[...] + pooled[:, :latent]).astype(BF16)
-    own = lax.dot_general(psum_ref[...], weight_ref[2 * latent :], COLS, preferred_element_type=F32)
-    part_ref[...] = cot_ref[...].astype(F32) + own + pooled[:, latent:]
-
-
-def node_call(place, ids, lat, cot, agg, psum, weight_in, pieces):
+    grad_ref[...] = (cot_ref[...].astype(F32) + back_ref[...] + pooled[:, latent:]).astype(BF16)
+
+
+def node_call(place, ids, lat, cot, agg, back, pieces):
     vmem = pl.BlockSpec(memory_space=pltpu.VMEM)
-    coarse = sum(piece.shape[0] for piece in pieces)
-    return pl.pallas_call(
+    coarse = sum(piece.shape[0] // 3 for piece in pieces)
+    width = 2 * lat.shape[1] + 128
+    return launch(
         node_kernel,
-        in_specs=[pl.BlockSpec(memory_space=pltpu.SMEM)] + [vmem] * (6 + len(pieces)),
-        scratch_shapes=[pltpu.VMEM((coarse, pieces[0].shape[1]), F32)],
-        out_shape=[jax.ShapeDtypeStruct(lat.shape, BF16), jax.ShapeDtypeStruct(lat.shape, F32)],
-        compiler_params=params(),
-        cost_estimate=cost(1.1),
+        in_specs=[pl.BlockSpec(memory_space=pltpu.SMEM)] + [vmem] * (5 + len(pieces)),
+        scratch_shapes=[pltpu.VMEM((coarse, width), F32)],
+        out_shape=[jax.ShapeDtypeStruct(lat.shape, BF16)] * 2,
+        compiler_params=params(),
+        cost_estimate=cost(2.0),
         name="node_outputs",
-    )(place, ids, lat, cot, agg, psum, weight_in, *pieces)
-
-
-def grad_node_kernel(part_ref, own_ref, far_ref, near_ref, weight_ref, out_ref):
-    latent = part_ref.shape[1]
+    )(place, ids, lat, cot, streamed(agg), back, *pieces)
+
+
+def node_back_kernel(own_ref, far_ref, near_ref, psum_ref, weight_ref, out_ref):
+    latent = own_ref.shape[1]
     total = own_ref[...].astype(F32) + far_ref[...].astype(F32) + near_ref[...].astype(F32)
     back = lax.dot_general(
         total.astype(BF16), weight_ref[latent : 2 * latent], COLS, preferred_element_type=F32
     )
-    out_ref[...] = (part_ref[...] + back).astype(BF16)
-
-
-def grad_node_call(part, own, far, near, weight_in):
-    return pl.pallas_call(
-        grad_node_kernel,
-        out_shape=jax.ShapeDtypeStruct(part.shape, BF16),
-        compiler_params=params(),
-        cost_estimate=cost(8),
+    own = lax.dot_general(psum_ref[...], weight_ref[2 * latent :], COLS, preferred_element_type=F32)
+    out_ref[...] = back + own
+
+
+def node_back_call(own, far, near, psum, weight_in):
+    return launch(
+        node_back_kernel,
+        out_shape=jax.ShapeDtypeStruct(own.shape, F32),
+        compiler_params=params(),
+        cost_estimate=cost(15.0),
         name="grad_node",
-    )(part, own, far, near, weight_in)
+    )(own, far, near, psum, weight_in)
 
 
 def xor_swap(value, axis, distance):
@@ -556,6 +608,7 @@
     edge_cotangent,
     node_cotangent,
 ):
+    Order.token = None
     node_count, latent = node_lat.shape
     degree = edge_lat.shape[1]
     edge_count = node_count * degree
@@ -608,16 +661,17 @@
     else:
         coarse = coarse_reduce(coarse, coarse_other, patch)
         got = jnp.zeros_like(coarse)
-    base = base_call(flat_edges, node_lat, ids_col, weight_in, bias, coarse, pieces[:-1], block)
-    to_lower, to_upper, coarse = select_call(send_rel[:, None], coarse, got, base, pieces)
+    base = base_call(flat_edges, node_lat, ids_col, weight_in, bias, pieces[:-1], block)
+    to_lower, to_upper = select_call(send_rel[:, None], pieces)
     from_lower = lax.ppermute(to_upper, "patch", ring_up)
     from_upper = lax.ppermute(to_lower, "patch", ring_down)
-    got = xor_swap(coarse, "feat", 1) if whole_step else jnp.zeros_like(coarse)
-    base = gather_call(base, ids_col, pieces[-1:], weight_in, patch_total - node_count, block)
-
-    edge_new, aggregate, hidden_act, grad_proj, grad_pre, pre_sum, grad_edge, coarse = edge_call(
+    coarse = add_pair_call(coarse, got)
+    got = xor_swap(coarse, "feat", 2) if whole_step else jnp.zeros_like(coarse)
+
+    edge_new, aggregate, hidden_act, grad_proj, grad_pre, pre_sum, grad_edge = edge_call(
         base,
         ids_col,
+        pieces[-1],
         from_lower,
         from_upper,
         flat_edges,
@@ -626,55 +680,67 @@
         weight_in,
         weight_out,
         gain,
-        coarse,
-        got,
-        patch_total,
-        block,
-    )
+        patch_total - node_count,
+        block)
 
     rim_low, rim_high = rim_sum_call(ids_row, grad_pre, patch_total, 2 * rim_rows)
     back_upper = lax.ppermute(rim_low, "patch", ring_down)
     back_lower = lax.ppermute(rim_high, "patch", ring_up)
-    got = xor_swap(coarse, "feat", 2) if whole_step else jnp.zeros_like(coarse)
     patch_sum = patch_sum_call(ids_row, grad_pre, patch_total, node_count)
     edge_grad, out_grad = edge_grads_call(flat_edges, grad_pre, hidden_act, grad_proj)
-    coarse, *sums = add_rim_call(send_rel[None, :], back_lower, back_upper, patch_sum, coarse, got, node_count)
+    tables = pieces + [from_lower, from_upper]
+    keep, send = pack_call(
+        core_bit, pre_sum, edge_grad, out_grad, patch_sum, rim_low, rim_high, tables, feat_count, patch_count
+    )
+    got_core = xor_swap(send, "patch", 1)
+    sums = add_rim_call(
+        send_rel[None, :], back_lower, back_upper, patch_sum, coarse, got, node_count, whole_step
+    )
+    span, width = keep.shape[2:]
+    steps = [("patch", d) for d in bits_of(patch_count)[1:]] + [("feat", d) for d in bits_of(feat_count)]
+
+    def fold(step, keep, received):
+        axis, distance = steps[step]
+        index = patch if axis == "patch" else feat
+        bit = ((index // distance) % 2).astype(jnp.int32).reshape(1)
+        shape = (-1, 2, span, width)
+        keep, send = add_split_call(bit, keep.reshape(shape), received.reshape(shape), BF16)
+        return keep, xor_swap(send, axis, distance)
+
+    keep, received = fold(0, keep, got_core)
     if feat_count == 4:
         relay = xor_swap(sums[3], "feat", 1)
-        far_sum = (sums[2].astype(F32) + relay.astype(F32)).astype(BF16)
+        if whole_step:
+            far_sum, coarse_all = far_sum_call(sums[2], sums[3], relay)
+        else:
+            far_sum = add_pair_call(sums[2], relay)
         got_far = xor_swap(far_sum, "feat", 2)
         got_near = xor_swap(sums[1], "feat", 1)
         own = [sums[0], got_far, got_near]
     else:
         parts = sums
         for distance in reversed(bits_of(feat_count)):
-            got = [xor_swap(part, "feat", distance) for part in parts[distance:]]
-            parts = [(a.astype(F32) + b.astype(F32)).astype(BF16) for a, b in zip(parts[:distance], got)]
+            arrived = [xor_swap(part, "feat", distance) for part in parts[distance:]]
+            parts = [add_pair_call(a, b) for a, b in zip(parts[:distance], arrived)]
         own = [parts[0], jnp.zeros_like(parts[0]), jnp.zeros_like(parts[0])]
-
-    keep, send = pack_call(core_bit, pre_sum, edge_grad, out_grad, pieces, sums, feat_count, patch_count)
-    span, width = keep.shape[2:]
-    steps = [("patch", d) for d in bits_of(patch_count)[1:]] + [("feat", d) for d in bits_of(feat_count)]
-    got = xor_swap(send, "patch", 1)
-    for axis, distance in steps:
-        index = patch if axis == "patch" else feat
-        bit = ((index // distance) % 2).astype(jnp.int32).reshape(1)
-        shape = (-1, 2, span, width)
-        keep, send = add_split_call(bit, keep.reshape(shape), got.reshape(shape), BF16)
-        got = xor_swap(send, axis, distance)
+    keep, received = fold(1, keep, received)
+    back = node_back_call(*own, pre_sum, weight_in)
+    keep, received = fold(2, keep, received)
+    if whole_step:
+        parts = [coarse_all] + [xor_swap(coarse_all, "patch", j) for j in range(1, 4)]
+        place = jnp.stack([((patch ^ j) % 2) * 2 + (patch ^ j) // 2 for j in range(4)]).astype(jnp.int32)
+    else:
+        counts = jnp.pad(coarse[:, 2 * latent :], ((0, 0), (128, latent - 256)))
+        parts = [jnp.concatenate([coarse[:, :latent], coarse[:, latent : 2 * latent], counts], axis=0)]
+        place = jnp.zeros((1,), jnp.int32)
+    node_new, grad_node = node_call(
+        place, coarse_row, node_lat, node_cotangent, aggregate, back, parts
+    )
+    for step in range(3, len(steps)):
+        keep, received = fold(step, keep, received)
     scale = 1.0 / math.sqrt(edge_count * patch_count * feat_count)
     in_rows = 3 * latent // patch_count
-    grads_in, grads_out = last_grads_call(scale, keep.reshape(span, width), got.reshape(span, width), in_rows)
-
-    if whole_step:
-        parts = [coarse] + [xor_swap(coarse, "patch", j) for j in range(1, 4)]
-        place = jnp.stack([((patch ^ j) % 2) * 2 + (patch ^ j) // 2 for j in range(4)]).astype(jnp.int32)
-    else:
-        parts, place = [coarse], jnp.zeros((1,), jnp.int32)
-    node_new, part = node_call(
-        place, coarse_row, node_lat, node_cotangent, aggregate, pre_sum, weight_in, parts
-    )
-    grad_node = grad_node_call(part, *own, weight_in)
+    grads_in, grads_out = last_grads_call(scale, keep.reshape(span, width), received.reshape(span, width), in_rows)
     return (
         edge_new.reshape(edge_lat.shape),
         node_new,

time: 110 us -> 95.1 us (0.86)
  waiting for transfers between devices: 33.7 us -> 26.4 us
  local copies, waits for them, and re-layouts: 13.6 us -> 7.44 us
  starting transfers between devices: 23.2 us -> 27.1 us
  Pallas kernels: 35.3 us -> 32.6 us
  other arithmetic: 2.53 us -> 0.11 us
    unnamed x60 -> x38, local copies, waits for them, and re-layouts: 13 us -> 6.75 us
    ppermute x17 -> x16, waiting for transfers between devices: 31.8 us -> 26.4 us  [xor_swap(): return lax.ppermute(value, axis, [(i, i ^ distance) for i in range(size)])]
    ppermute x17 -> x16, starting transfers between devices: 19.6 us -> 23.6 us  [xor_swap(): return lax.ppermute(value, axis, [(i, i ^ distance) for i in range(size)])]
    pallas_call x17 -> x18, Pallas kernels: 35.3 us -> 32.6 us  [call(): pl.pallas_call(body, out_shape=outs + [mark], in_specs=specs, out_specs=p...]
    convert_element_type x1 -> x0, other arithmetic: 1.72 us -> none  [shards(): far_sum = (sums[2].astype(F32) + relay.astype(F32)).astype(BF16)]
  transfers between devices with their start and end apart: 21 -> 20, of which waited for: 11 -> 10; matrix products, arithmetic and copies ran while one was open for 3% -> 1% of each run, Pallas kernels for 11% -> 34%
where the time goes in v3:
time: 95.1 us; the launch traced here: 94.7 us
  Pallas kernels  32.6 us (34%)
  starting transfers between devices  27.1 us (28%)
  waiting for transfers between devices  26.4 us (28%)
  local copies, waits for them, and re-layouts  7.44 us (8%)
  between operations  0.99 us (1%)
    pallas_call x18, Pallas kernels, call(): pl.pallas_call(body, out_shape=outs + [mark], in_specs=specs, out_specs=p...  32.6 us
    ppermute x16, waiting for transfers between devices, xor_swap(): return lax.ppermute(value, axis, [(i, i ^ distance) for i in range(size)])  26.4 us
    ppermute x16, starting transfers between devices, xor_swap(): return lax.ppermute(value, axis, [(i, i ^ distance) for i in range(size)])  23.6 us
    unnamed x38, local copies, waits for them, and re-layouts  6.75 us
  transfers between devices with their start and end apart: 20, of which 10 were waited for; matrix products, arithmetic and copies ran while one was open for 1% of the time, Pallas kernels for 34%

profile of v3, /device:TPU:0, one launch (start us, length us, event | category | flops | bytes accessed | tf_op | source)
XLA Modules:
  0.0 94.7 jit_solution(5040464779757302540)
XLA Ops:
  0.6 4.1 %collective-permute-start.1 = (bf16[256,512]{1,0:T(8,128)(2,1)}, bf16[256,512]{1,0:T(8,128)(2,1)S(1)}, u32[]{:S(2)}, u32[]{:S(2)}) collective-permute-start(bf16[256,512]{1,0:T(8,128)(2,1)} %refs_2_.3), channel_id=1, source_target_pairs={{0,2},{1,3},{2,0},{3,1},{4,6},{5,7},{6,4},{7,5},{8,10},{9,11},{10,... | collective-permute-start | bytes 786440 | tf_op jit(solution)/shard_map/ppermute | solution.py:569
  4.7 1.6 %collective-permute-start = (bf16[256,512]{1,0:T(8,128)(2,1)}, bf16[256,512]{1,0:T(8,128)(2,1)S(1)}, u32[]{:S(2)}, u32[]{:S(2)}) collective-permute-start(bf16[256,512]{1,0:T(8,128)(2,1)} %refs_2_.3), channel_id=1, source_target_pairs={{0,1},{1,0},{2,3},{3,2},{4,5},{5,4},{6,7},{7,6},{8,9},{9,8},{10,11... | collective-permute-start | bytes 786440 | tf_op jit(solution)/shard_map/ppermute | solution.py:569
  10.6 1.6 %collective-permute-start.6 = (f32[16,1152]{1,0:T(8,128)S(1)}, f32[16,1152]{1,0:T(8,128)S(1)}, u32[]{:S(2)}, u32[]{:S(2)}) collective-permute-start(f32[16,1152]{1,0:T(8,128)S(1)} %bitcast.39), channel_id=1, source_target_pairs={{0,8},{4,12},{8,0},{12,4},{1,9},{5,13},{9,1},{13,5},{2,10},{6,14},... | collective-permute-start | bytes 221192 | tf_op jit(solution)/shard_map/ppermute | solution.py:569
  12.2 4.7 %collective-permute-done.1.refs_7_.refs_3_.refs_9_ = bf16[256,512]{1,0:T(8,128)(2,1)S(1)} collective-permute-done((bf16[256,512]{1,0:T(8,128)(2,1)}, bf16[256,512]{1,0:T(8,128)(2,1)S(1)}, u32[]{:S(2)}, u32[]{:S(2)}) %collective-permute-start.1) | collective-permute-done | bytes 262176 | tf_op jit(solution)/shard_map/ppermute | solution.py:569
  17.7 5.9 %base_terms.1 = (f32[2048,512]{1,0:T(8,128)S(1)}, f32[8,128]{1,0:T(8,128)S(1)}) custom-call(bf16[2048,512]{1,0:T(8,128)(2,1)} %bitcast.30, bf16[256,512]{1,0:T(8,128)(2,1)S(1)} %copy-done.2, s32[2048,1]{1,0:T(8,128)S(1)} %broadcast_in_dim_reshape.8.refs_2_.refs_1_, bf16[1536,512]{1,0:T(8,128)(2,1)S(1)} %copy-done.3, f32[1,512]{1,0:T(1,128)S(1)} %bitcast.40, ...), custom_call_target="tpu_custom_call" | custom-call | flops 17250000896 | bytes 1048576 | tf_op jit(solution)/shard_map/base_terms/pallas_call | solution.py:55
  25.6 1.7 %collective-permute-start.5 = (bf16[128,512]{1,0:T(8,128)(2,1)S(1)}, bf16[128,512]{1,0:T(8,128)(2,1)S(1)}, u32[]{:S(2)}, u32[]{:S(2)}) collective-permute-start(bf16[128,512]{1,0:T(8,128)(2,1)S(1)} %get-tuple-element.69), channel_id=1, source_target_pairs={{4,0},{8,4},{12,8},{0,12},{5,1},{9,5},{13,9},{1,13},{6,2},{10,6},{... | collective-permute-start | bytes 393224 | tf_op jit(solution)/shard_map/ppermute | solution.py:667
  27.6 3.3 %collective-permute-start.9 = (f32[16,1152]{1,0:T(8,128)S(1)}, f32[16,1152]{1,0:T(8,128)S(1)}, u32[]{:S(2)}, u32[]{:S(2)}) collective-permute-start(f32[16,1152]{1,0:T(8,128)S(1)} %get-tuple-element.82.refs_4_), channel_id=1, source_target_pairs={{0,2},{1,3},{2,0},{3,1},{4,6},{5,7},{6,4},{7,5},{8,10},{9,11},{10,... | collective-permute-start | bytes 221192 | tf_op jit(solution)/shard_map/ppermute | solution.py:569
  30.9 14.0 %edge_block.1 = (bf16[2048,512]{1,0:T(8,128)(2,1)}, f32[256,512]{1,0:T(8,128)S(1)}, bf16[2048,512]{1,0:T(8,128)(2,1)S(1)}, bf16[2048,512]{1,0:T(8,128)(2,1)S(1)}...) custom-call(f32[2048,512]{1,0:T(8,128)} %copy-done.16, ...), custom_call_target="tpu_custom_call" | custom-call | flops 41400000512 | bytes 1048576 | tf_op jit(solution)/shard_map/edge_block/pallas_call | solution.py:55
  48.2 2.8 %patch_sums.1 = (f32[1024,512]{1,0:T(8,128)S(1)}, f32[8,128]{1,0:T(8,128)S(1)}) custom-call(s32[1,2048]{1,0:T(1,128)S(1)} %broadcast_in_dim_reshape.7.refs_0_, bf16[2048,512]{1,0:T(8,128)(2,1)S(1)} %get-tuple-element.76.refs_1_, f32[8,128]{1,0:T(8,128)S(1)} %get-tuple-element.80.refs_2_), custom_call_target="tpu_custom_call" | custom-call | flops 575000000 | bytes 1048576 | tf_op jit(solution)/shard_map/patch_sums/pallas_call | solution.py:55
  51.1 2.4 %edge_grads.1 = (f32[512,512]{1,0:T(8,128)S(1)}, f32[512,512]{1,0:T(8,128)S(1)}, f32[8,128]{1,0:T(8,128)S(1)}) custom-call(bf16[2048,512]{1,0:T(8,128)(2,1)S(1)} %bitcast.32, bf16[2048,512]{1,0:T(8,128)(2,1)S(1)} %get-tuple-element.76.refs_1_, bf16[2048,512]{1,0:T(8,128)(2,1)S(1)} %get-tuple-element.84.refs_2_, ...), custom_call_target="tpu_custom_call" | custom-call | flops 575000000 | bytes 1048576 | tf_op jit(solution)/shard_map/edge_grads/pallas_call | solution.py:55
  53.4 1.4 %pack_grads.1 = (f32[4,2,512,128]{3,2,1,0:T(8,128)S(1)}, bf16[4,2,512,128]{3,2,1,0:T(8,128)(2,1)S(1)}, f32[8,128]{1,0:T(8,128)S(1)}) custom-call(s32[1]{0:T(128)} %bitcast.5.refs_3_.refs_0_, bf16[256,512]{1,0:T(8,128)(2,1)S(1)} %get-tuple-element.83.refs_1_.refs_3_, f32[512,512]{1,0:T(8,128)S(1)} %get-tuple-element.87.refs_2_, ...), custom_call_target="tpu_custom_call" | custom-call | flops 575000000 | bytes 1048576 | tf_op jit(solution)/shard_map/pack_grads/pallas_call | solution.py:55
  55.7 1.3 %collective-permute-start.10 = (bf16[304,512]{1,0:T(8,128)(2,1)S(1)}, bf16[304,512]{1,0:T(8,128)(2,1)S(1)}, u32[]{:S(2)}, u32[]{:S(2)}) collective-permute-start(bf16[304,512]{1,0:T(8,128)(2,1)S(1)} %get-tuple-element.93.refs_1_), channel_id=1, source_target_pairs={{0,1},{1,0},{2,3},{3,2},{4,5},{5,4},{6,7},{7,6},{8,9},{9,8},{10,11... | collective-permute-start | bytes 933896 | tf_op jit(solution)/shard_map/ppermute | solution.py:569
  58.8 1.5 %collective-permute-start.14 = (bf16[4,512,128]{2,1,0:T(8,128)(2,1)S(1)}, bf16[4,512,128]{2,1,0:T(8,128)(2,1)S(1)}, u32[]{:S(2)}, u32[]{:S(2)}) collective-permute-start(bf16[4,512,128]{2,1,0:T(8,128)(2,1)S(1)} %get-tuple-element.101), channel_id=1, source_target_pairs={{0,8},{4,12},{8,0},{12,4},{1,9},{5,13},{9,1},{13,5},{2,10},{6,14},... | collective-permute-start | bytes 1572872 | tf_op jit(solution)/shard_map/ppermute | solution.py:569
  60.3 1.1 %collective-permute-start.13 = (bf16[256,512]{1,0:T(8,128)(2,1)S(1)}, bf16[256,512]{1,0:T(8,128)(2,1)S(1)}, u32[]{:S(2)}, u32[]{:S(2)}) collective-permute-start(bf16[256,512]{1,0:T(8,128)(2,1)S(1)} %get-tuple-element.99), channel_id=1, source_target_pairs={{0,1},{1,0},{2,3},{3,2},{4,5},{5,4},{6,7},{7,6},{8,9},{9,8},{10,11... | collective-permute-start | bytes 786440 | tf_op jit(solution)/shard_map/ppermute | solution.py:569
  61.5 4.4 %collective-permute-done.10.refs_2_ = bf16[304,512]{1,0:T(8,128)(2,1)S(1)} collective-permute-done((bf16[304,512]{1,0:T(8,128)(2,1)S(1)}, bf16[304,512]{1,0:T(8,128)(2,1)S(1)}, u32[]{:S(2)}, u32[]{:S(2)}) %collective-permute-start.10) | collective-permute-done | bytes 311328 | tf_op jit(solution)/shard_map/ppermute | solution.py:569
  66.0 3.3 %collective-permute-start.12 = (bf16[256,512]{1,0:T(8,128)(2,1)S(1)}, bf16[256,512]{1,0:T(8,128)(2,1)S(1)}, u32[]{:S(2)}, u32[]{:S(2)}) collective-permute-start(bf16[256,512]{1,0:T(8,128)(2,1)S(1)} %get-tuple-element.98), channel_id=1, source_target_pairs={{0,2},{1,3},{2,0},{3,1},{4,6},{5,7},{6,4},{7,5},{8,10},{9,11},{10,... | collective-permute-start | bytes 786440 | tf_op jit(solution)/shard_map/ppermute | solution.py:569
  69.3 1.4 %collective-permute-start.16 = (f32[48,512]{1,0:T(8,128)S(1)}, f32[48,512]{1,0:T(8,128)S(1)}, u32[]{:S(2)}, u32[]{:S(2)}) collective-permute-start(f32[48,512]{1,0:T(8,128)S(1)} %get-tuple-element.105.refs_6_), channel_id=1, source_target_pairs={{0,8},{4,12},{8,0},{12,4},{1,9},{5,13},{9,1},{13,5},{2,10},{6,14},... | collective-permute-start | bytes 294920 | tf_op jit(solution)/shard_map/ppermute | solution.py:569
  70.7 2.5 %collective-permute-done.14 = bf16[4,512,128]{2,1,0:T(8,128)(2,1)S(1)} collective-permute-done((bf16[4,512,128]{2,1,0:T(8,128)(2,1)S(1)}, bf16[4,512,128]{2,1,0:T(8,128)(2,1)S(1)}, u32[]{:S(2)}, u32[]{:S(2)}) %collective-permute-start.14) | collective-permute-done | bytes 524320 | tf_op jit(solution)/shard_map/ppermute | solution.py:569
  73.2 1.2 %copy-done.14 = f32[4,512,128]{2,1,0:T(8,128)S(1)} copy-done((f32[4,512,128]{2,1,0:T(8,128)S(1)}, f32[4,512,128]{2,1,0:T(8,128)}, u32[]{:S(2)}) %copy-start.14) | copy-done | bytes 1048600
  76.3 4.5 %collective-permute-done.12.refs_1_ = bf16[256,512]{1,0:T(8,128)(2,1)S(1)} collective-permute-done((bf16[256,512]{1,0:T(8,128)(2,1)S(1)}, bf16[256,512]{1,0:T(8,128)(2,1)S(1)}, u32[]{:S(2)}, u32[]{:S(2)}) %collective-permute-start.12) | collective-permute-done | bytes 262176 | tf_op jit(solution)/shard_map/ppermute | solution.py:569
  81.2 3.4 %collective-permute-done.18 = bf16[2,512,128]{2,1,0:T(8,128)(2,1)S(1)} collective-permute-done((bf16[2,512,128]{2,1,0:T(8,128)(2,1)S(1)}, bf16[2,512,128]{2,1,0:T(8,128)(2,1)S(1)}, u32[]{:S(2)}, u32[]{:S(2)}) %collective-permute-start.18) | collective-permute-done | bytes 262176 | tf_op jit(solution)/shard_map/ppermute | solution.py:569
  84.7 2.8 %collective-permute-start.19 = (bf16[1,512,128]{2,1,0:T(8,128)(2,1)S(1)}, bf16[1,512,128]{2,1,0:T(8,128)(2,1)S(1)}, u32[]{:S(2)}, u32[]{:S(2)}) collective-permute-start(bf16[1,512,128]{2,1,0:T(8,128)(2,1)S(1)} %get-tuple-element.114), channel_id=1, source_target_pairs={{0,2},{1,3},{2,0},{3,1},{4,6},{5,7},{6,4},{7,5},{8,10},{9,11},{10,... | collective-permute-start | bytes 393224 | tf_op jit(solution)/shard_map/ppermute | solution.py:569
  87.5 2.3 %node_outputs.1 = (bf16[256,512]{1,0:T(8,128)(2,1)}, bf16[256,512]{1,0:T(8,128)(2,1)}, f32[8,128]{1,0:T(8,128)S(1)}) custom-call(s32[4]{0:T(128)S(1)} %pad_add_fusion.refs_0_, s32[1,256]{1,0:T(1,128)S(1)} %bitcast.43, bf16[256,512]{1,0:T(8,128)(2,1)S(1)} %copy-done.2, bf16[256,512]{1,0:T(8,128)(2,1)S(1)} %copy-done.8, f32[256,512]{1,0:T(8,128)} %copy-done.15, ...), custom_call_target="tpu_custom_call" | custom-call | flops 2300000000 | bytes 1048576 | tf_op jit(solution)/shard_map/node_outputs/pallas_call | solution.py:55
  89.8 4.2 %collective-permute-done.19 = bf16[1,512,128]{2,1,0:T(8,128)(2,1)S(1)} collective-permute-done((bf16[1,512,128]{2,1,0:T(8,128)(2,1)S(1)}, bf16[1,512,128]{2,1,0:T(8,128)(2,1)S(1)}, u32[]{:S(2)}, u32[]{:S(2)}) %collective-permute-start.19) | collective-permute-done | bytes 131104 | tf_op jit(solution)/shard_map/ppermute | solution.py:569
  (79 shorter events, 16.2 us)
Async XLA Ops:
  0.6 16.3 %collective-permute-start.1 = (bf16[256,512]{1,0:T(8,128)(2,1)}, bf16[256,512]{1,0:T(8,128)(2,1)S(1)}, u32[]{:S(2)}, u32[]{:S(2)}) collective-permute-start(bf16[256,512]{1,0:T(8,128)(2,1)} %refs_2_.3), channel_id=1, source_target_pairs={{0,2},{1,3},{2,0},{3,1},{4,6},{5,7},{6,4},{7,5},{8,10},{9,11},{10,... | collective-permute-start | bytes 786440 | tf_op jit(solution)/shard_map/ppermute | solution.py:569
  4.7 13.0 %collective-permute-start = (bf16[256,512]{1,0:T(8,128)(2,1)}, bf16[256,512]{1,0:T(8,128)(2,1)S(1)}, u32[]{:S(2)}, u32[]{:S(2)}) collective-permute-start(bf16[256,512]{1,0:T(8,128)(2,1)} %refs_2_.3), channel_id=1, source_target_pairs={{0,1},{1,0},{2,3},{3,2},{4,5},{5,4},{6,7},{7,6},{8,9},{9,8},{10,11... | collective-permute-start | bytes 786440 | tf_op jit(solution)/shard_map/ppermute | solution.py:569
  9.2 1.4 %collective-permute-start.2 = (f32[32,1152]{1,0:T(8,128)S(1)}, f32[32,1152]{1,0:T(8,128)S(1)}, u32[]{:S(2)}, u32[]{:S(2)}) collective-permute-start(f32[32,1152]{1,0:T(8,128)S(1)} %get-tuple-element.63), channel_id=1, source_target_pairs={{0,4},{4,0},{8,12},{12,8},{1,5},{5,1},{9,13},{13,9},{2,6},{6,2},{1... | collective-permute-start | bytes 442376 | tf_op jit(solution)/shard_map/ppermute | solution.py:569
  10.6 7.1 %copy-start.2 = (bf16[256,512]{1,0:T(8,128)(2,1)S(1)}, bf16[256,512]{1,0:T(8,128)(2,1)}, u32[]{:S(2)}) copy-start(bf16[256,512]{1,0:T(8,128)(2,1)} %refs_2_.3) | copy-start | bytes 786436
  10.6 7.1 %copy-start.3 = (bf16[1536,512]{1,0:T(8,128)(2,1)S(1)}, bf16[1536,512]{1,0:T(8,128)(2,1)}, u32[]{:S(2)}) copy-start(bf16[1536,512]{1,0:T(8,128)(2,1)} %refs_4_.1) | copy-start | bytes 4718596
  10.6 7.1 %copy-start.9 = (f32[512]{0:T(512)S(1)}, f32[512]{0:T(512)}, u32[]{:S(2)}) copy-start(f32[512]{0:T(512)} %param.17) | copy-start | bytes 6148
  10.6 16.8 %collective-permute-start.6 = (f32[16,1152]{1,0:T(8,128)S(1)}, f32[16,1152]{1,0:T(8,128)S(1)}, u32[]{:S(2)}, u32[]{:S(2)}) collective-permute-start(f32[16,1152]{1,0:T(8,128)S(1)} %bitcast.39), channel_id=1, source_target_pairs={{0,8},{4,12},{8,0},{12,4},{1,9},{5,13},{9,1},{13,5},{2,10},{6,14},... | collective-permute-start | bytes 221192 | tf_op jit(solution)/shard_map/ppermute | solution.py:569
  17.0 7.4 %collective-permute-start.3 = (bf16[256,512]{1,0:T(8,128)(2,1)S(1)}, bf16[256,512]{1,0:T(8,128)(2,1)S(1)}, u32[]{:S(2)}, u32[]{:S(2)}) collective-permute-start(bf16[256,512]{1,0:T(8,128)(2,1)S(1)} %collective-permute-done.1.refs_7_.refs_3_.refs_9_), channel_id=1, source_target_pairs={{0,1},{1,0},{2,3},{3,2},{4,5},{5,4},{6,7},{7,6},{8,9},{9,8},{10,11... | collective-permute-start | bytes 786440 | tf_op jit(solution)/shard_map/ppermute | solution.py:569
  25.6 5.3 %collective-permute-start.4 = (bf16[128,512]{1,0:T(8,128)(2,1)S(1)}, bf16[128,512]{1,0:T(8,128)(2,1)S(1)}, u32[]{:S(2)}, u32[]{:S(2)}) collective-permute-start(bf16[128,512]{1,0:T(8,128)(2,1)S(1)} %get-tuple-element.68), channel_id=1, source_target_pairs={{0,4},{4,8},{8,12},{12,0},{1,5},{5,9},{9,13},{13,1},{2,6},{6,10},{... | collective-permute-start | bytes 393224 | tf_op jit(solution)/shard_map/ppermute | solution.py:666
  25.6 5.3 %collective-permute-start.5 = (bf16[128,512]{1,0:T(8,128)(2,1)S(1)}, bf16[128,512]{1,0:T(8,128)(2,1)S(1)}, u32[]{:S(2)}, u32[]{:S(2)}) collective-permute-start(bf16[128,512]{1,0:T(8,128)(2,1)S(1)} %get-tuple-element.69), channel_id=1, source_target_pairs={{4,0},{8,4},{12,8},{0,12},{5,1},{9,5},{13,9},{1,13},{6,2},{10,6},{... | collective-permute-start | bytes 393224 | tf_op jit(solution)/shard_map/ppermute | solution.py:667
  27.6 27.4 %collective-permute-start.9 = (f32[16,1152]{1,0:T(8,128)S(1)}, f32[16,1152]{1,0:T(8,128)S(1)}, u32[]{:S(2)}, u32[]{:S(2)}) collective-permute-start(f32[16,1152]{1,0:T(8,128)S(1)} %get-tuple-element.82.refs_4_), channel_id=1, source_target_pairs={{0,2},{1,3},{2,0},{3,1},{4,6},{5,7},{6,4},{7,5},{8,10},{9,11},{10,... | collective-permute-start | bytes 221192 | tf_op jit(solution)/shard_map/ppermute | solution.py:569
  46.4 8.5 %collective-permute-start.7 = (bf16[128,512]{1,0:T(8,128)(2,1)S(1)}, bf16[128,512]{1,0:T(8,128)(2,1)S(1)}, u32[]{:S(2)}, u32[]{:S(2)}) collective-permute-start(bf16[128,512]{1,0:T(8,128)(2,1)S(1)} %get-tuple-element.78.refs_6_), channel_id=1, source_target_pairs={{0,4},{4,8},{8,12},{12,0},{1,5},{5,9},{9,13},{13,1},{2,6},{6,10},{... | collective-permute-start | bytes 393224 | tf_op jit(solution)/shard_map/ppermute | solution.py:688
  47.2 7.8 %collective-permute-start.8 = (bf16[128,512]{1,0:T(8,128)(2,1)S(1)}, bf16[128,512]{1,0:T(8,128)(2,1)S(1)}, u32[]{:S(2)}, u32[]{:S(2)}) collective-permute-start(bf16[128,512]{1,0:T(8,128)(2,1)S(1)} %get-tuple-element.79.refs_5_), channel_id=1, source_target_pairs={{4,0},{8,4},{12,8},{0,12},{5,1},{9,5},{13,9},{1,13},{6,2},{10,6},{... | collective-permute-start | bytes 393224 | tf_op jit(solution)/shard_map/ppermute | solution.py:687
  54.9 2.7 %collective-permute-start.11 = (bf16[4,2,512,128]{3,2,1,0:T(8,128)(2,1)S(1)}, bf16[4,2,512,128]{3,2,1,0:T(8,128)(2,1)S(1)}, u32[]{:S(2)}, u32[]{:S(2)}) collective-permute-start(bf16[4,2,512,128]{3,2,1,0:T(8,128)(2,1)S(1)} %get-tuple-element.95), channel_id=1, source_target_pairs={{0,4},{4,0},{8,12},{12,8},{1,5},{5,1},{9,13},{13,9},{2,6},{6,2},{1... | collective-permute-start | bytes 3145736 | tf_op jit(solution)/shard_map/ppermute | solution.py:569
  55.7 10.2 %collective-permute-start.10 = (bf16[304,512]{1,0:T(8,128)(2,1)S(1)}, bf16[304,512]{1,0:T(8,128)(2,1)S(1)}, u32[]{:S(2)}, u32[]{:S(2)}) collective-permute-start(bf16[304,512]{1,0:T(8,128)(2,1)S(1)} %get-tuple-element.93.refs_1_), channel_id=1, source_target_pairs={{0,1},{1,0},{2,3},{3,2},{4,5},{5,4},{6,7},{7,6},{8,9},{9,8},{10,11... | collective-permute-start | bytes 933896 | tf_op jit(solution)/shard_map/ppermute | solution.py:569
  58.8 14.4 %collective-permute-start.14 = (bf16[4,512,128]{2,1,0:T(8,128)(2,1)S(1)}, bf16[4,512,128]{2,1,0:T(8,128)(2,1)S(1)}, u32[]{:S(2)}, u32[]{:S(2)}) collective-permute-start(bf16[4,512,128]{2,1,0:T(8,128)(2,1)S(1)} %get-tuple-element.101), channel_id=1, source_target_pairs={{0,8},{4,12},{8,0},{12,4},{1,9},{5,13},{9,1},{13,5},{2,10},{6,14},... | collective-permute-start | bytes 1572872 | tf_op jit(solution)/shard_map/ppermute | solution.py:569
  60.3 15.2 %collective-permute-start.13 = (bf16[256,512]{1,0:T(8,128)(2,1)S(1)}, bf16[256,512]{1,0:T(8,128)(2,1)S(1)}, u32[]{:S(2)}, u32[]{:S(2)}) collective-permute-start(bf16[256,512]{1,0:T(8,128)(2,1)S(1)} %get-tuple-element.99), channel_id=1, source_target_pairs={{0,1},{1,0},{2,3},{3,2},{4,5},{5,4},{6,7},{7,6},{8,9},{9,8},{10,11... | collective-permute-start | bytes 786440 | tf_op jit(solution)/shard_map/ppermute | solution.py:569
  66.0 14.8 %collective-permute-start.12 = (bf16[256,512]{1,0:T(8,128)(2,1)S(1)}, bf16[256,512]{1,0:T(8,128)(2,1)S(1)}, u32[]{:S(2)}, u32[]{:S(2)}) collective-permute-start(bf16[256,512]{1,0:T(8,128)(2,1)S(1)} %get-tuple-element.98), channel_id=1, source_target_pairs={{0,2},{1,3},{2,0},{3,1},{4,6},{5,7},{6,4},{7,5},{8,10},{9,11},{10,... | collective-permute-start | bytes 786440 | tf_op jit(solution)/shard_map/ppermute | solution.py:569
  69.3 18.1 %collective-permute-start.17 = (f32[48,512]{1,0:T(8,128)S(1)}, f32[48,512]{1,0:T(8,128)S(1)}, u32[]{:S(2)}, u32[]{:S(2)}) collective-permute-start(f32[48,512]{1,0:T(8,128)S(1)} %get-tuple-element.105.refs_6_), channel_id=1, source_target_pairs={{0,12},{4,8},{8,4},{12,0},{1,13},{5,9},{9,5},{13,1},{2,14},{6,10},... | collective-permute-start | bytes 294920 | tf_op jit(solution)/shard_map/ppermute | solution.py:569
  69.3 18.1 %collective-permute-start.16 = (f32[48,512]{1,0:T(8,128)S(1)}, f32[48,512]{1,0:T(8,128)S(1)}, u32[]{:S(2)}, u32[]{:S(2)}) collective-permute-start(f32[48,512]{1,0:T(8,128)S(1)} %get-tuple-element.105.refs_6_), channel_id=1, source_target_pairs={{0,8},{4,12},{8,0},{12,4},{1,9},{5,13},{9,1},{13,5},{2,10},{6,14},... | collective-permute-start | bytes 294920 | tf_op jit(solution)/shard_map/ppermute | solution.py:569
  73.2 14.2 %collective-permute-start.15 = (f32[48,512]{1,0:T(8,128)S(1)}, f32[48,512]{1,0:T(8,128)S(1)}, u32[]{:S(2)}, u32[]{:S(2)}) collective-permute-start(f32[48,512]{1,0:T(8,128)S(1)} %get-tuple-element.105.refs_6_), channel_id=1, source_target_pairs={{0,4},{4,0},{8,12},{12,8},{1,5},{5,1},{9,13},{13,9},{2,6},{6,2},{1... | collective-permute-start | bytes 294920 | tf_op jit(solution)/shard_map/ppermute | solution.py:569
  74.4 6.3 %copy-start.5 = (bf16[1536,512]{1,0:T(8,128)(2,1)S(1)}, bf16[1536,512]{1,0:T(8,128)(2,1)}, u32[]{:S(2)}) copy-start(bf16[1536,512]{1,0:T(8,128)(2,1)} %refs_4_.1) | copy-start | bytes 4718596
  75.5 9.1 %collective-permute-start.18 = (bf16[2,512,128]{2,1,0:T(8,128)(2,1)S(1)}, bf16[2,512,128]{2,1,0:T(8,128)(2,1)S(1)}, u32[]{:S(2)}, u32[]{:S(2)}) collective-permute-start(bf16[2,512,128]{2,1,0:T(8,128)(2,1)S(1)} %get-tuple-element.107), channel_id=1, source_target_pairs={{0,1},{1,0},{2,3},{3,2},{4,5},{5,4},{6,7},{7,6},{8,9},{9,8},{10,11... | collective-permute-start | bytes 786440 | tf_op jit(solution)/shard_map/ppermute | solution.py:569
  84.7 9.3 %collective-permute-start.19 = (bf16[1,512,128]{2,1,0:T(8,128)(2,1)S(1)}, bf16[1,512,128]{2,1,0:T(8,128)(2,1)S(1)}, u32[]{:S(2)}, u32[]{:S(2)}) collective-permute-start(bf16[1,512,128]{2,1,0:T(8,128)(2,1)S(1)} %get-tuple-element.114), channel_id=1, source_target_pairs={{0,2},{1,3},{2,0},{3,1},{4,6},{5,7},{6,4},{7,5},{8,10},{9,11},{10,... | collective-permute-start | bytes 393224 | tf_op jit(solution)/shard_map/ppermute | solution.py:569
  (15 other events, 30.3 us)

commit v4 on v3

--- a/solution.py
+++ b/solution.py
@@ -1,3 +1,4 @@
+import functools
 import math
 
 import jax
@@ -12,6 +13,7 @@
 F32 = jnp.float32
 BF16 = jnp.bfloat16
 VMEM_LIMIT = 24 * 1024 * 1024
+EDGE_LIMIT = 24 * 1024 * 1024
 COLS = (((1,), (1,)), ((), ()))
 ROWS = (((0,), (0,)), ((), ()))
 
@@ -20,11 +22,34 @@
     return jnp.dot(a, b, preferred_element_type=F32)
 
 
-def params():
-    return pltpu.CompilerParams(vmem_limit_bytes=VMEM_LIMIT)
-
-
-def cost(micros):
+def params(limit=None):
+    return pltpu.CompilerParams(vmem_limit_bytes=limit or VMEM_LIMIT)
+
+
+COST = {
+    "base_terms": 15,
+    "select_rows": 2,
+    "add_pair": 1,
+    "edge_block": 36,
+    "rim_sums": 2.4,
+    "patch_sums": 0.3,
+    "edge_grads": 0.3,
+    "add_rim_sums": 0.3,
+    "pack_grads": 0.3,
+    "far_sum": 30,
+    "node_outputs": 2,
+    "grad_node": 30,
+    "last_grads": 1.5,
+    "coarse_sums": 1,
+    "coarse_split": 1,
+    "fold0": 0.3,
+    "fold1": 0.3,
+    "fold2": 0.3,
+}
+
+
+def cost(name):
+    micros = COST[name]
     return pl.CostEstimate(flops=int(micros * 1.15e9), bytes_accessed=1 << 20, transcendentals=0)
 
 
@@ -110,13 +135,13 @@
     out_ref[...] = total.reshape(edges, hidden)
 
 
-def base_call(edges, nodes, ids, weight_in, bias, pieces, block):
+def base_call(edges, nodes, ids, weight_in, bias, early, pieces, block):
     count, latent = edges.shape
     hidden = weight_in.shape[1]
     degree = count // nodes.shape[0]
     size = sum(piece.shape[0] for piece in pieces)
     return launch(
-        lambda *refs: base_kernel(degree, *refs),
+        lambda *refs: base_kernel(degree, *refs[:5], *refs[5 + len(early) :]),
         grid=(count // block,),
         in_specs=[
             rows(edges, block),
@@ -125,14 +150,15 @@
             whole(weight_in),
             whole(bias),
         ]
+        + [pl.BlockSpec(memory_space=pl.ANY)] * len(early)
         + [whole(piece) for piece in pieces],
         out_specs=pl.BlockSpec((block, hidden), lambda i: (i, 0)),
         out_shape=jax.ShapeDtypeStruct((count, hidden), F32),
         scratch_shapes=[pltpu.VMEM((size, hidden), BF16)],
         compiler_params=params(),
-        cost_estimate=cost(15),
+        cost_estimate=cost("base_terms"),
         name="base_terms",
-    )(streamed(edges), nodes, ids, weight_in, bias, *pieces)
+    )(streamed(edges), nodes, ids, weight_in, bias, *early, *pieces)
 
 
 def edge_kernel(
@@ -170,7 +196,7 @@
     limit = first + table.shape[0]
     live = jnp.where(ids < limit, 1.0, 0.0)
     value = base_ref[...] + dot(one_hot(ids, first, table.shape[0]), table[...])
-    sig = jax.nn.sigmoid(value)
+    sig = 0.5 + 0.5 * jnp.tanh(0.5 * value)
     act = value * sig
     slope = sig + act * (1.0 - sig)
     hid = act.astype(BF16)
@@ -182,7 +208,9 @@
     gain = gain_ref[...]
     message = normed * gain
     new_ref[...] = (edge_ref[...].astype(F32) + message).astype(BF16)
-    agg_ref[...] = jnp.sum((message * live).reshape(nodes, degree, latent), axis=1)
+    pick = lax.broadcasted_iota(jnp.int32, (nodes, edges), 1) // degree
+    pick = jnp.where(pick == lax.broadcasted_iota(jnp.int32, (nodes, edges), 0), 1.0, 0.0).astype(BF16)
+    agg_ref[...] = dot(pick, (message * live).astype(BF16))
     ncot = jnp.broadcast_to(ncot_ref[...].astype(F32)[:, None, :], (nodes, degree, latent))
     cot = cot_ref[...].astype(F32)
     scaled = (cot + live * ncot.reshape(edges, latent)) * gain
@@ -192,7 +220,7 @@
     gproj_ref[...] = gproj
     gpre = (lax.dot_general(gproj, out_w_ref[...], COLS, preferred_element_type=F32) * slope).astype(BF16)
     gpre_ref[...] = gpre
-    psum_ref[...] = jnp.sum(gpre.astype(F32).reshape(nodes, degree, gpre.shape[1]), axis=1).astype(BF16)
+    psum_ref[...] = dot(pick, gpre).astype(BF16)
     back = lax.dot_general(gpre, weight_ref[:latent], COLS, preferred_element_type=F32)
     gedge_ref[...] = (cot + back).astype(BF16)
 
@@ -238,10 +266,10 @@
         out_specs=[spec for spec, _ in outs],
         out_shape=[shape for _, shape in outs],
         scratch_shapes=[pltpu.VMEM((last.shape[0] + 2 * low.shape[0], hidden), BF16)],
-        compiler_params=params(),
-        cost_estimate=cost(36),
+        compiler_params=params(EDGE_LIMIT),
+        cost_estimate=cost("edge_block"),
         name="edge_block",
-    )(streamed(base), ids, last, low, high, streamed(edges), streamed(cots), ncot, weight_in, weight_out, gain)
+    )(base, ids, last, low, high, streamed(edges), streamed(cots), ncot, weight_in, weight_out, gain)
 
 
 def select_kernel(ids_ref, *refs):
@@ -263,12 +291,13 @@
         select_kernel,
         out_shape=[half, half],
         compiler_params=params(),
-        cost_estimate=cost(2),
+        cost_estimate=cost("select_rows"),
         name="select_rows",
     )(ids, *pieces)
 
 
-def rim_sum_kernel(first, ids_ref, values_ref, low_ref, high_ref):
+def rim_sum_kernel(first, ids_ref, values_ref, mine_ref, got_ref, low_ref, high_ref, sum_ref):
+    sum_ref[...] = mine_ref[...] + got_ref[...]
     half = low_ref.shape[0]
     places = lax.broadcasted_iota(jnp.int32, (2 * half, ids_ref.shape[1]), 0) + first
     hot = jnp.where(places == ids_ref[...], 1.0, 0.0).astype(BF16)
@@ -277,15 +306,15 @@
     high_ref[...] = total[half:].astype(BF16)
 
 
-def rim_sum_call(ids, values, first, count):
+def rim_sum_call(ids, values, mine, got, first, count):
     half = jax.ShapeDtypeStruct((count // 2, values.shape[1]), BF16)
     return launch(
         lambda *refs: rim_sum_kernel(first, *refs),
-        out_shape=[half, half],
-        compiler_params=params(),
-        cost_estimate=cost(2.4),
+        out_shape=[half, half, jax.ShapeDtypeStruct(mine.shape, F32)],
+        compiler_params=params(),
+        cost_estimate=cost("rim_sums"),
         name="rim_sums",
-    )(ids, values)
+    )(ids, values, mine, got)
 
 
 def patch_sum_kernel(ids_ref, values_ref, out_ref):
@@ -304,16 +333,16 @@
         out_specs=pl.BlockSpec((block, width), lambda i: (i, 0)),
         out_shape=jax.ShapeDtypeStruct((count, width), F32),
         compiler_params=params(),
-        cost_estimate=cost(0.5),
+        cost_estimate=cost("patch_sums"),
         name="patch_sums",
     )(ids, values)
 
 
-def add_rim_kernel(ids_ref, low_ref, high_ref, start_ref, mine_ref, got_ref, *outs):
+def add_rim_kernel(ids_ref, low_ref, high_ref, start_ref, coarse_ref, *outs):
     half = low_ref.shape[0]
     size = outs[0].shape[0]
     latent = start_ref.shape[1]
-    coarse = mine_ref[...] + got_ref[...]
+    coarse = coarse_ref[...]
     few = coarse.shape[0]
     counts = coarse[:, 2 * latent :]
     high = jnp.floor(counts * (1.0 / 64.0))
@@ -331,17 +360,17 @@
             out[size + 2 * few :, 128:256] = (counts - 64.0 * high).astype(BF16)
 
 
-def add_rim_call(ids, low, high, start, mine, got, size, extended):
+def add_rim_call(ids, low, high, start, coarse, size, extended):
     count, width = start.shape
     pieces = count // size
-    extra = [3 * mine.shape[0] if extended and j == pieces - 1 else 0 for j in range(pieces)]
+    extra = [3 * coarse.shape[0] if extended and j == pieces - 1 else 0 for j in range(pieces)]
     return launch(
         add_rim_kernel,
         out_shape=[jax.ShapeDtypeStruct((size + more, width), BF16) for more in extra],
         compiler_params=params(),
-        cost_estimate=cost(15.0),
+        cost_estimate=cost("add_rim_sums"),
         name="add_rim_sums",
-    )(ids, low, high, start, mine, got)
+    )(ids, low, high, start, coarse)
 
 
 def edge_grads_kernel(edge_ref, gpre_ref, hid_ref, gproj_ref, in_ref, out_ref):
@@ -358,12 +387,12 @@
             jax.ShapeDtypeStruct((hidden, latent), F32),
         ],
         compiler_params=params(),
-        cost_estimate=cost(0.5),
+        cost_estimate=cost("edge_grads"),
         name="edge_grads",
     )(edges, gpre, hid, gproj)
 
 
-def pack_kernel(pieces, bit_ref, psum_ref, edge_ref, out_ref, patch_ref, low_ref, high_ref, *refs):
+def pack_kernel(pieces, where_ref, psum_ref, edge_ref, out_ref, patch_ref, low_ref, high_ref, *refs):
     tables = refs[:pieces]
     keep_ref, send_ref, total = refs[pieces:]
     latent = tables[0].shape[1]
@@ -381,7 +410,7 @@
     total[3 * latent :] = out_ref[...]
     feats, pairs, span, width = keep_ref.shape
     unit = span // 4
-    bit = bit_ref[0]
+    bit = where_ref[0] & 1
     for m in range(pairs):
         for slot in range(4):
             for ref, which in ((keep_ref, bit), (send_ref, 1 - bit)):
@@ -394,7 +423,7 @@
                     )
 
 
-def pack_call(bit, psum, edge_grad, out_grad, patch_sum, low, high, tables, feats, patches):
+def pack_call(where, psum, edge_grad, out_grad, patch_sum, low, high, tables, feats, patches):
     latent, hidden = edge_grad.shape
     shape = (feats, patches // 2, 4 * latent // patches, hidden // feats)
     vmem = pl.BlockSpec(memory_space=pltpu.VMEM)
@@ -404,15 +433,16 @@
         out_shape=[jax.ShapeDtypeStruct(shape, F32), jax.ShapeDtypeStruct(shape, BF16)],
         scratch_shapes=[pltpu.VMEM((4 * latent, hidden), F32)],
         compiler_params=params(),
-        cost_estimate=cost(0.5),
+        cost_estimate=cost("pack_grads"),
         name="pack_grads",
-    )(bit, psum, edge_grad, out_grad, patch_sum, low, high, *tables)
-
-
-def coarse_sum_kernel(ids_ref, lat_ref, cot_ref, bit_ref, mine_ref, other_ref):
+    )(where, psum, edge_grad, out_grad, patch_sum, low, high, *tables)
+
+
+def coarse_sum_kernel(ids_ref, lat_ref, cot_ref, where_ref, mine_ref, other_ref):
     latent = lat_ref.shape[1]
     half = mine_ref.shape[0]
-    for ref, bit in ((mine_ref, bit_ref[0]), (other_ref, 1 - bit_ref[0])):
+    core = where_ref[0] & 1
+    for ref, bit in ((mine_ref, core), (other_ref, 1 - core)):
         places = lax.broadcasted_iota(jnp.int32, (half, ids_ref.shape[1]), 0) + bit * half
         live = jnp.where(places == ids_ref[...], 1.0, 0.0)
         hot = live.astype(BF16)
@@ -421,7 +451,7 @@
         ref[:, 2 * latent :] = jnp.broadcast_to(jnp.sum(live, axis=1, keepdims=True), (half, 128))
 
 
-def coarse_sum_call(ids, lat, cot, bit, coarse):
+def coarse_sum_call(ids, lat, cot, where, coarse):
     vmem = pl.BlockSpec(memory_space=pltpu.VMEM)
     half = jax.ShapeDtypeStruct((coarse // 2, 2 * lat.shape[1] + 128), F32)
     return launch(
@@ -429,9 +459,9 @@
         in_specs=[vmem, vmem, vmem, pl.BlockSpec(memory_space=pltpu.SMEM)],
         out_shape=[half, half],
         compiler_params=params(),
-        cost_estimate=cost(1),
+        cost_estimate=cost("coarse_sums"),
         name="coarse_sums",
-    )(ids, lat, cot, bit)
+    )(ids, lat, cot, where)
 
 
 def add_pair_kernel(a_ref, b_ref, out_ref):
@@ -443,7 +473,7 @@
         add_pair_kernel,
         out_shape=jax.ShapeDtypeStruct(a.shape, a.dtype),
         compiler_params=params(),
-        cost_estimate=cost(1.0),
+        cost_estimate=cost("add_pair"),
         name="add_pair",
     )(a, b)
 
@@ -451,7 +481,7 @@
 def far_sum_kernel(own_ref, sent_ref, got_ref, far_ref, coarse_ref):
     size = own_ref.shape[0]
     far_ref[...] = (own_ref[...].astype(F32) + got_ref[:size].astype(F32)).astype(BF16)
-    coarse_ref[...] = sent_ref[size:].astype(F32) + got_ref[size:].astype(F32)
+    coarse_ref[...] = (sent_ref[size:].astype(F32) + got_ref[size:].astype(F32)).astype(BF16)
 
 
 def far_sum_call(own, sent, got):
@@ -460,32 +490,32 @@
         far_sum_kernel,
         out_shape=[
             jax.ShapeDtypeStruct((size, width), BF16),
-            jax.ShapeDtypeStruct((sent.shape[0] - size, width), F32),
+            jax.ShapeDtypeStruct((sent.shape[0] - size, width), BF16),
         ],
         compiler_params=params(),
-        cost_estimate=cost(1.0),
+        cost_estimate=cost("far_sum"),
         name="far_sum",
     )(own, sent, got)
 
 
-def add_split_kernel(bit_ref, keep_ref, got_ref, mine_ref, other_ref):
-    bit = bit_ref[0]
+def add_split_kernel(axis, shift, where_ref, keep_ref, got_ref, mine_ref, other_ref):
+    bit = (where_ref[axis] >> shift) & 1
     for ref, which in ((mine_ref, bit), (other_ref, 1 - bit)):
         for a in range(keep_ref.shape[0]):
             ref[a] = (keep_ref[a, which] + got_ref[a, which].astype(F32)).astype(ref.dtype)
 
 
-def add_split_call(bit, keep, got, send_type):
+def add_split_call(name, where, axis, distance, keep, got, send_type):
     vmem = pl.BlockSpec(memory_space=pltpu.VMEM)
     shape = keep.shape[:1] + keep.shape[2:]
     return launch(
-        add_split_kernel,
+        functools.partial(add_split_kernel, axis, distance.bit_length() - 1),
         in_specs=[pl.BlockSpec(memory_space=pltpu.SMEM), vmem, vmem],
         out_shape=[jax.ShapeDtypeStruct(shape, F32), jax.ShapeDtypeStruct(shape, send_type)],
         compiler_params=params(),
-        cost_estimate=cost(1.0),
-        name="add_split",
-    )(bit, keep, got)
+        cost_estimate=cost(name),
+        name=name,
+    )(where, keep, got)
 
 
 def last_grads_kernel(scale, keep_ref, got_ref, in_ref, out_ref):
@@ -503,20 +533,23 @@
             jax.ShapeDtypeStruct((span - rows_in, width), F32),
         ],
         compiler_params=params(),
-        cost_estimate=cost(1.5),
+        cost_estimate=cost("last_grads"),
         name="last_grads",
     )(keep, got)
 
 
-def node_kernel(place_ref, ids_ref, lat_ref, cot_ref, agg_ref, back_ref, *refs):
+def node_kernel(where_ref, ids_ref, lat_ref, cot_ref, agg_ref, back_ref, *refs):
     pieces, (new_ref, grad_ref, total) = refs[:-3], refs[-3:]
     latent = lat_ref.shape[1]
     for j, piece in enumerate(pieces):
         size = piece.shape[0] // 3
-        here = pl.ds(pl.multiple_of(place_ref[j] * size, size), size)
-        total[here, :latent] = piece[:size]
-        total[here, latent : 2 * latent] = piece[size : 2 * size]
-        total[here, 2 * latent :] = 64.0 * piece[2 * size :, :128] + piece[2 * size :, 128:256]
+        owner = where_ref[0] ^ j
+        place = (owner & 1) * 2 + (owner >> 1) if len(pieces) == 4 else j
+        here = pl.ds(pl.multiple_of(place * size, size), size)
+        total[here, :latent] = piece[:size].astype(F32)
+        total[here, latent : 2 * latent] = piece[size : 2 * size].astype(F32)
+        counts = piece[2 * size :].astype(F32)
+        total[here, 2 * latent :] = 64.0 * counts[:, :128] + counts[:, 128:256]
     sums = total[...]
     means = sums[:, : 2 * latent] / jnp.maximum(sums[:, 2 * latent : 2 * latent + 1], 1.0)
     places = lax.broadcasted_iota(jnp.int32, (sums.shape[0], ids_ref.shape[1]), 0)
@@ -529,7 +562,7 @@
     grad_ref[...] = (cot_ref[...].astype(F32) + back_ref[...] + pooled[:, latent:]).astype(BF16)
 
 
-def node_call(place, ids, lat, cot, agg, back, pieces):
+def node_call(where, ids, lat, cot, agg, back, pieces):
     vmem = pl.BlockSpec(memory_space=pltpu.VMEM)
     coarse = sum(piece.shape[0] // 3 for piece in pieces)
     width = 2 * lat.shape[1] + 128
@@ -539,9 +572,9 @@
         scratch_shapes=[pltpu.VMEM((coarse, width), F32)],
         out_shape=[jax.ShapeDtypeStruct(lat.shape, BF16)] * 2,
         compiler_params=params(),
-        cost_estimate=cost(2.0),
+        cost_estimate=cost("node_outputs"),
         name="node_outputs",
-    )(place, ids, lat, cot, streamed(agg), back, *pieces)
+    )(where, ids, lat, cot, agg, back, *pieces)
 
 
 def node_back_kernel(own_ref, far_ref, near_ref, psum_ref, weight_ref, out_ref):
@@ -559,7 +592,7 @@
         node_back_kernel,
         out_shape=jax.ShapeDtypeStruct(own.shape, F32),
         compiler_params=params(),
-        cost_estimate=cost(15.0),
+        cost_estimate=cost("grad_node"),
         name="grad_node",
     )(own, far, near, psum, weight_in)
 
@@ -633,11 +666,13 @@
     ids_col = ids[:, None]
     ids_row = ids[None, :]
     send_rel = relative(send_rows)
+    send_col = send_rel[:, None]
+    send_row = send_rel[None, :]
     bias = bias_in[None, :]
     gain = norm_gain[None, :]
     coarse_row = coarse_of[None, :]
 
-    core_bit = (patch % 2).astype(jnp.int32).reshape(1)
+    where = jnp.stack([patch, feat]).astype(jnp.int32)
     whole_step = feat_count == 4 and patch_count == 4
 
     if feat_count == 4:
@@ -650,19 +685,20 @@
         for distance in bits_of(feat_count):
             pieces = pieces + [xor_swap(piece, "feat", distance) for piece in pieces]
 
-    coarse, coarse_other = coarse_sum_call(coarse_row, node_lat, node_cotangent, core_bit, coarse_total)
+    coarse, coarse_other = coarse_sum_call(coarse_row, node_lat, node_cotangent, where, coarse_total)
     if whole_step:
         got = xor_swap(coarse_other, "patch", 1)
-        high_bit = (patch // 2).astype(jnp.int32).reshape(1)
         halves = (1, 2, coarse.shape[0] // 2, coarse.shape[1])
-        coarse, coarse_other = add_split_call(high_bit, coarse.reshape(halves), got.reshape(halves), F32)
+        coarse, coarse_other = add_split_call("coarse_split", where, 0, 2, coarse.reshape(halves), got.reshape(halves), F32)
         coarse, coarse_other = coarse[0], coarse_other[0]
         got = xor_swap(coarse_other, "patch", 2)
     else:
         coarse = coarse_reduce(coarse, coarse_other, patch)
         got = jnp.zeros_like(coarse)
-    base = base_call(flat_edges, node_lat, ids_col, weight_in, bias, pieces[:-1], block)
-    to_lower, to_upper = select_call(send_rel[:, None], pieces)
+    base = base_call(
+        flat_edges, node_lat, ids_col, weight_in, bias, (ids_row, send_col, send_row, coarse_row), pieces[:-1], block
+    )
+    to_lower, to_upper = select_call(send_col, pieces)
     from_lower = lax.ppermute(to_upper, "patch", ring_up)
     from_upper = lax.ppermute(to_lower, "patch", ring_down)
     coarse = add_pair_call(coarse, got)
@@ -683,30 +719,36 @@
         patch_total - node_count,
         block)
 
-    rim_low, rim_high = rim_sum_call(ids_row, grad_pre, patch_total, 2 * rim_rows)
+    rim_low, rim_high, coarse = rim_sum_call(ids_row, grad_pre, coarse, got, patch_total, 2 * rim_rows)
     back_upper = lax.ppermute(rim_low, "patch", ring_down)
     back_lower = lax.ppermute(rim_high, "patch", ring_up)
     patch_sum = patch_sum_call(ids_row, grad_pre, patch_total, node_count)
+    span, width = 4 * latent // patch_count, latent // feat_count
+    steps = [("patch", d) for d in bits_of(patch_count)[1:]] + [("feat", d) for d in bits_of(feat_count)]
+
+    def fold(step, keep, received):
+        axis, distance = steps[step]
+        shape = (-1, 2, span, width)
+        keep, send = add_split_call(
+            f"fold{min(step, 2)}",
+            where,
+            int(axis == "feat"),
+            distance,
+            keep.reshape(shape),
+            received.reshape(shape),
+            BF16,
+        )
+        return keep, xor_swap(send, axis, distance)
+
     edge_grad, out_grad = edge_grads_call(flat_edges, grad_pre, hidden_act, grad_proj)
+    sums = add_rim_call(
+        send_row, back_lower, back_upper, patch_sum, coarse, node_count, whole_step
+    )
     tables = pieces + [from_lower, from_upper]
     keep, send = pack_call(
-        core_bit, pre_sum, edge_grad, out_grad, patch_sum, rim_low, rim_high, tables, feat_count, patch_count
+        where, pre_sum, edge_grad, out_grad, patch_sum, rim_low, rim_high, tables, feat_count, patch_count
     )
     got_core = xor_swap(send, "patch", 1)
-    sums = add_rim_call(
-        send_rel[None, :], back_lower, back_upper, patch_sum, coarse, got, node_count, whole_step
-    )
-    span, width = keep.shape[2:]
-    steps = [("patch", d) for d in bits_of(patch_count)[1:]] + [("feat", d) for d in bits_of(feat_count)]
-
-    def fold(step, keep, received):
-        axis, distance = steps[step]
-        index = patch if axis == "patch" else feat
-        bit = ((index // distance) % 2).astype(jnp.int32).reshape(1)
-        shape = (-1, 2, span, width)
-        keep, send = add_split_call(bit, keep.reshape(shape), received.reshape(shape), BF16)
-        return keep, xor_swap(send, axis, distance)
-
     keep, received = fold(0, keep, got_core)
     if feat_count == 4:
         relay = xor_swap(sums[3], "feat", 1)
@@ -728,13 +770,11 @@
     keep, received = fold(2, keep, received)
     if whole_step:
         parts = [coarse_all] + [xor_swap(coarse_all, "patch", j) for j in range(1, 4)]
-        place = jnp.stack([((patch ^ j) % 2) * 2 + (patch ^ j) // 2 for j in range(4)]).astype(jnp.int32)
     else:
         counts = jnp.pad(coarse[:, 2 * latent :], ((0, 0), (128, latent - 256)))
         parts = [jnp.concatenate([coarse[:, :latent], coarse[:, latent : 2 * latent], counts], axis=0)]
-        place = jnp.zeros((1,), jnp.int32)
     node_new, grad_node = node_call(
-        place, coarse_row, node_lat, node_cotangent, aggregate, back, parts
+        where, coarse_row, node_lat, node_cotangent, aggregate, back, parts
     )
     for step in range(3, len(steps)):
         keep, received = fold(step, keep, received)

time: 95.1 us -> 93.7 us (0.985)
  local copies, waits for them, and re-layouts: 7.44 us -> 3.3 us
  waiting for transfers between devices: 26.4 us -> 28.6 us
  Pallas kernels: 32.6 us -> 34 us
    unnamed x38 -> x26, local copies, waits for them, and re-layouts: 6.75 us -> 2.62 us
    ppermute x16, waiting for transfers between devices: 26.4 us -> 28.6 us  [xor_swap(): return lax.ppermute(value, axis, [(i, i ^ distance) for i in range(size)])]
    pallas_call x18, Pallas kernels: 32.6 us -> 34 us  [call(): pl.pallas_call(body, out_shape=outs + [mark], in_specs=specs, out_specs=p...]
  transfers between devices with their start and end apart: 20 -> 20, of which waited for: 10 -> 10; matrix products, arithmetic and copies ran while one was open for 1% -> 1% of each run, Pallas kernels for 34% -> 32%
where the time goes in v4:
time: 93.7 us; the launch traced here: 93.4 us
  Pallas kernels  34 us (36%)
  waiting for transfers between devices  28.6 us (31%)
  starting transfers between devices  26.5 us (28%)
  local copies, waits for them, and re-layouts  3.3 us (4%)
    pallas_call x18, Pallas kernels, call(): pl.pallas_call(body, out_shape=outs + [mark], in_specs=specs, out_specs=p...  34 us
    ppermute x16, waiting for transfers between devices, xor_swap(): return lax.ppermute(value, axis, [(i, i ^ distance) for i in range(size)])  28.6 us
    ppermute x16, starting transfers between devices, xor_swap(): return lax.ppermute(value, axis, [(i, i ^ distance) for i in range(size)])  22.9 us
    unnamed x26, local copies, waits for them, and re-layouts  2.62 us
  transfers between devices with their start and end apart: 20, of which 10 were waited for; matrix products, arithmetic and copies ran while one was open for 1% of the time, Pallas kernels for 32%

profile of v4, /device:TPU:0, one launch (start us, length us, event | category | flops | bytes accessed | tf_op | source)
XLA Modules:
  0.0 93.4 jit_solution(16827881246292766408)
XLA Ops:
  0.6 4.1 %collective-permute-start.1 = (bf16[256,512]{1,0:T(8,128)(2,1)}, bf16[256,512]{1,0:T(8,128)(2,1)S(1)}, u32[]{:S(2)}, u32[]{:S(2)}) collective-permute-start(bf16[256,512]{1,0:T(8,128)(2,1)} %refs_2_.3), channel_id=1, source_target_pairs={{0,2},{1,3},{2,0},{3,1},{4,6},{5,7},{6,4},{7,5},{8,10},{9,11},{10,... | collective-permute-start | bytes 786440 | tf_op jit(solution)/shard_map/ppermute | solution.py:602
  4.7 1.6 %collective-permute-start = (bf16[256,512]{1,0:T(8,128)(2,1)}, bf16[256,512]{1,0:T(8,128)(2,1)S(1)}, u32[]{:S(2)}, u32[]{:S(2)}) collective-permute-start(bf16[256,512]{1,0:T(8,128)(2,1)} %refs_2_.3), channel_id=1, source_target_pairs={{0,1},{1,0},{2,3},{3,2},{4,5},{5,4},{6,7},{7,6},{8,9},{9,8},{10,11... | collective-permute-start | bytes 786440 | tf_op jit(solution)/shard_map/ppermute | solution.py:602
  6.4 0.9 %copy-done.1 = bf16[256,512]{1,0:T(8,128)(2,1)S(1)} copy-done((bf16[256,512]{1,0:T(8,128)(2,1)S(1)}, bf16[256,512]{1,0:T(8,128)(2,1)}, u32[]{:S(2)}) %copy-start.1) | copy-done | bytes 262168
  11.8 1.6 %collective-permute-start.6 = (f32[16,1152]{1,0:T(8,128)S(1)}, f32[16,1152]{1,0:T(8,128)S(1)}, u32[]{:S(2)}, u32[]{:S(2)}) collective-permute-start(f32[16,1152]{1,0:T(8,128)S(1)} %bitcast.35), channel_id=1, source_target_pairs={{0,8},{4,12},{8,0},{12,4},{1,9},{5,13},{9,1},{13,5},{2,10},{6,14},... | collective-permute-start | bytes 221192 | tf_op jit(solution)/shard_map/ppermute | solution.py:602
  13.4 3.6 %collective-permute-done.1.refs_11_.refs_3_.refs_9_ = bf16[256,512]{1,0:T(8,128)(2,1)S(1)} collective-permute-done((bf16[256,512]{1,0:T(8,128)(2,1)}, bf16[256,512]{1,0:T(8,128)(2,1)S(1)}, u32[]{:S(2)}, u32[]{:S(2)}) %collective-permute-start.1) | collective-permute-done | bytes 262176 | tf_op jit(solution)/shard_map/ppermute | solution.py:602
  17.7 5.9 %base_terms.1 = (f32[2048,512]{1,0:T(8,128)S(1)}, f32[8,128]{1,0:T(8,128)S(1)}) custom-call(bf16[2048,512]{1,0:T(8,128)(2,1)} %bitcast.23, bf16[256,512]{1,0:T(8,128)(2,1)S(1)} %copy-done.2, s32[2048,1]{1,0:T(8,128)S(1)} %broadcast_in_dim_reshape.8.refs_2_.refs_1_, bf16[1536,512]{1,0:T(8,128)(2,1)S(1)} %copy-done.3, f32[1,512]{1,0:T(1,128)S(1)} %bitcast.36, ...), custom_call_target="tpu_custom_call" | custom-call | flops 17250000896 | bytes 1048576 | tf_op jit(solution)/shard_map/base_terms/pallas_call | solution.py:80
  25.0 1.7 %collective-permute-start.5 = (bf16[128,512]{1,0:T(8,128)(2,1)S(1)}, bf16[128,512]{1,0:T(8,128)(2,1)S(1)}, u32[]{:S(2)}, u32[]{:S(2)}) collective-permute-start(bf16[128,512]{1,0:T(8,128)(2,1)S(1)} %get-tuple-element.70), channel_id=1, source_target_pairs={{4,0},{8,4},{12,8},{0,12},{5,1},{9,5},{13,9},{1,13},{6,2},{10,6},{... | collective-permute-start | bytes 393224 | tf_op jit(solution)/shard_map/ppermute | solution.py:703
  26.7 3.1 %collective-permute-start.7 = (f32[16,1152]{1,0:T(8,128)S(1)}, f32[16,1152]{1,0:T(8,128)S(1)}, u32[]{:S(2)}, u32[]{:S(2)}) collective-permute-start(f32[16,1152]{1,0:T(8,128)S(1)} %get-tuple-element.78.refs_2_), channel_id=1, source_target_pairs={{0,2},{1,3},{2,0},{3,1},{4,6},{5,7},{6,4},{7,5},{8,10},{9,11},{10,... | collective-permute-start | bytes 221192 | tf_op jit(solution)/shard_map/ppermute | solution.py:602
  29.9 12.5 %edge_block.1 = (bf16[2048,512]{1,0:T(8,128)(2,1)}, f32[256,512]{1,0:T(8,128)S(1)}, bf16[2048,512]{1,0:T(8,128)(2,1)S(1)}, bf16[2048,512]{1,0:T(8,128)(2,1)S(1)}...) custom-call(f32[2048,512]{1,0:T(8,128)S(1)} %get-tuple-element.67.re, ...), custom_call_target="tpu_custom_call" | custom-call | flops 41400000512 | bytes 1048576 | tf_op jit(solution)/shard_map/edge_block/pallas_call | solution.py:80
  44.9 2.8 %patch_sums.1 = (f32[1024,512]{1,0:T(8,128)S(1)}, f32[8,128]{1,0:T(8,128)S(1)}) custom-call(s32[1,2048]{1,0:T(1,128)S(1)} %broadcast_in_dim_reshape.7.refs_5_.refs_0_, bf16[2048,512]{1,0:T(8,128)(2,1)S(1)} %get-tuple-element.77.refs_1_, f32[8,128]{1,0:T(8,128)S(1)} %get-tuple-element.82.refs_2_), custom_call_target="tpu_custom_call" | custom-call | flops 345000000 | bytes 1048576 | tf_op jit(solution)/shard_map/patch_sums/pallas_call | solution.py:80
  47.7 2.4 %edge_grads.1 = (f32[512,512]{1,0:T(8,128)S(1)}, f32[512,512]{1,0:T(8,128)S(1)}, f32[8,128]{1,0:T(8,128)S(1)}) custom-call(bf16[2048,512]{1,0:T(8,128)(2,1)S(1)} %bitcast.25, bf16[2048,512]{1,0:T(8,128)(2,1)S(1)} %get-tuple-element.77.refs_1_, bf16[2048,512]{1,0:T(8,128)(2,1)S(1)} %get-tuple-element.85.refs_2_, ...), custom_call_target="tpu_custom_call" | custom-call | flops 345000000 | bytes 1048576 | tf_op jit(solution)/shard_map/edge_grads/pallas_call | solution.py:80
  50.8 2.1 %pack_grads.1 = (f32[4,2,512,128]{3,2,1,0:T(8,128)S(1)}, bf16[4,2,512,128]{3,2,1,0:T(8,128)(2,1)S(1)}, f32[8,128]{1,0:T(8,128)S(1)}) custom-call(s32[2]{0:T(128)S(1)} %pad_add_fusion.refs_3_.refs_0_, bf16[256,512]{1,0:T(8,128)(2,1)S(1)} %get-tuple-element.92.refs_1_.refs_3_, f32[512,512]{1,0:T(8,128)S(1)} %get-tuple-element.93.refs_2_, ...), custom_call_target="tpu_custom_call" | custom-call | flops 345000000 | bytes 1048576 | tf_op jit(solution)/shard_map/pack_grads/pallas_call | solution.py:80
  53.0 1.8 %collective-permute-start.10 = (bf16[304,512]{1,0:T(8,128)(2,1)S(1)}, bf16[304,512]{1,0:T(8,128)(2,1)S(1)}, u32[]{:S(2)}, u32[]{:S(2)}) collective-permute-start(bf16[304,512]{1,0:T(8,128)(2,1)S(1)} %get-tuple-element.91.refs_1_), channel_id=1, source_target_pairs={{0,1},{1,0},{2,3},{3,2},{4,5},{5,4},{6,7},{7,6},{8,9},{9,8},{10,11... | collective-permute-start | bytes 933896 | tf_op jit(solution)/shard_map/ppermute | solution.py:602
  56.4 1.6 %collective-permute-start.14 = (bf16[4,512,128]{2,1,0:T(8,128)(2,1)S(1)}, bf16[4,512,128]{2,1,0:T(8,128)(2,1)S(1)}, u32[]{:S(2)}, u32[]{:S(2)}) collective-permute-start(bf16[4,512,128]{2,1,0:T(8,128)(2,1)S(1)} %get-tuple-element.103), channel_id=1, source_target_pairs={{0,8},{4,12},{8,0},{12,4},{1,9},{5,13},{9,1},{13,5},{2,10},{6,14},... | collective-permute-start | bytes 1572872 | tf_op jit(solution)/shard_map/ppermute | solution.py:602
  58.0 5.2 %collective-permute-done.10.refs_2_ = bf16[304,512]{1,0:T(8,128)(2,1)S(1)} collective-permute-done((bf16[304,512]{1,0:T(8,128)(2,1)S(1)}, bf16[304,512]{1,0:T(8,128)(2,1)S(1)}, u32[]{:S(2)}, u32[]{:S(2)}) %collective-permute-start.10) | collective-permute-done | bytes 311328 | tf_op jit(solution)/shard_map/ppermute | solution.py:602
  63.3 3.2 %collective-permute-start.12 = (bf16[256,512]{1,0:T(8,128)(2,1)S(1)}, bf16[256,512]{1,0:T(8,128)(2,1)S(1)}, u32[]{:S(2)}, u32[]{:S(2)}) collective-permute-start(bf16[256,512]{1,0:T(8,128)(2,1)S(1)} %get-tuple-element.100), channel_id=1, source_target_pairs={{0,2},{1,3},{2,0},{3,1},{4,6},{5,7},{6,4},{7,5},{8,10},{9,11},{10,... | collective-permute-start | bytes 786440 | tf_op jit(solution)/shard_map/ppermute | solution.py:602
  66.5 1.5 %collective-permute-start.16 = (bf16[48,512]{1,0:T(8,128)(2,1)S(1)}, bf16[48,512]{1,0:T(8,128)(2,1)S(1)}, u32[]{:S(2)}, u32[]{:S(2)}) collective-permute-start(bf16[48,512]{1,0:T(8,128)(2,1)S(1)} %get-tuple-element.107.refs_6_), channel_id=1, source_target_pairs={{0,8},{4,12},{8,0},{12,4},{1,9},{5,13},{9,1},{13,5},{2,10},{6,14},... | collective-permute-start | bytes 147464 | tf_op jit(solution)/shard_map/ppermute | solution.py:602
  68.0 2.9 %collective-permute-done.14 = bf16[4,512,128]{2,1,0:T(8,128)(2,1)S(1)} collective-permute-done((bf16[4,512,128]{2,1,0:T(8,128)(2,1)S(1)}, bf16[4,512,128]{2,1,0:T(8,128)(2,1)S(1)}, u32[]{:S(2)}, u32[]{:S(2)}) %collective-permute-start.14) | collective-permute-done | bytes 524320 | tf_op jit(solution)/shard_map/ppermute | solution.py:602
  71.6 1.2 %collective-permute-done.13.refs_2_ = bf16[256,512]{1,0:T(8,128)(2,1)S(1)} collective-permute-done((bf16[256,512]{1,0:T(8,128)(2,1)S(1)}, bf16[256,512]{1,0:T(8,128)(2,1)S(1)}, u32[]{:S(2)}, u32[]{:S(2)}) %collective-permute-start.13) | collective-permute-done | bytes 262176 | tf_op jit(solution)/shard_map/ppermute | solution.py:602
  73.4 4.5 %collective-permute-done.12.refs_1_ = bf16[256,512]{1,0:T(8,128)(2,1)S(1)} collective-permute-done((bf16[256,512]{1,0:T(8,128)(2,1)S(1)}, bf16[256,512]{1,0:T(8,128)(2,1)S(1)}, u32[]{:S(2)}, u32[]{:S(2)}) %collective-permute-start.12) | collective-permute-done | bytes 262176 | tf_op jit(solution)/shard_map/ppermute | solution.py:602
  78.4 4.3 %collective-permute-done.18 = bf16[2,512,128]{2,1,0:T(8,128)(2,1)S(1)} collective-permute-done((bf16[2,512,128]{2,1,0:T(8,128)(2,1)S(1)}, bf16[2,512,128]{2,1,0:T(8,128)(2,1)S(1)}, u32[]{:S(2)}, u32[]{:S(2)}) %collective-permute-start.18) | collective-permute-done | bytes 262176 | tf_op jit(solution)/shard_map/ppermute | solution.py:602
  83.3 2.7 %collective-permute-start.19 = (bf16[1,512,128]{2,1,0:T(8,128)(2,1)S(1)}, bf16[1,512,128]{2,1,0:T(8,128)(2,1)S(1)}, u32[]{:S(2)}, u32[]{:S(2)}) collective-permute-start(bf16[1,512,128]{2,1,0:T(8,128)(2,1)S(1)} %get-tuple-element.116), channel_id=1, source_target_pairs={{0,2},{1,3},{2,0},{3,1},{4,6},{5,7},{6,4},{7,5},{8,10},{9,11},{10,... | collective-permute-start | bytes 393224 | tf_op jit(solution)/shard_map/ppermute | solution.py:602
  86.0 1.8 %node_outputs.1 = (bf16[256,512]{1,0:T(8,128)(2,1)}, bf16[256,512]{1,0:T(8,128)(2,1)}, f32[8,128]{1,0:T(8,128)S(1)}) custom-call(s32[2]{0:T(128)S(1)} %pad_add_fusion.refs_3_.refs_0_, s32[1,256]{1,0:T(1,128)S(1)} %bitcast.40, bf16[256,512]{1,0:T(8,128)(2,1)S(1)} %copy-done.2, bf16[256,512]{1,0:T(8,128)(2,1)S(1)} %copy-done.6, ...), custom_call_target="tpu_custom_call" | custom-call | flops 2300000000 | bytes 1048576 | tf_op jit(solution)/shard_map/node_outputs/pallas_call | solution.py:80
  87.8 4.9 %collective-permute-done.19 = bf16[1,512,128]{2,1,0:T(8,128)(2,1)S(1)} collective-permute-done((bf16[1,512,128]{2,1,0:T(8,128)(2,1)S(1)}, bf16[1,512,128]{2,1,0:T(8,128)(2,1)S(1)}, u32[]{:S(2)}, u32[]{:S(2)}) %collective-permute-start.19) | collective-permute-done | bytes 131104 | tf_op jit(solution)/shard_map/ppermute | solution.py:602
  (67 shorter events, 14.6 us)
Async XLA Ops:
  0.6 16.3 %collective-permute-start.1 = (bf16[256,512]{1,0:T(8,128)(2,1)}, bf16[256,512]{1,0:T(8,128)(2,1)S(1)}, u32[]{:S(2)}, u32[]{:S(2)}) collective-permute-start(bf16[256,512]{1,0:T(8,128)(2,1)} %refs_2_.3), channel_id=1, source_target_pairs={{0,2},{1,3},{2,0},{3,1},{4,6},{5,7},{6,4},{7,5},{8,10},{9,11},{10,... | collective-permute-start | bytes 786440 | tf_op jit(solution)/shard_map/ppermute | solution.py:602
  4.7 13.0 %collective-permute-start = (bf16[256,512]{1,0:T(8,128)(2,1)}, bf16[256,512]{1,0:T(8,128)(2,1)S(1)}, u32[]{:S(2)}, u32[]{:S(2)}) collective-permute-start(bf16[256,512]{1,0:T(8,128)(2,1)} %refs_2_.3), channel_id=1, source_target_pairs={{0,1},{1,0},{2,3},{3,2},{4,5},{5,4},{6,7},{7,6},{8,9},{9,8},{10,11... | collective-permute-start | bytes 786440 | tf_op jit(solution)/shard_map/ppermute | solution.py:602
  9.8 1.4 %collective-permute-start.2 = (f32[32,1152]{1,0:T(8,128)S(1)}, f32[32,1152]{1,0:T(8,128)S(1)}, u32[]{:S(2)}, u32[]{:S(2)}) collective-permute-start(f32[32,1152]{1,0:T(8,128)S(1)} %get-tuple-element.64), channel_id=1, source_target_pairs={{0,4},{4,0},{8,12},{12,8},{1,5},{5,1},{9,13},{13,9},{2,6},{6,2},{1... | collective-permute-start | bytes 442376 | tf_op jit(solution)/shard_map/ppermute | solution.py:602
  11.2 6.5 %copy-start.2 = (bf16[256,512]{1,0:T(8,128)(2,1)S(1)}, bf16[256,512]{1,0:T(8,128)(2,1)}, u32[]{:S(2)}) copy-start(bf16[256,512]{1,0:T(8,128)(2,1)} %refs_2_.3) | copy-start | bytes 786436
  11.2 6.5 %copy-start.3 = (bf16[1536,512]{1,0:T(8,128)(2,1)S(1)}, bf16[1536,512]{1,0:T(8,128)(2,1)}, u32[]{:S(2)}) copy-start(bf16[1536,512]{1,0:T(8,128)(2,1)} %refs_4_.1) | copy-start | bytes 4718596
  11.2 6.5 %copy-start.7 = (f32[512]{0:T(512)S(1)}, f32[512]{0:T(512)}, u32[]{:S(2)}) copy-start(f32[512]{0:T(512)} %param.17) | copy-start | bytes 6148
  11.2 6.5 %copy-start.10 = (s32[256]{0:T(256)S(1)}, s32[256]{0:T(256)}, u32[]{:S(2)}) copy-start(s32[256]{0:T(256)} %param.15) | copy-start | bytes 3076
  11.8 14.9 %collective-permute-start.6 = (f32[16,1152]{1,0:T(8,128)S(1)}, f32[16,1152]{1,0:T(8,128)S(1)}, u32[]{:S(2)}, u32[]{:S(2)}) collective-permute-start(f32[16,1152]{1,0:T(8,128)S(1)} %bitcast.35), channel_id=1, source_target_pairs={{0,8},{4,12},{8,0},{12,4},{1,9},{5,13},{9,1},{13,5},{2,10},{6,14},... | collective-permute-start | bytes 221192 | tf_op jit(solution)/shard_map/ppermute | solution.py:602
  17.0 7.4 %collective-permute-start.3 = (bf16[256,512]{1,0:T(8,128)(2,1)S(1)}, bf16[256,512]{1,0:T(8,128)(2,1)S(1)}, u32[]{:S(2)}, u32[]{:S(2)}) collective-permute-start(bf16[256,512]{1,0:T(8,128)(2,1)S(1)} %collective-permute-done.1.refs_11_.refs_3_.refs_9_), channel_id=1, source_target_pairs={{0,1},{1,0},{2,3},{3,2},{4,5},{5,4},{6,7},{7,6},{8,9},{9,8},{10,11... | collective-permute-start | bytes 786440 | tf_op jit(solution)/shard_map/ppermute | solution.py:602
  24.9 4.9 %collective-permute-start.4 = (bf16[128,512]{1,0:T(8,128)(2,1)S(1)}, bf16[128,512]{1,0:T(8,128)(2,1)S(1)}, u32[]{:S(2)}, u32[]{:S(2)}) collective-permute-start(bf16[128,512]{1,0:T(8,128)(2,1)S(1)} %get-tuple-element.69), channel_id=1, source_target_pairs={{0,4},{4,8},{8,12},{12,0},{1,5},{5,9},{9,13},{13,1},{2,6},{6,10},{... | collective-permute-start | bytes 393224 | tf_op jit(solution)/shard_map/ppermute | solution.py:702
  25.0 4.9 %collective-permute-start.5 = (bf16[128,512]{1,0:T(8,128)(2,1)S(1)}, bf16[128,512]{1,0:T(8,128)(2,1)S(1)}, u32[]{:S(2)}, u32[]{:S(2)}) collective-permute-start(bf16[128,512]{1,0:T(8,128)(2,1)S(1)} %get-tuple-element.70), channel_id=1, source_target_pairs={{4,0},{8,4},{12,8},{0,12},{5,1},{9,5},{13,9},{1,13},{6,2},{10,6},{... | collective-permute-start | bytes 393224 | tf_op jit(solution)/shard_map/ppermute | solution.py:703
  26.7 15.6 %collective-permute-start.7 = (f32[16,1152]{1,0:T(8,128)S(1)}, f32[16,1152]{1,0:T(8,128)S(1)}, u32[]{:S(2)}, u32[]{:S(2)}) collective-permute-start(f32[16,1152]{1,0:T(8,128)S(1)} %get-tuple-element.78.refs_2_), channel_id=1, source_target_pairs={{0,2},{1,3},{2,0},{3,1},{4,6},{5,7},{6,4},{7,5},{8,10},{9,11},{10,... | collective-permute-start | bytes 221192 | tf_op jit(solution)/shard_map/ppermute | solution.py:602
  43.1 7.0 %collective-permute-start.8 = (bf16[128,512]{1,0:T(8,128)(2,1)S(1)}, bf16[128,512]{1,0:T(8,128)(2,1)S(1)}, u32[]{:S(2)}, u32[]{:S(2)}) collective-permute-start(bf16[128,512]{1,0:T(8,128)(2,1)S(1)} %get-tuple-element.80.refs_6_), channel_id=1, source_target_pairs={{0,4},{4,8},{8,12},{12,0},{1,5},{5,9},{9,13},{13,1},{2,6},{6,10},{... | collective-permute-start | bytes 393224 | tf_op jit(solution)/shard_map/ppermute | solution.py:724
  44.0 6.1 %collective-permute-start.9 = (bf16[128,512]{1,0:T(8,128)(2,1)S(1)}, bf16[128,512]{1,0:T(8,128)(2,1)S(1)}, u32[]{:S(2)}, u32[]{:S(2)}) collective-permute-start(bf16[128,512]{1,0:T(8,128)(2,1)S(1)} %get-tuple-element.81.refs_5_), channel_id=1, source_target_pairs={{4,0},{8,4},{12,8},{0,12},{5,1},{9,5},{13,9},{1,13},{6,2},{10,6},{... | collective-permute-start | bytes 393224 | tf_op jit(solution)/shard_map/ppermute | solution.py:723
  52.9 2.7 %collective-permute-start.11 = (bf16[4,2,512,128]{3,2,1,0:T(8,128)(2,1)S(1)}, bf16[4,2,512,128]{3,2,1,0:T(8,128)(2,1)S(1)}, u32[]{:S(2)}, u32[]{:S(2)}) collective-permute-start(bf16[4,2,512,128]{3,2,1,0:T(8,128)(2,1)S(1)} %get-tuple-element.97), channel_id=1, source_target_pairs={{0,4},{4,0},{8,12},{12,8},{1,5},{5,1},{9,13},{13,9},{2,6},{6,2},{1... | collective-permute-start | bytes 3145736 | tf_op jit(solution)/shard_map/ppermute | solution.py:602
  53.0 10.2 %collective-permute-start.10 = (bf16[304,512]{1,0:T(8,128)(2,1)S(1)}, bf16[304,512]{1,0:T(8,128)(2,1)S(1)}, u32[]{:S(2)}, u32[]{:S(2)}) collective-permute-start(bf16[304,512]{1,0:T(8,128)(2,1)S(1)} %get-tuple-element.91.refs_1_), channel_id=1, source_target_pairs={{0,1},{1,0},{2,3},{3,2},{4,5},{5,4},{6,7},{7,6},{8,9},{9,8},{10,11... | collective-permute-start | bytes 933896 | tf_op jit(solution)/shard_map/ppermute | solution.py:602
  54.8 18.0 %collective-permute-start.13 = (bf16[256,512]{1,0:T(8,128)(2,1)S(1)}, bf16[256,512]{1,0:T(8,128)(2,1)S(1)}, u32[]{:S(2)}, u32[]{:S(2)}) collective-permute-start(bf16[256,512]{1,0:T(8,128)(2,1)S(1)} %get-tuple-element.101), channel_id=1, source_target_pairs={{0,1},{1,0},{2,3},{3,2},{4,5},{5,4},{6,7},{7,6},{8,9},{9,8},{10,11... | collective-permute-start | bytes 786440 | tf_op jit(solution)/shard_map/ppermute | solution.py:602
  56.4 14.6 %collective-permute-start.14 = (bf16[4,512,128]{2,1,0:T(8,128)(2,1)S(1)}, bf16[4,512,128]{2,1,0:T(8,128)(2,1)S(1)}, u32[]{:S(2)}, u32[]{:S(2)}) collective-permute-start(bf16[4,512,128]{2,1,0:T(8,128)(2,1)S(1)} %get-tuple-element.103), channel_id=1, source_target_pairs={{0,8},{4,12},{8,0},{12,4},{1,9},{5,13},{9,1},{13,5},{2,10},{6,14},... | collective-permute-start | bytes 1572872 | tf_op jit(solution)/shard_map/ppermute | solution.py:602
  63.3 14.7 %collective-permute-start.12 = (bf16[256,512]{1,0:T(8,128)(2,1)S(1)}, bf16[256,512]{1,0:T(8,128)(2,1)S(1)}, u32[]{:S(2)}, u32[]{:S(2)}) collective-permute-start(bf16[256,512]{1,0:T(8,128)(2,1)S(1)} %get-tuple-element.100), channel_id=1, source_target_pairs={{0,2},{1,3},{2,0},{3,1},{4,6},{5,7},{6,4},{7,5},{8,10},{9,11},{10,... | collective-permute-start | bytes 786440 | tf_op jit(solution)/shard_map/ppermute | solution.py:602
  66.5 19.5 %collective-permute-start.15 = (bf16[48,512]{1,0:T(8,128)(2,1)S(1)}, bf16[48,512]{1,0:T(8,128)(2,1)S(1)}, u32[]{:S(2)}, u32[]{:S(2)}) collective-permute-start(bf16[48,512]{1,0:T(8,128)(2,1)S(1)} %get-tuple-element.107.refs_6_), channel_id=1, source_target_pairs={{0,4},{4,0},{8,12},{12,8},{1,5},{5,1},{9,13},{13,9},{2,6},{6,2},{1... | collective-permute-start | bytes 147464 | tf_op jit(solution)/shard_map/ppermute | solution.py:602
  66.5 19.5 %collective-permute-start.16 = (bf16[48,512]{1,0:T(8,128)(2,1)S(1)}, bf16[48,512]{1,0:T(8,128)(2,1)S(1)}, u32[]{:S(2)}, u32[]{:S(2)}) collective-permute-start(bf16[48,512]{1,0:T(8,128)(2,1)S(1)} %get-tuple-element.107.refs_6_), channel_id=1, source_target_pairs={{0,8},{4,12},{8,0},{12,4},{1,9},{5,13},{9,1},{13,5},{2,10},{6,14},... | collective-permute-start | bytes 147464 | tf_op jit(solution)/shard_map/ppermute | solution.py:602
  70.9 15.0 %collective-permute-start.17 = (bf16[48,512]{1,0:T(8,128)(2,1)S(1)}, bf16[48,512]{1,0:T(8,128)(2,1)S(1)}, u32[]{:S(2)}, u32[]{:S(2)}) collective-permute-start(bf16[48,512]{1,0:T(8,128)(2,1)S(1)} %get-tuple-element.107.refs_6_), channel_id=1, source_target_pairs={{0,12},{4,8},{8,4},{12,0},{1,13},{5,9},{9,5},{13,1},{2,14},{6,10},... | collective-permute-start | bytes 147464 | tf_op jit(solution)/shard_map/ppermute | solution.py:602
  72.8 9.9 %collective-permute-start.18 = (bf16[2,512,128]{2,1,0:T(8,128)(2,1)S(1)}, bf16[2,512,128]{2,1,0:T(8,128)(2,1)S(1)}, u32[]{:S(2)}, u32[]{:S(2)}) collective-permute-start(bf16[2,512,128]{2,1,0:T(8,128)(2,1)S(1)} %get-tuple-element.109), channel_id=1, source_target_pairs={{0,1},{1,0},{2,3},{3,2},{4,5},{5,4},{6,7},{7,6},{8,9},{9,8},{10,11... | collective-permute-start | bytes 786440 | tf_op jit(solution)/shard_map/ppermute | solution.py:602
  83.3 9.4 %collective-permute-start.19 = (bf16[1,512,128]{2,1,0:T(8,128)(2,1)S(1)}, bf16[1,512,128]{2,1,0:T(8,128)(2,1)S(1)}, u32[]{:S(2)}, u32[]{:S(2)}) collective-permute-start(bf16[1,512,128]{2,1,0:T(8,128)(2,1)S(1)} %get-tuple-element.116), channel_id=1, source_target_pairs={{0,2},{1,3},{2,0},{3,1},{4,6},{5,7},{6,4},{7,5},{8,10},{9,11},{10,... | collective-permute-start | bytes 393224 | tf_op jit(solution)/shard_map/ppermute | solution.py:602
  (9 other events, 19.1 us)

commit v5 on v4

--- a/solution.py
+++ b/solution.py
@@ -36,14 +36,16 @@
     "edge_grads": 0.3,
     "add_rim_sums": 0.3,
     "pack_grads": 0.3,
+    "coarse_rows": 0.3,
     "far_sum": 30,
     "node_outputs": 2,
-    "grad_node": 30,
+    "grad_node": .1,
     "last_grads": 1.5,
     "coarse_sums": 1,
     "coarse_split": 1,
     "fold0": 0.3,
     "fold1": 0.3,
+    "fold3": 0.3,
     "fold2": 0.3,
 }
 
@@ -402,25 +404,29 @@
     for table, part in zip(tables, parts + [low_ref[...], high_ref[...]]):
         term = lax.dot_general(table[...], part, ROWS, preferred_element_type=F32)
         grad = term if grad is None else grad + term
-    total[:latent] = edge_ref[...]
-    total[latent : 2 * latent] = grad
-    total[2 * latent : 3 * latent] = lax.dot_general(
-        tables[0][...], psum_ref[...], ROWS, preferred_element_type=F32
-    )
-    total[3 * latent :] = out_ref[...]
+    total[:latent] = grad
+    total[latent:] = lax.dot_general(tables[0][...], psum_ref[...], ROWS, preferred_element_type=F32)
     feats, pairs, span, width = keep_ref.shape
     unit = span // 4
-    bit = where_ref[0] & 1
-    for m in range(pairs):
-        for slot in range(4):
-            for ref, which in ((keep_ref, bit), (send_ref, 1 - bit)):
-                patch = 2 * m + which
-                row = (patch * 3 + slot) * unit if slot < 3 else 3 * latent + patch * unit
-                block = total[pl.ds(pl.multiple_of(row, unit), unit), :]
-                for f in range(feats):
-                    ref[f, m, slot * unit : (slot + 1) * unit, :] = block[:, f * width : (f + 1) * width].astype(
-                        ref.dtype
-                    )
+
+    def block(patch, slot):
+        row = (patch * 3 + slot) * unit if slot < 3 else 3 * latent + patch * unit
+        for ref, start, end in ((edge_ref, 0, latent), (total, latent, 3 * latent), (out_ref, 3 * latent, 4 * latent)):
+            if start <= row < end:
+                return ref[row - start : row - start + unit]
+
+    for bit in range(2):
+
+        @pl.when((where_ref[0] & 1) == bit)
+        def _():
+            for m in range(pairs):
+                for slot in range(4):
+                    for ref, which in ((keep_ref, bit), (send_ref, 1 - bit)):
+                        rows_in = block(2 * m + which, slot)
+                        for f in range(feats):
+                            ref[f, m, slot * unit : (slot + 1) * unit, :] = rows_in[
+                                :, f * width : (f + 1) * width
+                            ].astype(ref.dtype)
 
 
 def pack_call(where, psum, edge_grad, out_grad, patch_sum, low, high, tables, feats, patches):
@@ -431,7 +437,7 @@
         lambda *refs: pack_kernel(len(tables), *refs),
         in_specs=[pl.BlockSpec(memory_space=pltpu.SMEM)] + [vmem] * (6 + len(tables)),
         out_shape=[jax.ShapeDtypeStruct(shape, F32), jax.ShapeDtypeStruct(shape, BF16)],
-        scratch_shapes=[pltpu.VMEM((4 * latent, hidden), F32)],
+        scratch_shapes=[pltpu.VMEM((2 * latent, hidden), F32)],
         compiler_params=params(),
         cost_estimate=cost("pack_grads"),
         name="pack_grads",
@@ -478,44 +484,68 @@
     )(a, b)
 
 
-def far_sum_kernel(own_ref, sent_ref, got_ref, far_ref, coarse_ref):
+def coarse_rows_kernel(sent_ref, got_ref, out_ref):
+    few = out_ref.shape[0]
+    out_ref[...] = (sent_ref[-few:].astype(F32) + got_ref[-few:].astype(F32)).astype(BF16)
+
+
+def coarse_rows_call(sent, got, few):
+    return launch(
+        coarse_rows_kernel,
+        out_shape=jax.ShapeDtypeStruct((few, sent.shape[1]), BF16),
+        compiler_params=params(),
+        cost_estimate=cost("coarse_rows"),
+        name="coarse_rows",
+    )(sent, got)
+
+
+def far_sum_kernel(own_ref, got_ref, out_ref):
     size = own_ref.shape[0]
-    far_ref[...] = (own_ref[...].astype(F32) + got_ref[:size].astype(F32)).astype(BF16)
-    coarse_ref[...] = (sent_ref[size:].astype(F32) + got_ref[size:].astype(F32)).astype(BF16)
-
-
-def far_sum_call(own, sent, got):
-    size, width = own.shape
+    out_ref[...] = (own_ref[...].astype(F32) + got_ref[:size].astype(F32)).astype(BF16)
+
+
+def far_sum_call(own, got):
     return launch(
         far_sum_kernel,
-        out_shape=[
-            jax.ShapeDtypeStruct((size, width), BF16),
-            jax.ShapeDtypeStruct((sent.shape[0] - size, width), BF16),
-        ],
+        out_shape=jax.ShapeDtypeStruct(own.shape, BF16),
         compiler_params=params(),
         cost_estimate=cost("far_sum"),
         name="far_sum",
-    )(own, sent, got)
-
-
-def add_split_kernel(axis, shift, where_ref, keep_ref, got_ref, mine_ref, other_ref):
+    )(own, got)
+
+
+def add_split_kernel(axis, shift, count, where_ref, *refs):
+    keeps, gots = refs[:count], refs[count : 2 * count]
+    outs = refs[2 * count :]
+    parts = len(outs) // 2
     bit = (where_ref[axis] >> shift) & 1
-    for ref, which in ((mine_ref, bit), (other_ref, 1 - bit)):
-        for a in range(keep_ref.shape[0]):
-            ref[a] = (keep_ref[a, which] + got_ref[a, which].astype(F32)).astype(ref.dtype)
-
-
-def add_split_call(name, where, axis, distance, keep, got, send_type):
+    for refs_out, which in ((outs[:parts], bit), (outs[parts:], 1 - bit)):
+        piece = refs_out[0].shape[1]
+        for a in range(keeps[0].shape[0]):
+            at = 0
+            for keep, got in zip(keeps, gots):
+                size = min(piece, keep.shape[2])
+                for row in range(0, keep.shape[2], size):
+                    rows_in = slice(row, row + size)
+                    out, first = refs_out[at // piece], at % piece
+                    total = keep[a, which, rows_in] + got[a, which, rows_in].astype(F32)
+                    out[a, first : first + size] = total.astype(out.dtype)
+                    at += size
+
+
+def add_split_call(name, where, axis, distance, keeps, gots, parts, send_type):
     vmem = pl.BlockSpec(memory_space=pltpu.VMEM)
-    shape = keep.shape[:1] + keep.shape[2:]
-    return launch(
-        functools.partial(add_split_kernel, axis, distance.bit_length() - 1),
-        in_specs=[pl.BlockSpec(memory_space=pltpu.SMEM), vmem, vmem],
-        out_shape=[jax.ShapeDtypeStruct(shape, F32), jax.ShapeDtypeStruct(shape, send_type)],
+    total = sum(keep.shape[2] for keep in keeps)
+    shape = keeps[0].shape[:1] + (total // parts,) + keeps[0].shape[3:]
+    outs = launch(
+        functools.partial(add_split_kernel, axis, distance.bit_length() - 1, len(keeps)),
+        in_specs=[pl.BlockSpec(memory_space=pltpu.SMEM)] + [vmem] * (2 * len(keeps)),
+        out_shape=[jax.ShapeDtypeStruct(shape, F32)] * parts + [jax.ShapeDtypeStruct(shape, send_type)] * parts,
         compiler_params=params(),
         cost_estimate=cost(name),
         name=name,
-    )(where, keep, got)
+    )(where, *keeps, *gots)
+    return outs[:parts], outs[parts:]
 
 
 def last_grads_kernel(scale, keep_ref, got_ref, in_ref, out_ref):
@@ -689,7 +719,9 @@
     if whole_step:
         got = xor_swap(coarse_other, "patch", 1)
         halves = (1, 2, coarse.shape[0] // 2, coarse.shape[1])
-        coarse, coarse_other = add_split_call("coarse_split", where, 0, 2, coarse.reshape(halves), got.reshape(halves), F32)
+        (coarse,), (coarse_other,) = add_split_call(
+            "coarse_split", where, 0, 2, [coarse.reshape(halves)], [got.reshape(halves)], 1, F32
+        )
         coarse, coarse_other = coarse[0], coarse_other[0]
         got = xor_swap(coarse_other, "patch", 2)
     else:
@@ -726,36 +758,38 @@
     span, width = 4 * latent // patch_count, latent // feat_count
     steps = [("patch", d) for d in bits_of(patch_count)[1:]] + [("feat", d) for d in bits_of(feat_count)]
 
-    def fold(step, keep, received):
+    def fold(name, step, keeps, gots, parts):
         axis, distance = steps[step]
-        shape = (-1, 2, span, width)
-        keep, send = add_split_call(
-            f"fold{min(step, 2)}",
+        shape = lambda x: (-1, 2) + x.shape[-2:]
+        keeps, sends = add_split_call(
+            name,
             where,
             int(axis == "feat"),
             distance,
-            keep.reshape(shape),
-            received.reshape(shape),
+            [x.reshape(shape(x)) for x in keeps],
+            [x.reshape(shape(x)) for x in gots],
+            parts,
             BF16,
         )
-        return keep, xor_swap(send, axis, distance)
-
-    edge_grad, out_grad = edge_grads_call(flat_edges, grad_pre, hidden_act, grad_proj)
+        return keeps, [xor_swap(x, axis, distance) for x in sends]
+
+    def fold_half(name, keep, got):
+        for step in range(1, len(steps) - 1):
+            (keep,), (got,) = fold(name, step, [keep], [got], 1)
+        return keep, got
+
     sums = add_rim_call(
         send_row, back_lower, back_upper, patch_sum, coarse, node_count, whole_step
     )
+    edge_grad, out_grad = edge_grads_call(flat_edges, grad_pre, hidden_act, grad_proj)
     tables = pieces + [from_lower, from_upper]
     keep, send = pack_call(
         where, pre_sum, edge_grad, out_grad, patch_sum, rim_low, rim_high, tables, feat_count, patch_count
     )
     got_core = xor_swap(send, "patch", 1)
-    keep, received = fold(0, keep, got_core)
     if feat_count == 4:
         relay = xor_swap(sums[3], "feat", 1)
-        if whole_step:
-            far_sum, coarse_all = far_sum_call(sums[2], sums[3], relay)
-        else:
-            far_sum = add_pair_call(sums[2], relay)
+        far_sum = far_sum_call(sums[2], relay)
         got_far = xor_swap(far_sum, "feat", 2)
         got_near = xor_swap(sums[1], "feat", 1)
         own = [sums[0], got_far, got_near]
@@ -765,19 +799,20 @@
             arrived = [xor_swap(part, "feat", distance) for part in parts[distance:]]
             parts = [add_pair_call(a, b) for a, b in zip(parts[:distance], arrived)]
         own = [parts[0], jnp.zeros_like(parts[0]), jnp.zeros_like(parts[0])]
-    keep, received = fold(1, keep, received)
-    back = node_back_call(*own, pre_sum, weight_in)
-    keep, received = fold(2, keep, received)
+    (keep_a, keep_b), (got_a, got_b) = fold("fold0", 0, [keep], [got_core], 2)
+    keep_a, got_a = fold_half("fold1", keep_a, got_a)
+    keep_b, got_b = fold_half("fold3", keep_b, got_b)
     if whole_step:
+        coarse_all = coarse_rows_call(sums[3], relay, 3 * coarse.shape[0])
         parts = [coarse_all] + [xor_swap(coarse_all, "patch", j) for j in range(1, 4)]
     else:
         counts = jnp.pad(coarse[:, 2 * latent :], ((0, 0), (128, latent - 256)))
         parts = [jnp.concatenate([coarse[:, :latent], coarse[:, latent : 2 * latent], counts], axis=0)]
+    back = node_back_call(*own, pre_sum, weight_in)
+    (keep,), (received,) = fold("fold2", len(steps) - 1, [keep_a, keep_b], [got_a, got_b], 1)
     node_new, grad_node = node_call(
         where, coarse_row, node_lat, node_cotangent, aggregate, back, parts
     )
-    for step in range(3, len(steps)):
-        keep, received = fold(step, keep, received)
     scale = 1.0 / math.sqrt(edge_count * patch_count * feat_count)
     in_rows = 3 * latent // patch_count
     grads_in, grads_out = last_grads_call(scale, keep.reshape(span, width), received.reshape(span, width), in_rows)

time: 93.7 us -> 91.4 us (0.975)
  waiting for transfers between devices: 28.6 us -> 21.4 us
  starting transfers between devices: 26.5 us -> 31.1 us
    ppermute x16 -> x18, waiting for transfers between devices: 28.6 us -> 21.2 us  [xor_swap(): return lax.ppermute(value, axis, [(i, i ^ distance) for i in range(size)])]
    ppermute x16 -> x18, starting transfers between devices: 22.9 us -> 27.6 us  [xor_swap(): return lax.ppermute(value, axis, [(i, i ^ distance) for i in range(size)])]
    pallas_call x18 -> x20, Pallas kernels: 34 us -> 34.2 us  [call(): pl.pallas_call(body, out_shape=outs + [mark], in_specs=specs, out_specs=p...]
  transfers between devices with their start and end apart: 20 -> 22, of which waited for: 10 -> 11; matrix products, arithmetic and copies ran while one was open for 1% -> 1% of each run, Pallas kernels for 32% -> 34%
where the time goes in v5:
time: 91.4 us; the launch traced here: 91.1 us
  Pallas kernels  34.2 us (37%)
  starting transfers between devices  31.1 us (34%)
  waiting for transfers between devices  21.4 us (23%)
  local copies, waits for them, and re-layouts  3.3 us (4%)
  between operations  0.92 us (1%)
    pallas_call x20, Pallas kernels, call(): pl.pallas_call(body, out_shape=outs + [mark], in_specs=specs, out_specs=p...  34.2 us
    ppermute x18, starting transfers between devices, xor_swap(): return lax.ppermute(value, axis, [(i, i ^ distance) for i in range(size)])  27.6 us
    ppermute x18, waiting for transfers between devices, xor_swap(): return lax.ppermute(value, axis, [(i, i ^ distance) for i in range(size)])  21.2 us
    unnamed x26, local copies, waits for them, and re-layouts  2.61 us
  transfers between devices with their start and end apart: 22, of which 11 were waited for; matrix products, arithmetic and copies ran while one was open for 1% of the time, Pallas kernels for 34%

profile of v5, /device:TPU:0, one launch (start us, length us, event | category | flops | bytes accessed | tf_op | source)
XLA Modules:
  0.0 91.1 jit_solution(1926118175553115001)
XLA Ops:
  0.6 4.1 %collective-permute-start.1 = (bf16[256,512]{1,0:T(8,128)(2,1)}, bf16[256,512]{1,0:T(8,128)(2,1)S(1)}, u32[]{:S(2)}, u32[]{:S(2)}) collective-permute-start(bf16[256,512]{1,0:T(8,128)(2,1)} %refs_2_.3), channel_id=1, source_target_pairs={{0,2},{1,3},{2,0},{3,1},{4,6},{5,7},{6,4},{7,5},{8,10},{9,11},{10,... | collective-permute-start | bytes 786440 | tf_op jit(solution)/shard_map/ppermute | solution.py:632
  4.7 1.6 %collective-permute-start = (bf16[256,512]{1,0:T(8,128)(2,1)}, bf16[256,512]{1,0:T(8,128)(2,1)S(1)}, u32[]{:S(2)}, u32[]{:S(2)}) collective-permute-start(bf16[256,512]{1,0:T(8,128)(2,1)} %refs_2_.3), channel_id=1, source_target_pairs={{0,1},{1,0},{2,3},{3,2},{4,5},{5,4},{6,7},{7,6},{8,9},{9,8},{10,11... | collective-permute-start | bytes 786440 | tf_op jit(solution)/shard_map/ppermute | solution.py:632
  11.8 1.6 %collective-permute-start.6 = (f32[16,1152]{1,0:T(8,128)S(1)}, f32[16,1152]{1,0:T(8,128)S(1)}, u32[]{:S(2)}, u32[]{:S(2)}) collective-permute-start(f32[16,1152]{1,0:T(8,128)S(1)} %bitcast.41), channel_id=1, source_target_pairs={{0,8},{4,12},{8,0},{12,4},{1,9},{5,13},{9,1},{13,5},{2,10},{6,14},... | collective-permute-start | bytes 221192 | tf_op jit(solution)/shard_map/ppermute | solution.py:632
  13.4 3.6 %collective-permute-done.1.refs_11_.refs_3_.refs_9_ = bf16[256,512]{1,0:T(8,128)(2,1)S(1)} collective-permute-done((bf16[256,512]{1,0:T(8,128)(2,1)}, bf16[256,512]{1,0:T(8,128)(2,1)S(1)}, u32[]{:S(2)}, u32[]{:S(2)}) %collective-permute-start.1) | collective-permute-done | bytes 262176 | tf_op jit(solution)/shard_map/ppermute | solution.py:632
  17.7 5.9 %base_terms.1 = (f32[2048,512]{1,0:T(8,128)S(1)}, f32[8,128]{1,0:T(8,128)S(1)}) custom-call(bf16[2048,512]{1,0:T(8,128)(2,1)} %bitcast.27, bf16[256,512]{1,0:T(8,128)(2,1)S(1)} %copy-done.3, s32[2048,1]{1,0:T(8,128)S(1)} %broadcast_in_dim_reshape.8.refs_2_.refs_1_, bf16[1536,512]{1,0:T(8,128)(2,1)S(1)} %copy-done.1, f32[1,512]{1,0:T(1,128)S(1)} %bitcast.42, ...), custom_call_target="tpu_custom_call" | custom-call | flops 17250000896 | bytes 1048576 | tf_op jit(solution)/shard_map/base_terms/pallas_call | solution.py:82
  25.0 1.7 %collective-permute-start.5 = (bf16[128,512]{1,0:T(8,128)(2,1)S(1)}, bf16[128,512]{1,0:T(8,128)(2,1)S(1)}, u32[]{:S(2)}, u32[]{:S(2)}) collective-permute-start(bf16[128,512]{1,0:T(8,128)(2,1)S(1)} %get-tuple-element.76), channel_id=1, source_target_pairs={{4,0},{8,4},{12,8},{0,12},{5,1},{9,5},{13,9},{1,13},{6,2},{10,6},{... | collective-permute-start | bytes 393224 | tf_op jit(solution)/shard_map/ppermute | solution.py:735
  26.7 3.1 %collective-permute-start.7 = (f32[16,1152]{1,0:T(8,128)S(1)}, f32[16,1152]{1,0:T(8,128)S(1)}, u32[]{:S(2)}, u32[]{:S(2)}) collective-permute-start(f32[16,1152]{1,0:T(8,128)S(1)} %get-tuple-element.84.refs_2_), channel_id=1, source_target_pairs={{0,2},{1,3},{2,0},{3,1},{4,6},{5,7},{6,4},{7,5},{8,10},{9,11},{10,... | collective-permute-start | bytes 221192 | tf_op jit(solution)/shard_map/ppermute | solution.py:632
  29.9 12.3 %edge_block.1 = (bf16[2048,512]{1,0:T(8,128)(2,1)}, f32[256,512]{1,0:T(8,128)S(1)}, bf16[2048,512]{1,0:T(8,128)(2,1)S(1)}, bf16[2048,512]{1,0:T(8,128)(2,1)S(1)}...) custom-call(f32[2048,512]{1,0:T(8,128)S(1)} %get-tuple-element.73.re, ...), custom_call_target="tpu_custom_call" | custom-call | flops 41400000512 | bytes 1048576 | tf_op jit(solution)/shard_map/edge_block/pallas_call | solution.py:82
  44.7 2.8 %patch_sums.1 = (f32[1024,512]{1,0:T(8,128)S(1)}, f32[8,128]{1,0:T(8,128)S(1)}) custom-call(s32[1,2048]{1,0:T(1,128)S(1)} %broadcast_in_dim_reshape.7.refs_5_.refs_0_, bf16[2048,512]{1,0:T(8,128)(2,1)S(1)} %get-tuple-element.83.refs_1_, f32[8,128]{1,0:T(8,128)S(1)} %get-tuple-element.88.refs_2_), custom_call_target="tpu_custom_call" | custom-call | flops 345000000 | bytes 1048576 | tf_op jit(solution)/shard_map/patch_sums/pallas_call | solution.py:82
  48.4 1.8 %collective-permute-start.10 = (bf16[304,512]{1,0:T(8,128)(2,1)S(1)}, bf16[304,512]{1,0:T(8,128)(2,1)S(1)}, u32[]{:S(2)}, u32[]{:S(2)}) collective-permute-start(bf16[304,512]{1,0:T(8,128)(2,1)S(1)} %get-tuple-element.94.refs_0_), channel_id=1, source_target_pairs={{0,1},{1,0},{2,3},{3,2},{4,5},{5,4},{6,7},{7,6},{8,9},{9,8},{10,11... | collective-permute-start | bytes 933896 | tf_op jit(solution)/shard_map/ppermute | solution.py:632
  50.2 2.3 %edge_grads.1 = (f32[512,512]{1,0:T(8,128)S(1)}, f32[512,512]{1,0:T(8,128)S(1)}, f32[8,128]{1,0:T(8,128)S(1)}) custom-call(bf16[2048,512]{1,0:T(8,128)(2,1)S(1)} %bitcast.29, bf16[2048,512]{1,0:T(8,128)(2,1)S(1)} %get-tuple-element.83.refs_1_, bf16[2048,512]{1,0:T(8,128)(2,1)S(1)} %get-tuple-element.96.refs_2_, ...), custom_call_target="tpu_custom_call" | custom-call | flops 345000000 | bytes 1048576 | tf_op jit(solution)/shard_map/edge_grads/pallas_call | solution.py:82
  52.6 1.9 %pack_grads.1 = (f32[4,2,512,128]{3,2,1,0:T(8,128)S(1)}, bf16[4,2,512,128]{3,2,1,0:T(8,128)(2,1)S(1)}, f32[8,128]{1,0:T(8,128)S(1)}) custom-call(s32[2]{0:T(128)S(1)} %pad_add_fusion.refs_3_.refs_0_, bf16[256,512]{1,0:T(8,128)(2,1)S(1)} %get-tuple-element.95.refs_1_.refs_3_, f32[512,512]{1,0:T(8,128)S(1)} %get-tuple-element.99.refs_2_, ...), custom_call_target="tpu_custom_call" | custom-call | flops 345000000 | bytes 1048576 | tf_op jit(solution)/shard_map/pack_grads/pallas_call | solution.py:82
  55.5 3.0 %collective-permute-done.10.refs_1_ = bf16[304,512]{1,0:T(8,128)(2,1)S(1)} collective-permute-done((bf16[304,512]{1,0:T(8,128)(2,1)S(1)}, bf16[304,512]{1,0:T(8,128)(2,1)S(1)}, u32[]{:S(2)}, u32[]{:S(2)}) %collective-permute-start.10) | collective-permute-done | bytes 311328 | tf_op jit(solution)/shard_map/ppermute | solution.py:632
  59.3 1.6 %collective-permute-start.15 = (bf16[4,256,128]{2,1,0:T(8,128)(2,1)S(1)}, bf16[4,256,128]{2,1,0:T(8,128)(2,1)S(1)}, u32[]{:S(2)}, u32[]{:S(2)}) collective-permute-start(bf16[4,256,128]{2,1,0:T(8,128)(2,1)S(1)} %get-tuple-element.111), channel_id=1, source_target_pairs={{0,8},{4,12},{8,0},{12,4},{1,9},{5,13},{9,1},{13,5},{2,10},{6,14},... | collective-permute-start | bytes 786440 | tf_op jit(solution)/shard_map/ppermute | solution.py:632
  61.4 1.7 %collective-permute-start.12 = (bf16[256,512]{1,0:T(8,128)(2,1)S(1)}, bf16[256,512]{1,0:T(8,128)(2,1)S(1)}, u32[]{:S(2)}, u32[]{:S(2)}) collective-permute-start(bf16[256,512]{1,0:T(8,128)(2,1)S(1)} %get-tuple-element.104), channel_id=1, source_target_pairs={{0,1},{1,0},{2,3},{3,2},{4,5},{5,4},{6,7},{7,6},{8,9},{9,8},{10,11... | collective-permute-start | bytes 786440 | tf_op jit(solution)/shard_map/ppermute | solution.py:632
  63.2 3.2 %collective-permute-start.11 = (bf16[256,512]{1,0:T(8,128)(2,1)S(1)}, bf16[256,512]{1,0:T(8,128)(2,1)S(1)}, u32[]{:S(2)}, u32[]{:S(2)}) collective-permute-start(bf16[256,512]{1,0:T(8,128)(2,1)S(1)} %get-tuple-element.103), channel_id=1, source_target_pairs={{0,2},{1,3},{2,0},{3,1},{4,6},{5,7},{6,4},{7,5},{8,10},{9,11},{10,... | collective-permute-start | bytes 786440 | tf_op jit(solution)/shard_map/ppermute | solution.py:632
  66.3 2.2 %collective-permute-done.15 = bf16[4,256,128]{2,1,0:T(8,128)(2,1)S(1)} collective-permute-done((bf16[4,256,128]{2,1,0:T(8,128)(2,1)S(1)}, bf16[4,256,128]{2,1,0:T(8,128)(2,1)S(1)}, u32[]{:S(2)}, u32[]{:S(2)}) %collective-permute-start.15) | collective-permute-done | bytes 262176 | tf_op jit(solution)/shard_map/ppermute | solution.py:632
  69.2 4.2 %collective-permute-done.14 = bf16[4,256,128]{2,1,0:T(8,128)(2,1)S(1)} collective-permute-done((bf16[4,256,128]{2,1,0:T(8,128)(2,1)S(1)}, bf16[4,256,128]{2,1,0:T(8,128)(2,1)S(1)}, u32[]{:S(2)}, u32[]{:S(2)}) %collective-permute-start.14) | collective-permute-done | bytes 262176 | tf_op jit(solution)/shard_map/ppermute | solution.py:632
  73.9 1.8 %collective-permute-start.20 = (bf16[2,256,128]{2,1,0:T(8,128)(2,1)S(1)}, bf16[2,256,128]{2,1,0:T(8,128)(2,1)S(1)}, u32[]{:S(2)}, u32[]{:S(2)}) collective-permute-start(bf16[2,256,128]{2,1,0:T(8,128)(2,1)S(1)} %get-tuple-element.121), channel_id=1, source_target_pairs={{0,1},{1,0},{2,3},{3,2},{4,5},{5,4},{6,7},{7,6},{8,9},{9,8},{10,11... | collective-permute-start | bytes 393224 | tf_op jit(solution)/shard_map/ppermute | solution.py:632
  78.5 1.9 %collective-permute-done.20 = bf16[2,256,128]{2,1,0:T(8,128)(2,1)S(1)} collective-permute-done((bf16[2,256,128]{2,1,0:T(8,128)(2,1)S(1)}, bf16[2,256,128]{2,1,0:T(8,128)(2,1)S(1)}, u32[]{:S(2)}, u32[]{:S(2)}) %collective-permute-start.20) | collective-permute-done | bytes 131104 | tf_op jit(solution)/shard_map/ppermute | solution.py:632
  80.4 1.4 %collective-permute-done.19 = bf16[2,256,128]{2,1,0:T(8,128)(2,1)S(1)} collective-permute-done((bf16[2,256,128]{2,1,0:T(8,128)(2,1)S(1)}, bf16[2,256,128]{2,1,0:T(8,128)(2,1)S(1)}, u32[]{:S(2)}, u32[]{:S(2)}) %collective-permute-start.19) | collective-permute-done | bytes 131104 | tf_op jit(solution)/shard_map/ppermute | solution.py:632
  82.4 3.0 %collective-permute-start.21 = (bf16[1,512,128]{2,1,0:T(8,128)(2,1)S(1)}, bf16[1,512,128]{2,1,0:T(8,128)(2,1)S(1)}, u32[]{:S(2)}, u32[]{:S(2)}) collective-permute-start(bf16[1,512,128]{2,1,0:T(8,128)(2,1)S(1)} %get-tuple-element.128), channel_id=1, source_target_pairs={{0,2},{1,3},{2,0},{3,1},{4,6},{5,7},{6,4},{7,5},{8,10},{9,11},{10,... | collective-permute-start | bytes 393224 | tf_op jit(solution)/shard_map/ppermute | solution.py:632
  85.4 1.8 %node_outputs.1 = (bf16[256,512]{1,0:T(8,128)(2,1)}, bf16[256,512]{1,0:T(8,128)(2,1)}, f32[8,128]{1,0:T(8,128)S(1)}) custom-call(s32[2]{0:T(128)S(1)} %pad_add_fusion.refs_3_.refs_0_, s32[1,256]{1,0:T(1,128)S(1)} %bitcast.46, bf16[256,512]{1,0:T(8,128)(2,1)S(1)} %copy-done.3, bf16[256,512]{1,0:T(8,128)(2,1)S(1)} %copy-done.6, ...), custom_call_target="tpu_custom_call" | custom-call | flops 2300000000 | bytes 1048576 | tf_op jit(solution)/shard_map/node_outputs/pallas_call | solution.py:82
  87.2 3.1 %collective-permute-done.21 = bf16[1,512,128]{2,1,0:T(8,128)(2,1)S(1)} collective-permute-done((bf16[1,512,128]{2,1,0:T(8,128)(2,1)S(1)}, bf16[1,512,128]{2,1,0:T(8,128)(2,1)S(1)}, u32[]{:S(2)}, u32[]{:S(2)}) %collective-permute-start.21) | collective-permute-done | bytes 131104 | tf_op jit(solution)/shard_map/ppermute | solution.py:632
  (73 shorter events, 18.4 us)
Async XLA Ops:
  0.6 16.3 %collective-permute-start.1 = (bf16[256,512]{1,0:T(8,128)(2,1)}, bf16[256,512]{1,0:T(8,128)(2,1)S(1)}, u32[]{:S(2)}, u32[]{:S(2)}) collective-permute-start(bf16[256,512]{1,0:T(8,128)(2,1)} %refs_2_.3), channel_id=1, source_target_pairs={{0,2},{1,3},{2,0},{3,1},{4,6},{5,7},{6,4},{7,5},{8,10},{9,11},{10,... | collective-permute-start | bytes 786440 | tf_op jit(solution)/shard_map/ppermute | solution.py:632
  4.7 13.0 %collective-permute-start = (bf16[256,512]{1,0:T(8,128)(2,1)}, bf16[256,512]{1,0:T(8,128)(2,1)S(1)}, u32[]{:S(2)}, u32[]{:S(2)}) collective-permute-start(bf16[256,512]{1,0:T(8,128)(2,1)} %refs_2_.3), channel_id=1, source_target_pairs={{0,1},{1,0},{2,3},{3,2},{4,5},{5,4},{6,7},{7,6},{8,9},{9,8},{10,11... | collective-permute-start | bytes 786440 | tf_op jit(solution)/shard_map/ppermute | solution.py:632
  9.8 1.4 %collective-permute-start.2 = (f32[32,1152]{1,0:T(8,128)S(1)}, f32[32,1152]{1,0:T(8,128)S(1)}, u32[]{:S(2)}, u32[]{:S(2)}) collective-permute-start(f32[32,1152]{1,0:T(8,128)S(1)} %get-tuple-element.70), channel_id=1, source_target_pairs={{0,4},{4,0},{8,12},{12,8},{1,5},{5,1},{9,13},{13,9},{2,6},{6,2},{1... | collective-permute-start | bytes 442376 | tf_op jit(solution)/shard_map/ppermute | solution.py:632
  11.2 6.5 %copy-start.7 = (f32[512]{0:T(512)S(1)}, f32[512]{0:T(512)}, u32[]{:S(2)}) copy-start(f32[512]{0:T(512)} %param.17) | copy-start | bytes 6148
  11.2 6.5 %copy-start.10 = (s32[256]{0:T(256)S(1)}, s32[256]{0:T(256)}, u32[]{:S(2)}) copy-start(s32[256]{0:T(256)} %param.15) | copy-start | bytes 3076
  11.8 14.9 %collective-permute-start.6 = (f32[16,1152]{1,0:T(8,128)S(1)}, f32[16,1152]{1,0:T(8,128)S(1)}, u32[]{:S(2)}, u32[]{:S(2)}) collective-permute-start(f32[16,1152]{1,0:T(8,128)S(1)} %bitcast.41), channel_id=1, source_target_pairs={{0,8},{4,12},{8,0},{12,4},{1,9},{5,13},{9,1},{13,5},{2,10},{6,14},... | collective-permute-start | bytes 221192 | tf_op jit(solution)/shard_map/ppermute | solution.py:632
  17.0 7.4 %collective-permute-start.3 = (bf16[256,512]{1,0:T(8,128)(2,1)S(1)}, bf16[256,512]{1,0:T(8,128)(2,1)S(1)}, u32[]{:S(2)}, u32[]{:S(2)}) collective-permute-start(bf16[256,512]{1,0:T(8,128)(2,1)S(1)} %collective-permute-done.1.refs_11_.refs_3_.refs_9_), channel_id=1, source_target_pairs={{0,1},{1,0},{2,3},{3,2},{4,5},{5,4},{6,7},{7,6},{8,9},{9,8},{10,11... | collective-permute-start | bytes 786440 | tf_op jit(solution)/shard_map/ppermute | solution.py:632
  24.9 4.9 %collective-permute-start.4 = (bf16[128,512]{1,0:T(8,128)(2,1)S(1)}, bf16[128,512]{1,0:T(8,128)(2,1)S(1)}, u32[]{:S(2)}, u32[]{:S(2)}) collective-permute-start(bf16[128,512]{1,0:T(8,128)(2,1)S(1)} %get-tuple-element.75), channel_id=1, source_target_pairs={{0,4},{4,8},{8,12},{12,0},{1,5},{5,9},{9,13},{13,1},{2,6},{6,10},{... | collective-permute-start | bytes 393224 | tf_op jit(solution)/shard_map/ppermute | solution.py:734
  25.0 4.9 %collective-permute-start.5 = (bf16[128,512]{1,0:T(8,128)(2,1)S(1)}, bf16[128,512]{1,0:T(8,128)(2,1)S(1)}, u32[]{:S(2)}, u32[]{:S(2)}) collective-permute-start(bf16[128,512]{1,0:T(8,128)(2,1)S(1)} %get-tuple-element.76), channel_id=1, source_target_pairs={{4,0},{8,4},{12,8},{0,12},{5,1},{9,5},{13,9},{1,13},{6,2},{10,6},{... | collective-permute-start | bytes 393224 | tf_op jit(solution)/shard_map/ppermute | solution.py:735
  26.7 15.4 %collective-permute-start.7 = (f32[16,1152]{1,0:T(8,128)S(1)}, f32[16,1152]{1,0:T(8,128)S(1)}, u32[]{:S(2)}, u32[]{:S(2)}) collective-permute-start(f32[16,1152]{1,0:T(8,128)S(1)} %get-tuple-element.84.refs_2_), channel_id=1, source_target_pairs={{0,2},{1,3},{2,0},{3,1},{4,6},{5,7},{6,4},{7,5},{8,10},{9,11},{10,... | collective-permute-start | bytes 221192 | tf_op jit(solution)/shard_map/ppermute | solution.py:632
  42.9 4.6 %collective-permute-start.8 = (bf16[128,512]{1,0:T(8,128)(2,1)S(1)}, bf16[128,512]{1,0:T(8,128)(2,1)S(1)}, u32[]{:S(2)}, u32[]{:S(2)}) collective-permute-start(bf16[128,512]{1,0:T(8,128)(2,1)S(1)} %get-tuple-element.86.refs_6_), channel_id=1, source_target_pairs={{0,4},{4,8},{8,12},{12,0},{1,5},{5,9},{9,13},{13,1},{2,6},{6,10},{... | collective-permute-start | bytes 393224 | tf_op jit(solution)/shard_map/ppermute | solution.py:756
  43.8 4.0 %collective-permute-start.9 = (bf16[128,512]{1,0:T(8,128)(2,1)S(1)}, bf16[128,512]{1,0:T(8,128)(2,1)S(1)}, u32[]{:S(2)}, u32[]{:S(2)}) collective-permute-start(bf16[128,512]{1,0:T(8,128)(2,1)S(1)} %get-tuple-element.87.refs_5_), channel_id=1, source_target_pairs={{4,0},{8,4},{12,8},{0,12},{5,1},{9,5},{13,9},{1,13},{6,2},{10,6},{... | collective-permute-start | bytes 393224 | tf_op jit(solution)/shard_map/ppermute | solution.py:755
  48.4 10.1 %collective-permute-start.10 = (bf16[304,512]{1,0:T(8,128)(2,1)S(1)}, bf16[304,512]{1,0:T(8,128)(2,1)S(1)}, u32[]{:S(2)}, u32[]{:S(2)}) collective-permute-start(bf16[304,512]{1,0:T(8,128)(2,1)S(1)} %get-tuple-element.94.refs_0_), channel_id=1, source_target_pairs={{0,1},{1,0},{2,3},{3,2},{4,5},{5,4},{6,7},{7,6},{8,9},{9,8},{10,11... | collective-permute-start | bytes 933896 | tf_op jit(solution)/shard_map/ppermute | solution.py:632
  54.5 4.1 %collective-permute-start.13 = (bf16[4,2,512,128]{3,2,1,0:T(8,128)(2,1)S(1)}, bf16[4,2,512,128]{3,2,1,0:T(8,128)(2,1)S(1)}, u32[]{:S(2)}, u32[]{:S(2)}) collective-permute-start(bf16[4,2,512,128]{3,2,1,0:T(8,128)(2,1)S(1)} %get-tuple-element.106), channel_id=1, source_target_pairs={{0,4},{4,0},{8,12},{12,8},{1,5},{5,1},{9,13},{13,9},{2,6},{6,2},{1... | collective-permute-start | bytes 3145736 | tf_op jit(solution)/shard_map/ppermute | solution.py:632
  59.3 9.2 %collective-permute-start.15 = (bf16[4,256,128]{2,1,0:T(8,128)(2,1)S(1)}, bf16[4,256,128]{2,1,0:T(8,128)(2,1)S(1)}, u32[]{:S(2)}, u32[]{:S(2)}) collective-permute-start(bf16[4,256,128]{2,1,0:T(8,128)(2,1)S(1)} %get-tuple-element.111), channel_id=1, source_target_pairs={{0,8},{4,12},{8,0},{12,4},{1,9},{5,13},{9,1},{13,5},{2,10},{6,14},... | collective-permute-start | bytes 786440 | tf_op jit(solution)/shard_map/ppermute | solution.py:632
  61.0 12.4 %collective-permute-start.14 = (bf16[4,256,128]{2,1,0:T(8,128)(2,1)S(1)}, bf16[4,256,128]{2,1,0:T(8,128)(2,1)S(1)}, u32[]{:S(2)}, u32[]{:S(2)}) collective-permute-start(bf16[4,256,128]{2,1,0:T(8,128)(2,1)S(1)} %get-tuple-element.109), channel_id=1, source_target_pairs={{0,8},{4,12},{8,0},{12,4},{1,9},{5,13},{9,1},{13,5},{2,10},{6,14},... | collective-permute-start | bytes 786440 | tf_op jit(solution)/shard_map/ppermute | solution.py:632
  61.4 14.7 %collective-permute-start.12 = (bf16[256,512]{1,0:T(8,128)(2,1)S(1)}, bf16[256,512]{1,0:T(8,128)(2,1)S(1)}, u32[]{:S(2)}, u32[]{:S(2)}) collective-permute-start(bf16[256,512]{1,0:T(8,128)(2,1)S(1)} %get-tuple-element.104), channel_id=1, source_target_pairs={{0,1},{1,0},{2,3},{3,2},{4,5},{5,4},{6,7},{7,6},{8,9},{9,8},{10,11... | collective-permute-start | bytes 786440 | tf_op jit(solution)/shard_map/ppermute | solution.py:632
  63.2 14.7 %collective-permute-start.11 = (bf16[256,512]{1,0:T(8,128)(2,1)S(1)}, bf16[256,512]{1,0:T(8,128)(2,1)S(1)}, u32[]{:S(2)}, u32[]{:S(2)}) collective-permute-start(bf16[256,512]{1,0:T(8,128)(2,1)S(1)} %get-tuple-element.103), channel_id=1, source_target_pairs={{0,2},{1,3},{2,0},{3,1},{4,6},{5,7},{6,4},{7,5},{8,10},{9,11},{10,... | collective-permute-start | bytes 786440 | tf_op jit(solution)/shard_map/ppermute | solution.py:632
  73.9 6.4 %collective-permute-start.20 = (bf16[2,256,128]{2,1,0:T(8,128)(2,1)S(1)}, bf16[2,256,128]{2,1,0:T(8,128)(2,1)S(1)}, u32[]{:S(2)}, u32[]{:S(2)}) collective-permute-start(bf16[2,256,128]{2,1,0:T(8,128)(2,1)S(1)} %get-tuple-element.121), channel_id=1, source_target_pairs={{0,1},{1,0},{2,3},{3,2},{4,5},{5,4},{6,7},{7,6},{8,9},{9,8},{10,11... | collective-permute-start | bytes 393224 | tf_op jit(solution)/shard_map/ppermute | solution.py:632
  75.7 6.0 %collective-permute-start.19 = (bf16[2,256,128]{2,1,0:T(8,128)(2,1)S(1)}, bf16[2,256,128]{2,1,0:T(8,128)(2,1)S(1)}, u32[]{:S(2)}, u32[]{:S(2)}) collective-permute-start(bf16[2,256,128]{2,1,0:T(8,128)(2,1)S(1)} %get-tuple-element.120), channel_id=1, source_target_pairs={{0,1},{1,0},{2,3},{3,2},{4,5},{5,4},{6,7},{7,6},{8,9},{9,8},{10,11... | collective-permute-start | bytes 393224 | tf_op jit(solution)/shard_map/ppermute | solution.py:632
  76.1 9.3 %collective-permute-start.18 = (bf16[48,512]{1,0:T(8,128)(2,1)S(1)}, bf16[48,512]{1,0:T(8,128)(2,1)S(1)}, u32[]{:S(2)}, u32[]{:S(2)}) collective-permute-start(bf16[48,512]{1,0:T(8,128)(2,1)S(1)} %get-tuple-element.117.refs_6_), channel_id=1, source_target_pairs={{0,12},{4,8},{8,4},{12,0},{1,13},{5,9},{9,5},{13,1},{2,14},{6,10},... | collective-permute-start | bytes 147464 | tf_op jit(solution)/shard_map/ppermute | solution.py:632
  76.1 9.2 %collective-permute-start.17 = (bf16[48,512]{1,0:T(8,128)(2,1)S(1)}, bf16[48,512]{1,0:T(8,128)(2,1)S(1)}, u32[]{:S(2)}, u32[]{:S(2)}) collective-permute-start(bf16[48,512]{1,0:T(8,128)(2,1)S(1)} %get-tuple-element.117.refs_6_), channel_id=1, source_target_pairs={{0,8},{4,12},{8,0},{12,4},{1,9},{5,13},{9,1},{13,5},{2,10},{6,14},... | collective-permute-start | bytes 147464 | tf_op jit(solution)/shard_map/ppermute | solution.py:632
  77.8 7.6 %collective-permute-start.16 = (bf16[48,512]{1,0:T(8,128)(2,1)S(1)}, bf16[48,512]{1,0:T(8,128)(2,1)S(1)}, u32[]{:S(2)}, u32[]{:S(2)}) collective-permute-start(bf16[48,512]{1,0:T(8,128)(2,1)S(1)} %get-tuple-element.117.refs_6_), channel_id=1, source_target_pairs={{0,4},{4,0},{8,12},{12,8},{1,5},{5,1},{9,13},{13,9},{2,6},{6,2},{1... | collective-permute-start | bytes 147464 | tf_op jit(solution)/shard_map/ppermute | solution.py:632
  82.4 8.0 %collective-permute-start.21 = (bf16[1,512,128]{2,1,0:T(8,128)(2,1)S(1)}, bf16[1,512,128]{2,1,0:T(8,128)(2,1)S(1)}, u32[]{:S(2)}, u32[]{:S(2)}) collective-permute-start(bf16[1,512,128]{2,1,0:T(8,128)(2,1)S(1)} %get-tuple-element.128), channel_id=1, source_target_pairs={{0,2},{1,3},{2,0},{3,1},{4,6},{5,7},{6,4},{7,5},{8,10},{9,11},{10,... | collective-permute-start | bytes 393224 | tf_op jit(solution)/shard_map/ppermute | solution.py:632
  (11 other events, 33.0 us)

commit v6 on v5

--- a/solution.py
+++ b/solution.py
@@ -754,7 +754,7 @@
     rim_low, rim_high, coarse = rim_sum_call(ids_row, grad_pre, coarse, got, patch_total, 2 * rim_rows)
     back_upper = lax.ppermute(rim_low, "patch", ring_down)
     back_lower = lax.ppermute(rim_high, "patch", ring_up)
-    patch_sum = patch_sum_call(ids_row, grad_pre, patch_total, node_count)
+    patch_sum = patch_sum_call(ids_row, grad_pre, patch_total, 2 * node_count)
     span, width = 4 * latent // patch_count, latent // feat_count
     steps = [("patch", d) for d in bits_of(patch_count)[1:]] + [("feat", d) for d in bits_of(feat_count)]
 
@@ -799,9 +799,8 @@
             arrived = [xor_swap(part, "feat", distance) for part in parts[distance:]]
             parts = [add_pair_call(a, b) for a, b in zip(parts[:distance], arrived)]
         own = [parts[0], jnp.zeros_like(parts[0]), jnp.zeros_like(parts[0])]
-    (keep_a, keep_b), (got_a, got_b) = fold("fold0", 0, [keep], [got_core], 2)
+    (keep_a,), (got_a,) = fold("fold0", 0, [keep], [got_core], 1)
     keep_a, got_a = fold_half("fold1", keep_a, got_a)
-    keep_b, got_b = fold_half("fold3", keep_b, got_b)
     if whole_step:
         coarse_all = coarse_rows_call(sums[3], relay, 3 * coarse.shape[0])
         parts = [coarse_all] + [xor_swap(coarse_all, "patch", j) for j in range(1, 4)]
@@ -809,7 +808,7 @@
         counts = jnp.pad(coarse[:, 2 * latent :], ((0, 0), (128, latent - 256)))
         parts = [jnp.concatenate([coarse[:, :latent], coarse[:, latent : 2 * latent], counts], axis=0)]
     back = node_back_call(*own, pre_sum, weight_in)
-    (keep,), (received,) = fold("fold2", len(steps) - 1, [keep_a, keep_b], [got_a, got_b], 1)
+    (keep,), (received,) = fold("fold2", len(steps) - 1, [keep_a], [got_a], 1)
     node_new, grad_node = node_call(
         where, coarse_row, node_lat, node_cotangent, aggregate, back, parts
     )

time: 91.4 us -> 91.3 us (level)
  waiting for transfers between devices: 21.4 us -> 22.6 us
    pallas_call x20 -> x19, Pallas kernels: 34.2 us -> 33.3 us  [call(): pl.pallas_call(body, out_shape=outs + [mark], in_specs=specs, out_specs=p...]
    ppermute x18 -> x16, waiting for transfers between devices: 21.2 us -> 22 us  [xor_swap(): return lax.ppermute(value, axis, [(i, i ^ distance) for i in range(size)])]
    ppermute x18 -> x16, starting transfers between devices: 27.6 us -> 27.2 us  [xor_swap(): return lax.ppermute(value, axis, [(i, i ^ distance) for i in range(size)])]
  transfers between devices with their start and end apart: 22 -> 20, of which waited for: 11 -> 9; matrix products, arithmetic and copies ran while one was open for 1% -> 1% of each run, Pallas kernels for 34% -> 33%
where the time goes in v6:
time: 91.3 us; the launch traced here: 91 us
  Pallas kernels  33.3 us (36%)
  starting transfers between devices  30.8 us (34%)
  waiting for transfers between devices  22.6 us (25%)
  local copies, waits for them, and re-layouts  3.3 us (4%)
    pallas_call x19, Pallas kernels, call(): pl.pallas_call(body, out_shape=outs + [mark], in_specs=specs, out_specs=p...  33.3 us
    ppermute x16, starting transfers between devices, xor_swap(): return lax.ppermute(value, axis, [(i, i ^ distance) for i in range(size)])  27.2 us
    ppermute x16, waiting for transfers between devices, xor_swap(): return lax.ppermute(value, axis, [(i, i ^ distance) for i in range(size)])  22 us
    unnamed x26, local copies, waits for them, and re-layouts  2.61 us
  transfers between devices with their start and end apart: 20, of which 9 were waited for; matrix products, arithmetic and copies ran while one was open for 1% of the time, Pallas kernels for 33%

profile of v6, /device:TPU:0, one launch (start us, length us, event | category | flops | bytes accessed | tf_op | source)
XLA Modules:
  0.0 91.0 jit_solution(18384401201266600235)
XLA Ops:
  0.6 4.1 %collective-permute-start.1 = (bf16[256,512]{1,0:T(8,128)(2,1)}, bf16[256,512]{1,0:T(8,128)(2,1)S(1)}, u32[]{:S(2)}, u32[]{:S(2)}) collective-permute-start(bf16[256,512]{1,0:T(8,128)(2,1)} %refs_2_.3), channel_id=1, source_target_pairs={{0,2},{1,3},{2,0},{3,1},{4,6},{5,7},{6,4},{7,5},{8,10},{9,11},{10,... | collective-permute-start | bytes 786440 | tf_op jit(solution)/shard_map/ppermute | solution.py:632
  4.7 1.6 %collective-permute-start = (bf16[256,512]{1,0:T(8,128)(2,1)}, bf16[256,512]{1,0:T(8,128)(2,1)S(1)}, u32[]{:S(2)}, u32[]{:S(2)}) collective-permute-start(bf16[256,512]{1,0:T(8,128)(2,1)} %refs_2_.3), channel_id=1, source_target_pairs={{0,1},{1,0},{2,3},{3,2},{4,5},{5,4},{6,7},{7,6},{8,9},{9,8},{10,11... | collective-permute-start | bytes 786440 | tf_op jit(solution)/shard_map/ppermute | solution.py:632
  11.8 1.6 %collective-permute-start.6 = (f32[16,1152]{1,0:T(8,128)S(1)}, f32[16,1152]{1,0:T(8,128)S(1)}, u32[]{:S(2)}, u32[]{:S(2)}) collective-permute-start(f32[16,1152]{1,0:T(8,128)S(1)} %bitcast.35), channel_id=1, source_target_pairs={{0,8},{4,12},{8,0},{12,4},{1,9},{5,13},{9,1},{13,5},{2,10},{6,14},... | collective-permute-start | bytes 221192 | tf_op jit(solution)/shard_map/ppermute | solution.py:632
  13.4 3.6 %collective-permute-done.1.refs_11_.refs_3_.refs_9_ = bf16[256,512]{1,0:T(8,128)(2,1)S(1)} collective-permute-done((bf16[256,512]{1,0:T(8,128)(2,1)}, bf16[256,512]{1,0:T(8,128)(2,1)S(1)}, u32[]{:S(2)}, u32[]{:S(2)}) %collective-permute-start.1) | collective-permute-done | bytes 262176 | tf_op jit(solution)/shard_map/ppermute | solution.py:632
  17.7 5.9 %base_terms.1 = (f32[2048,512]{1,0:T(8,128)S(1)}, f32[8,128]{1,0:T(8,128)S(1)}) custom-call(bf16[2048,512]{1,0:T(8,128)(2,1)} %bitcast.23, bf16[256,512]{1,0:T(8,128)(2,1)S(1)} %copy-done.3, s32[2048,1]{1,0:T(8,128)S(1)} %broadcast_in_dim_reshape.8.refs_2_.refs_1_, bf16[1536,512]{1,0:T(8,128)(2,1)S(1)} %copy-done.1, f32[1,512]{1,0:T(1,128)S(1)} %bitcast.36, ...), custom_call_target="tpu_custom_call" | custom-call | flops 17250000896 | bytes 1048576 | tf_op jit(solution)/shard_map/base_terms/pallas_call | solution.py:82
  25.0 1.7 %collective-permute-start.5 = (bf16[128,512]{1,0:T(8,128)(2,1)S(1)}, bf16[128,512]{1,0:T(8,128)(2,1)S(1)}, u32[]{:S(2)}, u32[]{:S(2)}) collective-permute-start(bf16[128,512]{1,0:T(8,128)(2,1)S(1)} %get-tuple-element.71), channel_id=1, source_target_pairs={{4,0},{8,4},{12,8},{0,12},{5,1},{9,5},{13,9},{1,13},{6,2},{10,6},{... | collective-permute-start | bytes 393224 | tf_op jit(solution)/shard_map/ppermute | solution.py:735
  26.7 3.1 %collective-permute-start.7 = (f32[16,1152]{1,0:T(8,128)S(1)}, f32[16,1152]{1,0:T(8,128)S(1)}, u32[]{:S(2)}, u32[]{:S(2)}) collective-permute-start(f32[16,1152]{1,0:T(8,128)S(1)} %get-tuple-element.79.refs_2_), channel_id=1, source_target_pairs={{0,2},{1,3},{2,0},{3,1},{4,6},{5,7},{6,4},{7,5},{8,10},{9,11},{10,... | collective-permute-start | bytes 221192 | tf_op jit(solution)/shard_map/ppermute | solution.py:632
  29.9 12.3 %edge_block.1 = (bf16[2048,512]{1,0:T(8,128)(2,1)}, f32[256,512]{1,0:T(8,128)S(1)}, bf16[2048,512]{1,0:T(8,128)(2,1)S(1)}, bf16[2048,512]{1,0:T(8,128)(2,1)S(1)}...) custom-call(f32[2048,512]{1,0:T(8,128)S(1)} %get-tuple-element.68.re, ...), custom_call_target="tpu_custom_call" | custom-call | flops 41400000512 | bytes 1048576 | tf_op jit(solution)/shard_map/edge_block/pallas_call | solution.py:82
  44.7 2.5 %patch_sums.1 = (f32[1024,512]{1,0:T(8,128)S(1)}, f32[8,128]{1,0:T(8,128)S(1)}) custom-call(s32[1,2048]{1,0:T(1,128)S(1)} %broadcast_in_dim_reshape.7.refs_5_.refs_0_, bf16[2048,512]{1,0:T(8,128)(2,1)S(1)} %get-tuple-element.78.refs_1_, f32[8,128]{1,0:T(8,128)S(1)} %get-tuple-element.83.refs_2_), custom_call_target="tpu_custom_call" | custom-call | flops 345000000 | bytes 1048576 | tf_op jit(solution)/shard_map/patch_sums/pallas_call | solution.py:82
  48.4 1.8 %collective-permute-start.10 = (bf16[304,512]{1,0:T(8,128)(2,1)S(1)}, bf16[304,512]{1,0:T(8,128)(2,1)S(1)}, u32[]{:S(2)}, u32[]{:S(2)}) collective-permute-start(bf16[304,512]{1,0:T(8,128)(2,1)S(1)} %get-tuple-element.89.refs_0_), channel_id=1, source_target_pairs={{0,1},{1,0},{2,3},{3,2},{4,5},{5,4},{6,7},{7,6},{8,9},{9,8},{10,11... | collective-permute-start | bytes 933896 | tf_op jit(solution)/shard_map/ppermute | solution.py:632
  50.2 2.3 %edge_grads.1 = (f32[512,512]{1,0:T(8,128)S(1)}, f32[512,512]{1,0:T(8,128)S(1)}, f32[8,128]{1,0:T(8,128)S(1)}) custom-call(bf16[2048,512]{1,0:T(8,128)(2,1)S(1)} %bitcast.25, bf16[2048,512]{1,0:T(8,128)(2,1)S(1)} %get-tuple-element.78.refs_1_, bf16[2048,512]{1,0:T(8,128)(2,1)S(1)} %get-tuple-element.91.refs_2_, ...), custom_call_target="tpu_custom_call" | custom-call | flops 345000000 | bytes 1048576 | tf_op jit(solution)/shard_map/edge_grads/pallas_call | solution.py:82
  52.6 1.9 %pack_grads.1 = (f32[4,2,512,128]{3,2,1,0:T(8,128)S(1)}, bf16[4,2,512,128]{3,2,1,0:T(8,128)(2,1)S(1)}, f32[8,128]{1,0:T(8,128)S(1)}) custom-call(s32[2]{0:T(128)S(1)} %pad_add_fusion.refs_3_.refs_0_, bf16[256,512]{1,0:T(8,128)(2,1)S(1)} %get-tuple-element.90.refs_1_.refs_3_, f32[512,512]{1,0:T(8,128)S(1)} %get-tuple-element.94.refs_2_, ...), custom_call_target="tpu_custom_call" | custom-call | flops 345000000 | bytes 1048576 | tf_op jit(solution)/shard_map/pack_grads/pallas_call | solution.py:82
  54.5 1.0 %collective-permute-start.13 = (bf16[4,2,512,128]{3,2,1,0:T(8,128)(2,1)S(1)}, bf16[4,2,512,128]{3,2,1,0:T(8,128)(2,1)S(1)}, u32[]{:S(2)}, u32[]{:S(2)}) collective-permute-start(bf16[4,2,512,128]{3,2,1,0:T(8,128)(2,1)S(1)} %get-tuple-element.101), channel_id=1, source_target_pairs={{0,4},{4,0},{8,12},{12,8},{1,5},{5,1},{9,13},{13,9},{2,6},{6,2},{1... | collective-permute-start | bytes 3145736 | tf_op jit(solution)/shard_map/ppermute | solution.py:632
  55.5 3.0 %collective-permute-done.10.refs_1_ = bf16[304,512]{1,0:T(8,128)(2,1)S(1)} collective-permute-done((bf16[304,512]{1,0:T(8,128)(2,1)S(1)}, bf16[304,512]{1,0:T(8,128)(2,1)S(1)}, u32[]{:S(2)}, u32[]{:S(2)}) %collective-permute-start.10) | collective-permute-done | bytes 311328 | tf_op jit(solution)/shard_map/ppermute | solution.py:632
  59.4 1.6 %collective-permute-start.14 = (bf16[4,512,128]{2,1,0:T(8,128)(2,1)S(1)}, bf16[4,512,128]{2,1,0:T(8,128)(2,1)S(1)}, u32[]{:S(2)}, u32[]{:S(2)}) collective-permute-start(bf16[4,512,128]{2,1,0:T(8,128)(2,1)S(1)} %get-tuple-element.104), channel_id=1, source_target_pairs={{0,8},{4,12},{8,0},{12,4},{1,9},{5,13},{9,1},{13,5},{2,10},{6,14},... | collective-permute-start | bytes 1572872 | tf_op jit(solution)/shard_map/ppermute | solution.py:632
  61.0 1.7 %collective-permute-start.12 = (bf16[256,512]{1,0:T(8,128)(2,1)S(1)}, bf16[256,512]{1,0:T(8,128)(2,1)S(1)}, u32[]{:S(2)}, u32[]{:S(2)}) collective-permute-start(bf16[256,512]{1,0:T(8,128)(2,1)S(1)} %get-tuple-element.99), channel_id=1, source_target_pairs={{0,1},{1,0},{2,3},{3,2},{4,5},{5,4},{6,7},{7,6},{8,9},{9,8},{10,11... | collective-permute-start | bytes 786440 | tf_op jit(solution)/shard_map/ppermute | solution.py:632
  62.7 3.2 %collective-permute-start.11 = (bf16[256,512]{1,0:T(8,128)(2,1)S(1)}, bf16[256,512]{1,0:T(8,128)(2,1)S(1)}, u32[]{:S(2)}, u32[]{:S(2)}) collective-permute-start(bf16[256,512]{1,0:T(8,128)(2,1)S(1)} %get-tuple-element.98), channel_id=1, source_target_pairs={{0,2},{1,3},{2,0},{3,1},{4,6},{5,7},{6,4},{7,5},{8,10},{9,11},{10,... | collective-permute-start | bytes 786440 | tf_op jit(solution)/shard_map/ppermute | solution.py:632
  65.9 7.5 %collective-permute-done.14 = bf16[4,512,128]{2,1,0:T(8,128)(2,1)S(1)} collective-permute-done((bf16[4,512,128]{2,1,0:T(8,128)(2,1)S(1)}, bf16[4,512,128]{2,1,0:T(8,128)(2,1)S(1)}, u32[]{:S(2)}, u32[]{:S(2)}) %collective-permute-start.14) | collective-permute-done | bytes 524320 | tf_op jit(solution)/shard_map/ppermute | solution.py:632
  74.0 1.8 %collective-permute-start.18 = (bf16[2,512,128]{2,1,0:T(8,128)(2,1)S(1)}, bf16[2,512,128]{2,1,0:T(8,128)(2,1)S(1)}, u32[]{:S(2)}, u32[]{:S(2)}) collective-permute-start(bf16[2,512,128]{2,1,0:T(8,128)(2,1)S(1)} %get-tuple-element.111), channel_id=1, source_target_pairs={{0,1},{1,0},{2,3},{3,2},{4,5},{5,4},{6,7},{7,6},{8,9},{9,8},{10,11... | collective-permute-start | bytes 786440 | tf_op jit(solution)/shard_map/ppermute | solution.py:632
  75.9 1.3 %collective-permute-start.16 = (bf16[48,512]{1,0:T(8,128)(2,1)S(1)}, bf16[48,512]{1,0:T(8,128)(2,1)S(1)}, u32[]{:S(2)}, u32[]{:S(2)}) collective-permute-start(bf16[48,512]{1,0:T(8,128)(2,1)S(1)} %get-tuple-element.109.refs_6_), channel_id=1, source_target_pairs={{0,8},{4,12},{8,0},{12,4},{1,9},{5,13},{9,1},{13,5},{2,10},{6,14},... | collective-permute-start | bytes 147464 | tf_op jit(solution)/shard_map/ppermute | solution.py:632
  78.3 3.5 %collective-permute-done.18 = bf16[2,512,128]{2,1,0:T(8,128)(2,1)S(1)} collective-permute-done((bf16[2,512,128]{2,1,0:T(8,128)(2,1)S(1)}, bf16[2,512,128]{2,1,0:T(8,128)(2,1)S(1)}, u32[]{:S(2)}, u32[]{:S(2)}) %collective-permute-start.18) | collective-permute-done | bytes 262176 | tf_op jit(solution)/shard_map/ppermute | solution.py:632
  82.4 3.0 %collective-permute-start.19 = (bf16[1,512,128]{2,1,0:T(8,128)(2,1)S(1)}, bf16[1,512,128]{2,1,0:T(8,128)(2,1)S(1)}, u32[]{:S(2)}, u32[]{:S(2)}) collective-permute-start(bf16[1,512,128]{2,1,0:T(8,128)(2,1)S(1)} %get-tuple-element.118), channel_id=1, source_target_pairs={{0,2},{1,3},{2,0},{3,1},{4,6},{5,7},{6,4},{7,5},{8,10},{9,11},{10,... | collective-permute-start | bytes 393224 | tf_op jit(solution)/shard_map/ppermute | solution.py:632
  85.4 1.8 %node_outputs.1 = (bf16[256,512]{1,0:T(8,128)(2,1)}, bf16[256,512]{1,0:T(8,128)(2,1)}, f32[8,128]{1,0:T(8,128)S(1)}) custom-call(s32[2]{0:T(128)S(1)} %pad_add_fusion.refs_3_.refs_0_, s32[1,256]{1,0:T(1,128)S(1)} %bitcast.40, bf16[256,512]{1,0:T(8,128)(2,1)S(1)} %copy-done.3, bf16[256,512]{1,0:T(8,128)(2,1)S(1)} %copy-done.6, ...), custom_call_target="tpu_custom_call" | custom-call | flops 2300000000 | bytes 1048576 | tf_op jit(solution)/shard_map/node_outputs/pallas_call | solution.py:82
  87.2 3.0 %collective-permute-done.19 = bf16[1,512,128]{2,1,0:T(8,128)(2,1)S(1)} collective-permute-done((bf16[1,512,128]{2,1,0:T(8,128)(2,1)S(1)}, bf16[1,512,128]{2,1,0:T(8,128)(2,1)S(1)}, u32[]{:S(2)}, u32[]{:S(2)}) %collective-permute-start.19) | collective-permute-done | bytes 131104 | tf_op jit(solution)/shard_map/ppermute | solution.py:632
  (68 shorter events, 15.1 us)
Async XLA Ops:
  0.6 16.3 %collective-permute-start.1 = (bf16[256,512]{1,0:T(8,128)(2,1)}, bf16[256,512]{1,0:T(8,128)(2,1)S(1)}, u32[]{:S(2)}, u32[]{:S(2)}) collective-permute-start(bf16[256,512]{1,0:T(8,128)(2,1)} %refs_2_.3), channel_id=1, source_target_pairs={{0,2},{1,3},{2,0},{3,1},{4,6},{5,7},{6,4},{7,5},{8,10},{9,11},{10,... | collective-permute-start | bytes 786440 | tf_op jit(solution)/shard_map/ppermute | solution.py:632
  4.7 13.0 %collective-permute-start = (bf16[256,512]{1,0:T(8,128)(2,1)}, bf16[256,512]{1,0:T(8,128)(2,1)S(1)}, u32[]{:S(2)}, u32[]{:S(2)}) collective-permute-start(bf16[256,512]{1,0:T(8,128)(2,1)} %refs_2_.3), channel_id=1, source_target_pairs={{0,1},{1,0},{2,3},{3,2},{4,5},{5,4},{6,7},{7,6},{8,9},{9,8},{10,11... | collective-permute-start | bytes 786440 | tf_op jit(solution)/shard_map/ppermute | solution.py:632
  9.8 1.4 %collective-permute-start.2 = (f32[32,1152]{1,0:T(8,128)S(1)}, f32[32,1152]{1,0:T(8,128)S(1)}, u32[]{:S(2)}, u32[]{:S(2)}) collective-permute-start(f32[32,1152]{1,0:T(8,128)S(1)} %get-tuple-element.65), channel_id=1, source_target_pairs={{0,4},{4,0},{8,12},{12,8},{1,5},{5,1},{9,13},{13,9},{2,6},{6,2},{1... | collective-permute-start | bytes 442376 | tf_op jit(solution)/shard_map/ppermute | solution.py:632
  11.2 6.5 %copy-start.1 = (bf16[1536,512]{1,0:T(8,128)(2,1)S(1)}, bf16[1536,512]{1,0:T(8,128)(2,1)}, u32[]{:S(2)}) copy-start(bf16[1536,512]{1,0:T(8,128)(2,1)} %refs_4_.1) | copy-start | bytes 4718596
  11.2 6.5 %copy-start.3 = (bf16[256,512]{1,0:T(8,128)(2,1)S(1)}, bf16[256,512]{1,0:T(8,128)(2,1)}, u32[]{:S(2)}) copy-start(bf16[256,512]{1,0:T(8,128)(2,1)} %refs_2_.3) | copy-start | bytes 786436
  11.2 6.5 %copy-start.7 = (f32[512]{0:T(512)S(1)}, f32[512]{0:T(512)}, u32[]{:S(2)}) copy-start(f32[512]{0:T(512)} %param.17) | copy-start | bytes 6148
  11.2 6.5 %copy-start.10 = (s32[256]{0:T(256)S(1)}, s32[256]{0:T(256)}, u32[]{:S(2)}) copy-start(s32[256]{0:T(256)} %param.15) | copy-start | bytes 3076
  11.8 14.9 %collective-permute-start.6 = (f32[16,1152]{1,0:T(8,128)S(1)}, f32[16,1152]{1,0:T(8,128)S(1)}, u32[]{:S(2)}, u32[]{:S(2)}) collective-permute-start(f32[16,1152]{1,0:T(8,128)S(1)} %bitcast.35), channel_id=1, source_target_pairs={{0,8},{4,12},{8,0},{12,4},{1,9},{5,13},{9,1},{13,5},{2,10},{6,14},... | collective-permute-start | bytes 221192 | tf_op jit(solution)/shard_map/ppermute | solution.py:632
  17.0 7.4 %collective-permute-start.3 = (bf16[256,512]{1,0:T(8,128)(2,1)S(1)}, bf16[256,512]{1,0:T(8,128)(2,1)S(1)}, u32[]{:S(2)}, u32[]{:S(2)}) collective-permute-start(bf16[256,512]{1,0:T(8,128)(2,1)S(1)} %collective-permute-done.1.refs_11_.refs_3_.refs_9_), channel_id=1, source_target_pairs={{0,1},{1,0},{2,3},{3,2},{4,5},{5,4},{6,7},{7,6},{8,9},{9,8},{10,11... | collective-permute-start | bytes 786440 | tf_op jit(solution)/shard_map/ppermute | solution.py:632
  24.9 4.9 %collective-permute-start.4 = (bf16[128,512]{1,0:T(8,128)(2,1)S(1)}, bf16[128,512]{1,0:T(8,128)(2,1)S(1)}, u32[]{:S(2)}, u32[]{:S(2)}) collective-permute-start(bf16[128,512]{1,0:T(8,128)(2,1)S(1)} %get-tuple-element.70), channel_id=1, source_target_pairs={{0,4},{4,8},{8,12},{12,0},{1,5},{5,9},{9,13},{13,1},{2,6},{6,10},{... | collective-permute-start | bytes 393224 | tf_op jit(solution)/shard_map/ppermute | solution.py:734
  25.0 4.9 %collective-permute-start.5 = (bf16[128,512]{1,0:T(8,128)(2,1)S(1)}, bf16[128,512]{1,0:T(8,128)(2,1)S(1)}, u32[]{:S(2)}, u32[]{:S(2)}) collective-permute-start(bf16[128,512]{1,0:T(8,128)(2,1)S(1)} %get-tuple-element.71), channel_id=1, source_target_pairs={{4,0},{8,4},{12,8},{0,12},{5,1},{9,5},{13,9},{1,13},{6,2},{10,6},{... | collective-permute-start | bytes 393224 | tf_op jit(solution)/shard_map/ppermute | solution.py:735
  26.7 15.4 %collective-permute-start.7 = (f32[16,1152]{1,0:T(8,128)S(1)}, f32[16,1152]{1,0:T(8,128)S(1)}, u32[]{:S(2)}, u32[]{:S(2)}) collective-permute-start(f32[16,1152]{1,0:T(8,128)S(1)} %get-tuple-element.79.refs_2_), channel_id=1, source_target_pairs={{0,2},{1,3},{2,0},{3,1},{4,6},{5,7},{6,4},{7,5},{8,10},{9,11},{10,... | collective-permute-start | bytes 221192 | tf_op jit(solution)/shard_map/ppermute | solution.py:632
  42.9 4.4 %collective-permute-start.8 = (bf16[128,512]{1,0:T(8,128)(2,1)S(1)}, bf16[128,512]{1,0:T(8,128)(2,1)S(1)}, u32[]{:S(2)}, u32[]{:S(2)}) collective-permute-start(bf16[128,512]{1,0:T(8,128)(2,1)S(1)} %get-tuple-element.81.refs_6_), channel_id=1, source_target_pairs={{0,4},{4,8},{8,12},{12,0},{1,5},{5,9},{9,13},{13,1},{2,6},{6,10},{... | collective-permute-start | bytes 393224 | tf_op jit(solution)/shard_map/ppermute | solution.py:756
  43.8 4.0 %collective-permute-start.9 = (bf16[128,512]{1,0:T(8,128)(2,1)S(1)}, bf16[128,512]{1,0:T(8,128)(2,1)S(1)}, u32[]{:S(2)}, u32[]{:S(2)}) collective-permute-start(bf16[128,512]{1,0:T(8,128)(2,1)S(1)} %get-tuple-element.82.refs_5_), channel_id=1, source_target_pairs={{4,0},{8,4},{12,8},{0,12},{5,1},{9,5},{13,9},{1,13},{6,2},{10,6},{... | collective-permute-start | bytes 393224 | tf_op jit(solution)/shard_map/ppermute | solution.py:755
  48.4 10.1 %collective-permute-start.10 = (bf16[304,512]{1,0:T(8,128)(2,1)S(1)}, bf16[304,512]{1,0:T(8,128)(2,1)S(1)}, u32[]{:S(2)}, u32[]{:S(2)}) collective-permute-start(bf16[304,512]{1,0:T(8,128)(2,1)S(1)} %get-tuple-element.89.refs_0_), channel_id=1, source_target_pairs={{0,1},{1,0},{2,3},{3,2},{4,5},{5,4},{6,7},{7,6},{8,9},{9,8},{10,11... | collective-permute-start | bytes 933896 | tf_op jit(solution)/shard_map/ppermute | solution.py:632
  54.5 4.0 %collective-permute-start.13 = (bf16[4,2,512,128]{3,2,1,0:T(8,128)(2,1)S(1)}, bf16[4,2,512,128]{3,2,1,0:T(8,128)(2,1)S(1)}, u32[]{:S(2)}, u32[]{:S(2)}) collective-permute-start(bf16[4,2,512,128]{3,2,1,0:T(8,128)(2,1)S(1)} %get-tuple-element.101), channel_id=1, source_target_pairs={{0,4},{4,0},{8,12},{12,8},{1,5},{5,1},{9,13},{13,9},{2,6},{6,2},{1... | collective-permute-start | bytes 3145736 | tf_op jit(solution)/shard_map/ppermute | solution.py:632
  59.4 14.0 %collective-permute-start.14 = (bf16[4,512,128]{2,1,0:T(8,128)(2,1)S(1)}, bf16[4,512,128]{2,1,0:T(8,128)(2,1)S(1)}, u32[]{:S(2)}, u32[]{:S(2)}) collective-permute-start(bf16[4,512,128]{2,1,0:T(8,128)(2,1)S(1)} %get-tuple-element.104), channel_id=1, source_target_pairs={{0,8},{4,12},{8,0},{12,4},{1,9},{5,13},{9,1},{13,5},{2,10},{6,14},... | collective-permute-start | bytes 1572872 | tf_op jit(solution)/shard_map/ppermute | solution.py:632
  61.0 16.3 %collective-permute-start.12 = (bf16[256,512]{1,0:T(8,128)(2,1)S(1)}, bf16[256,512]{1,0:T(8,128)(2,1)S(1)}, u32[]{:S(2)}, u32[]{:S(2)}) collective-permute-start(bf16[256,512]{1,0:T(8,128)(2,1)S(1)} %get-tuple-element.99), channel_id=1, source_target_pairs={{0,1},{1,0},{2,3},{3,2},{4,5},{5,4},{6,7},{7,6},{8,9},{9,8},{10,11... | collective-permute-start | bytes 786440 | tf_op jit(solution)/shard_map/ppermute | solution.py:632
  62.7 15.1 %collective-permute-start.11 = (bf16[256,512]{1,0:T(8,128)(2,1)S(1)}, bf16[256,512]{1,0:T(8,128)(2,1)S(1)}, u32[]{:S(2)}, u32[]{:S(2)}) collective-permute-start(bf16[256,512]{1,0:T(8,128)(2,1)S(1)} %get-tuple-element.98), channel_id=1, source_target_pairs={{0,2},{1,3},{2,0},{3,1},{4,6},{5,7},{6,4},{7,5},{8,10},{9,11},{10,... | collective-permute-start | bytes 786440 | tf_op jit(solution)/shard_map/ppermute | solution.py:632
  74.0 7.8 %collective-permute-start.18 = (bf16[2,512,128]{2,1,0:T(8,128)(2,1)S(1)}, bf16[2,512,128]{2,1,0:T(8,128)(2,1)S(1)}, u32[]{:S(2)}, u32[]{:S(2)}) collective-permute-start(bf16[2,512,128]{2,1,0:T(8,128)(2,1)S(1)} %get-tuple-element.111), channel_id=1, source_target_pairs={{0,1},{1,0},{2,3},{3,2},{4,5},{5,4},{6,7},{7,6},{8,9},{9,8},{10,11... | collective-permute-start | bytes 786440 | tf_op jit(solution)/shard_map/ppermute | solution.py:632
  75.9 9.6 %collective-permute-start.17 = (bf16[48,512]{1,0:T(8,128)(2,1)S(1)}, bf16[48,512]{1,0:T(8,128)(2,1)S(1)}, u32[]{:S(2)}, u32[]{:S(2)}) collective-permute-start(bf16[48,512]{1,0:T(8,128)(2,1)S(1)} %get-tuple-element.109.refs_6_), channel_id=1, source_target_pairs={{0,12},{4,8},{8,4},{12,0},{1,13},{5,9},{9,5},{13,1},{2,14},{6,10},... | collective-permute-start | bytes 147464 | tf_op jit(solution)/shard_map/ppermute | solution.py:632
  75.9 9.5 %collective-permute-start.16 = (bf16[48,512]{1,0:T(8,128)(2,1)S(1)}, bf16[48,512]{1,0:T(8,128)(2,1)S(1)}, u32[]{:S(2)}, u32[]{:S(2)}) collective-permute-start(bf16[48,512]{1,0:T(8,128)(2,1)S(1)} %get-tuple-element.109.refs_6_), channel_id=1, source_target_pairs={{0,8},{4,12},{8,0},{12,4},{1,9},{5,13},{9,1},{13,5},{2,10},{6,14},... | collective-permute-start | bytes 147464 | tf_op jit(solution)/shard_map/ppermute | solution.py:632
  77.3 8.2 %collective-permute-start.15 = (bf16[48,512]{1,0:T(8,128)(2,1)S(1)}, bf16[48,512]{1,0:T(8,128)(2,1)S(1)}, u32[]{:S(2)}, u32[]{:S(2)}) collective-permute-start(bf16[48,512]{1,0:T(8,128)(2,1)S(1)} %get-tuple-element.109.refs_6_), channel_id=1, source_target_pairs={{0,4},{4,0},{8,12},{12,8},{1,5},{5,1},{9,13},{13,9},{2,6},{6,2},{1... | collective-permute-start | bytes 147464 | tf_op jit(solution)/shard_map/ppermute | solution.py:632
  82.4 7.9 %collective-permute-start.19 = (bf16[1,512,128]{2,1,0:T(8,128)(2,1)S(1)}, bf16[1,512,128]{2,1,0:T(8,128)(2,1)S(1)}, u32[]{:S(2)}, u32[]{:S(2)}) collective-permute-start(bf16[1,512,128]{2,1,0:T(8,128)(2,1)S(1)} %get-tuple-element.118), channel_id=1, source_target_pairs={{0,2},{1,3},{2,0},{3,1},{4,6},{5,7},{6,4},{7,5},{8,10},{9,11},{10,... | collective-permute-start | bytes 393224 | tf_op jit(solution)/shard_map/ppermute | solution.py:632
  (9 other events, 20.0 us)

commit v7 on v6

--- a/solution.py
+++ b/solution.py
@@ -37,6 +37,7 @@
     "add_rim_sums": 0.3,
     "pack_grads": 0.3,
     "coarse_rows": 0.3,
+    "near_sum": 0.3,
     "far_sum": 30,
     "node_outputs": 2,
     "grad_node": .1,
@@ -514,6 +515,20 @@
     )(own, got)
 
 
+def near_sum_kernel(own_ref, got_ref, out_ref):
+    out_ref[...] = own_ref[...].astype(F32) + got_ref[...].astype(F32)
+
+
+def near_sum_call(own, got):
+    return launch(
+        near_sum_kernel,
+        out_shape=jax.ShapeDtypeStruct(own.shape, F32),
+        compiler_params=params(),
+        cost_estimate=cost("near_sum"),
+        name="near_sum",
+    )(own, got)
+
+
 def add_split_kernel(axis, shift, count, where_ref, *refs):
     keeps, gots = refs[:count], refs[count : 2 * count]
     outs = refs[2 * count :]
@@ -607,9 +622,9 @@
     )(where, ids, lat, cot, agg, back, *pieces)
 
 
-def node_back_kernel(own_ref, far_ref, near_ref, psum_ref, weight_ref, out_ref):
+def node_back_kernel(own_ref, far_ref, psum_ref, weight_ref, out_ref):
     latent = own_ref.shape[1]
-    total = own_ref[...].astype(F32) + far_ref[...].astype(F32) + near_ref[...].astype(F32)
+    total = own_ref[...] + far_ref[...].astype(F32)
     back = lax.dot_general(
         total.astype(BF16), weight_ref[latent : 2 * latent], COLS, preferred_element_type=F32
     )
@@ -617,14 +632,14 @@
     out_ref[...] = back + own
 
 
-def node_back_call(own, far, near, psum, weight_in):
+def node_back_call(own, far, psum, weight_in):
     return launch(
         node_back_kernel,
         out_shape=jax.ShapeDtypeStruct(own.shape, F32),
         compiler_params=params(),
         cost_estimate=cost("grad_node"),
         name="grad_node",
-    )(own, far, near, psum, weight_in)
+    )(own, far, psum, weight_in)
 
 
 def xor_swap(value, axis, distance):
@@ -792,14 +807,16 @@
         far_sum = far_sum_call(sums[2], relay)
         got_far = xor_swap(far_sum, "feat", 2)
         got_near = xor_swap(sums[1], "feat", 1)
-        own = [sums[0], got_far, got_near]
+        own = [got_near, got_far]
     else:
         parts = sums
         for distance in reversed(bits_of(feat_count)):
             arrived = [xor_swap(part, "feat", distance) for part in parts[distance:]]
             parts = [add_pair_call(a, b) for a, b in zip(parts[:distance], arrived)]
-        own = [parts[0], jnp.zeros_like(parts[0]), jnp.zeros_like(parts[0])]
+        sums = parts
+        own = [jnp.zeros_like(parts[0]), jnp.zeros_like(parts[0])]
     (keep_a,), (got_a,) = fold("fold0", 0, [keep], [got_core], 1)
+    own_sum = near_sum_call(sums[0], own[0])
     keep_a, got_a = fold_half("fold1", keep_a, got_a)
     if whole_step:
         coarse_all = coarse_rows_call(sums[3], relay, 3 * coarse.shape[0])
@@ -807,7 +824,7 @@
     else:
         counts = jnp.pad(coarse[:, 2 * latent :], ((0, 0), (128, latent - 256)))
         parts = [jnp.concatenate([coarse[:, :latent], coarse[:, latent : 2 * latent], counts], axis=0)]
-    back = node_back_call(*own, pre_sum, weight_in)
+    back = node_back_call(own_sum, own[1], pre_sum, weight_in)
     (keep,), (received,) = fold("fold2", len(steps) - 1, [keep_a], [got_a], 1)
     node_new, grad_node = node_call(
         where, coarse_row, node_lat, node_cotangent, aggregate, back, parts

time: 91.3 us -> 91.3 us (level)
    pallas_call x19 -> x20, Pallas kernels: 33.3 us -> 33.4 us  [call(): pl.pallas_call(body, out_shape=outs + [mark], in_specs=specs, out_specs=p...]
  transfers between devices with their start and end apart: 20 -> 20, of which waited for: 9 -> 9; matrix products, arithmetic and copies ran while one was open for 1% -> 1% of each run, Pallas kernels for 33% -> 34%
where the time goes in v7:
time: 91.3 us; the launch traced here: 91 us
  Pallas kernels  33.4 us (37%)
  starting transfers between devices  29.9 us (33%)
  waiting for transfers between devices  23.4 us (26%)
  local copies, waits for them, and re-layouts  3.3 us (4%)
    pallas_call x20, Pallas kernels, call(): pl.pallas_call(body, out_shape=outs + [mark], in_specs=specs, out_specs=p...  33.4 us
    ppermute x16, starting transfers between devices, xor_swap(): return lax.ppermute(value, axis, [(i, i ^ distance) for i in range(size)])  26.3 us
    ppermute x16, waiting for transfers between devices, xor_swap(): return lax.ppermute(value, axis, [(i, i ^ distance) for i in range(size)])  22.8 us
    unnamed x26, local copies, waits for them, and re-layouts  2.61 us
  transfers between devices with their start and end apart: 20, of which 9 were waited for; matrix products, arithmetic and copies ran while one was open for 1% of the time, Pallas kernels for 34%

profile of v7, /device:TPU:0, one launch (start us, length us, event | category | flops | bytes accessed | tf_op | source)
XLA Modules:
  0.0 91.0 jit_solution(15766806045718084026)
XLA Ops:
  0.6 4.1 %collective-permute-start.1 = (bf16[256,512]{1,0:T(8,128)(2,1)}, bf16[256,512]{1,0:T(8,128)(2,1)S(1)}, u32[]{:S(2)}, u32[]{:S(2)}) collective-permute-start(bf16[256,512]{1,0:T(8,128)(2,1)} %refs_2_.3), channel_id=1, source_target_pairs={{0,2},{1,3},{2,0},{3,1},{4,6},{5,7},{6,4},{7,5},{8,10},{9,11},{10,... | collective-permute-start | bytes 786440 | tf_op jit(solution)/shard_map/ppermute | solution.py:647
  4.7 1.6 %collective-permute-start = (bf16[256,512]{1,0:T(8,128)(2,1)}, bf16[256,512]{1,0:T(8,128)(2,1)S(1)}, u32[]{:S(2)}, u32[]{:S(2)}) collective-permute-start(bf16[256,512]{1,0:T(8,128)(2,1)} %refs_2_.3), channel_id=1, source_target_pairs={{0,1},{1,0},{2,3},{3,2},{4,5},{5,4},{6,7},{7,6},{8,9},{9,8},{10,11... | collective-permute-start | bytes 786440 | tf_op jit(solution)/shard_map/ppermute | solution.py:647
  6.4 0.9 %copy-done.2 = bf16[256,512]{1,0:T(8,128)(2,1)S(1)} copy-done((bf16[256,512]{1,0:T(8,128)(2,1)S(1)}, bf16[256,512]{1,0:T(8,128)(2,1)}, u32[]{:S(2)}) %copy-start.2) | copy-done | bytes 262168
  11.8 1.6 %collective-permute-start.6 = (f32[16,1152]{1,0:T(8,128)S(1)}, f32[16,1152]{1,0:T(8,128)S(1)}, u32[]{:S(2)}, u32[]{:S(2)}) collective-permute-start(f32[16,1152]{1,0:T(8,128)S(1)} %bitcast.35), channel_id=1, source_target_pairs={{0,8},{4,12},{8,0},{12,4},{1,9},{5,13},{9,1},{13,5},{2,10},{6,14},... | collective-permute-start | bytes 221192 | tf_op jit(solution)/shard_map/ppermute | solution.py:647
  13.4 3.6 %collective-permute-done.1.refs_11_.refs_3_.refs_9_ = bf16[256,512]{1,0:T(8,128)(2,1)S(1)} collective-permute-done((bf16[256,512]{1,0:T(8,128)(2,1)}, bf16[256,512]{1,0:T(8,128)(2,1)S(1)}, u32[]{:S(2)}, u32[]{:S(2)}) %collective-permute-start.1) | collective-permute-done | bytes 262176 | tf_op jit(solution)/shard_map/ppermute | solution.py:647
  17.7 5.9 %base_terms.1 = (f32[2048,512]{1,0:T(8,128)S(1)}, f32[8,128]{1,0:T(8,128)S(1)}) custom-call(bf16[2048,512]{1,0:T(8,128)(2,1)} %bitcast.23, bf16[256,512]{1,0:T(8,128)(2,1)S(1)} %copy-done.3, s32[2048,1]{1,0:T(8,128)S(1)} %broadcast_in_dim_reshape.8.refs_2_.refs_1_, bf16[1536,512]{1,0:T(8,128)(2,1)S(1)} %copy-done.1, f32[1,512]{1,0:T(1,128)S(1)} %bitcast.36, ...), custom_call_target="tpu_custom_call" | custom-call | flops 17250000896 | bytes 1048576 | tf_op jit(solution)/shard_map/base_terms/pallas_call | solution.py:83
  25.0 1.7 %collective-permute-start.5 = (bf16[128,512]{1,0:T(8,128)(2,1)S(1)}, bf16[128,512]{1,0:T(8,128)(2,1)S(1)}, u32[]{:S(2)}, u32[]{:S(2)}) collective-permute-start(bf16[128,512]{1,0:T(8,128)(2,1)S(1)} %get-tuple-element.73), channel_id=1, source_target_pairs={{4,0},{8,4},{12,8},{0,12},{5,1},{9,5},{13,9},{1,13},{6,2},{10,6},{... | collective-permute-start | bytes 393224 | tf_op jit(solution)/shard_map/ppermute | solution.py:750
  26.7 3.1 %collective-permute-start.7 = (f32[16,1152]{1,0:T(8,128)S(1)}, f32[16,1152]{1,0:T(8,128)S(1)}, u32[]{:S(2)}, u32[]{:S(2)}) collective-permute-start(f32[16,1152]{1,0:T(8,128)S(1)} %get-tuple-element.81.refs_2_), channel_id=1, source_target_pairs={{0,2},{1,3},{2,0},{3,1},{4,6},{5,7},{6,4},{7,5},{8,10},{9,11},{10,... | collective-permute-start | bytes 221192 | tf_op jit(solution)/shard_map/ppermute | solution.py:647
  29.9 12.3 %edge_block.1 = (bf16[2048,512]{1,0:T(8,128)(2,1)}, f32[256,512]{1,0:T(8,128)S(1)}, bf16[2048,512]{1,0:T(8,128)(2,1)S(1)}, bf16[2048,512]{1,0:T(8,128)(2,1)S(1)}...) custom-call(f32[2048,512]{1,0:T(8,128)S(1)} %get-tuple-element.70.re, ...), custom_call_target="tpu_custom_call" | custom-call | flops 41400000512 | bytes 1048576 | tf_op jit(solution)/shard_map/edge_block/pallas_call | solution.py:83
  44.7 2.5 %patch_sums.1 = (f32[1024,512]{1,0:T(8,128)S(1)}, f32[8,128]{1,0:T(8,128)S(1)}) custom-call(s32[1,2048]{1,0:T(1,128)S(1)} %broadcast_in_dim_reshape.7.refs_5_.refs_0_, bf16[2048,512]{1,0:T(8,128)(2,1)S(1)} %get-tuple-element.80.refs_1_, f32[8,128]{1,0:T(8,128)S(1)} %get-tuple-element.85.refs_2_), custom_call_target="tpu_custom_call" | custom-call | flops 345000000 | bytes 1048576 | tf_op jit(solution)/shard_map/patch_sums/pallas_call | solution.py:83
  48.5 1.8 %collective-permute-start.12 = (bf16[304,512]{1,0:T(8,128)(2,1)S(1)}, bf16[304,512]{1,0:T(8,128)(2,1)S(1)}, u32[]{:S(2)}, u32[]{:S(2)}) collective-permute-start(bf16[304,512]{1,0:T(8,128)(2,1)S(1)} %get-tuple-element.101.refs_0_), channel_id=1, source_target_pairs={{0,1},{1,0},{2,3},{3,2},{4,5},{5,4},{6,7},{7,6},{8,9},{9,8},{10,11... | collective-permute-start | bytes 933896 | tf_op jit(solution)/shard_map/ppermute | solution.py:647
  50.3 2.3 %edge_grads.1 = (f32[512,512]{1,0:T(8,128)S(1)}, f32[512,512]{1,0:T(8,128)S(1)}, f32[8,128]{1,0:T(8,128)S(1)}) custom-call(bf16[2048,512]{1,0:T(8,128)(2,1)S(1)} %bitcast.25, bf16[2048,512]{1,0:T(8,128)(2,1)S(1)} %get-tuple-element.80.refs_1_, bf16[2048,512]{1,0:T(8,128)(2,1)S(1)} %get-tuple-element.92.refs_2_, ...), custom_call_target="tpu_custom_call" | custom-call | flops 345000000 | bytes 1048576 | tf_op jit(solution)/shard_map/edge_grads/pallas_call | solution.py:83
  52.6 1.9 %pack_grads.1 = (f32[4,2,512,128]{3,2,1,0:T(8,128)S(1)}, bf16[4,2,512,128]{3,2,1,0:T(8,128)(2,1)S(1)}, f32[8,128]{1,0:T(8,128)S(1)}) custom-call(s32[2]{0:T(128)S(1)} %pad_add_fusion.refs_3_.refs_0_, bf16[256,512]{1,0:T(8,128)(2,1)S(1)} %get-tuple-element.91.refs_1_.refs_2_, f32[512,512]{1,0:T(8,128)S(1)} %get-tuple-element.95.refs_2_, ...), custom_call_target="tpu_custom_call" | custom-call | flops 345000000 | bytes 1048576 | tf_op jit(solution)/shard_map/pack_grads/pallas_call | solution.py:83
  54.6 1.0 %collective-permute-start.11 = (bf16[4,2,512,128]{3,2,1,0:T(8,128)(2,1)S(1)}, bf16[4,2,512,128]{3,2,1,0:T(8,128)(2,1)S(1)}, u32[]{:S(2)}, u32[]{:S(2)}) collective-permute-start(bf16[4,2,512,128]{3,2,1,0:T(8,128)(2,1)S(1)} %get-tuple-element.99), channel_id=1, source_target_pairs={{0,4},{4,0},{8,12},{12,8},{1,5},{5,1},{9,13},{13,9},{2,6},{6,2},{1... | collective-permute-start | bytes 3145736 | tf_op jit(solution)/shard_map/ppermute | solution.py:647
  55.5 3.0 %collective-permute-done.12.refs_1_ = bf16[304,512]{1,0:T(8,128)(2,1)S(1)} collective-permute-done((bf16[304,512]{1,0:T(8,128)(2,1)S(1)}, bf16[304,512]{1,0:T(8,128)(2,1)S(1)}, u32[]{:S(2)}, u32[]{:S(2)}) %collective-permute-start.12) | collective-permute-done | bytes 311328 | tf_op jit(solution)/shard_map/ppermute | solution.py:647
  59.3 1.6 %collective-permute-start.14 = (bf16[4,512,128]{2,1,0:T(8,128)(2,1)S(1)}, bf16[4,512,128]{2,1,0:T(8,128)(2,1)S(1)}, u32[]{:S(2)}, u32[]{:S(2)}) collective-permute-start(bf16[4,512,128]{2,1,0:T(8,128)(2,1)S(1)} %get-tuple-element.108), channel_id=1, source_target_pairs={{0,8},{4,12},{8,0},{12,4},{1,9},{5,13},{9,1},{13,5},{2,10},{6,14},... | collective-permute-start | bytes 1572872 | tf_op jit(solution)/shard_map/ppermute | solution.py:647
  61.0 1.7 %collective-permute-start.10 = (bf16[256,512]{1,0:T(8,128)(2,1)S(1)}, bf16[256,512]{1,0:T(8,128)(2,1)S(1)}, u32[]{:S(2)}, u32[]{:S(2)}) collective-permute-start(bf16[256,512]{1,0:T(8,128)(2,1)S(1)} %get-tuple-element.90), channel_id=1, source_target_pairs={{0,1},{1,0},{2,3},{3,2},{4,5},{5,4},{6,7},{7,6},{8,9},{9,8},{10,11... | collective-permute-start | bytes 786440 | tf_op jit(solution)/shard_map/ppermute | solution.py:647
  62.7 3.2 %collective-permute-start.13 = (bf16[256,512]{1,0:T(8,128)(2,1)S(1)}, bf16[256,512]{1,0:T(8,128)(2,1)S(1)}, u32[]{:S(2)}, u32[]{:S(2)}) collective-permute-start(bf16[256,512]{1,0:T(8,128)(2,1)S(1)} %get-tuple-element.106), channel_id=1, source_target_pairs={{0,2},{1,3},{2,0},{3,1},{4,6},{5,7},{6,4},{7,5},{8,10},{9,11},{10,... | collective-permute-start | bytes 786440 | tf_op jit(solution)/shard_map/ppermute | solution.py:647
  65.9 8.3 %collective-permute-done.10.refs_1_ = bf16[256,512]{1,0:T(8,128)(2,1)S(1)} collective-permute-done((bf16[256,512]{1,0:T(8,128)(2,1)S(1)}, bf16[256,512]{1,0:T(8,128)(2,1)S(1)}, u32[]{:S(2)}, u32[]{:S(2)}) %collective-permute-start.10) | collective-permute-done | bytes 262176 | tf_op jit(solution)/shard_map/ppermute | solution.py:647
  75.9 1.3 %collective-permute-start.16 = (bf16[48,512]{1,0:T(8,128)(2,1)S(1)}, bf16[48,512]{1,0:T(8,128)(2,1)S(1)}, u32[]{:S(2)}, u32[]{:S(2)}) collective-permute-start(bf16[48,512]{1,0:T(8,128)(2,1)S(1)} %get-tuple-element.113.refs_6_), channel_id=1, source_target_pairs={{0,8},{4,12},{8,0},{12,4},{1,9},{5,13},{9,1},{13,5},{2,10},{6,14},... | collective-permute-start | bytes 147464 | tf_op jit(solution)/shard_map/ppermute | solution.py:647
  78.2 3.5 %collective-permute-done.18 = bf16[2,512,128]{2,1,0:T(8,128)(2,1)S(1)} collective-permute-done((bf16[2,512,128]{2,1,0:T(8,128)(2,1)S(1)}, bf16[2,512,128]{2,1,0:T(8,128)(2,1)S(1)}, u32[]{:S(2)}, u32[]{:S(2)}) %collective-permute-start.18) | collective-permute-done | bytes 262176 | tf_op jit(solution)/shard_map/ppermute | solution.py:647
  82.4 3.0 %collective-permute-start.19 = (bf16[1,512,128]{2,1,0:T(8,128)(2,1)S(1)}, bf16[1,512,128]{2,1,0:T(8,128)(2,1)S(1)}, u32[]{:S(2)}, u32[]{:S(2)}) collective-permute-start(bf16[1,512,128]{2,1,0:T(8,128)(2,1)S(1)} %get-tuple-element.122), channel_id=1, source_target_pairs={{0,2},{1,3},{2,0},{3,1},{4,6},{5,7},{6,4},{7,5},{8,10},{9,11},{10,... | collective-permute-start | bytes 393224 | tf_op jit(solution)/shard_map/ppermute | solution.py:647
  85.4 1.8 %node_outputs.1 = (bf16[256,512]{1,0:T(8,128)(2,1)}, bf16[256,512]{1,0:T(8,128)(2,1)}, f32[8,128]{1,0:T(8,128)S(1)}) custom-call(s32[2]{0:T(128)S(1)} %pad_add_fusion.refs_3_.refs_0_, s32[1,256]{1,0:T(1,128)S(1)} %bitcast.40, bf16[256,512]{1,0:T(8,128)(2,1)S(1)} %copy-done.3, bf16[256,512]{1,0:T(8,128)(2,1)S(1)} %copy-done.6, ...), custom_call_target="tpu_custom_call" | custom-call | flops 2300000000 | bytes 1048576 | tf_op jit(solution)/shard_map/node_outputs/pallas_call | solution.py:83
  87.2 3.0 %collective-permute-done.19 = bf16[1,512,128]{2,1,0:T(8,128)(2,1)S(1)} collective-permute-done((bf16[1,512,128]{2,1,0:T(8,128)(2,1)S(1)}, bf16[1,512,128]{2,1,0:T(8,128)(2,1)S(1)}, u32[]{:S(2)}, u32[]{:S(2)}) %collective-permute-start.19) | collective-permute-done | bytes 131104 | tf_op jit(solution)/shard_map/ppermute | solution.py:647
  (69 shorter events, 15.1 us)
Async XLA Ops:
  0.6 16.3 %collective-permute-start.1 = (bf16[256,512]{1,0:T(8,128)(2,1)}, bf16[256,512]{1,0:T(8,128)(2,1)S(1)}, u32[]{:S(2)}, u32[]{:S(2)}) collective-permute-start(bf16[256,512]{1,0:T(8,128)(2,1)} %refs_2_.3), channel_id=1, source_target_pairs={{0,2},{1,3},{2,0},{3,1},{4,6},{5,7},{6,4},{7,5},{8,10},{9,11},{10,... | collective-permute-start | bytes 786440 | tf_op jit(solution)/shard_map/ppermute | solution.py:647
  4.7 13.0 %collective-permute-start = (bf16[256,512]{1,0:T(8,128)(2,1)}, bf16[256,512]{1,0:T(8,128)(2,1)S(1)}, u32[]{:S(2)}, u32[]{:S(2)}) collective-permute-start(bf16[256,512]{1,0:T(8,128)(2,1)} %refs_2_.3), channel_id=1, source_target_pairs={{0,1},{1,0},{2,3},{3,2},{4,5},{5,4},{6,7},{7,6},{8,9},{9,8},{10,11... | collective-permute-start | bytes 786440 | tf_op jit(solution)/shard_map/ppermute | solution.py:647
  9.8 1.4 %collective-permute-start.2 = (f32[32,1152]{1,0:T(8,128)S(1)}, f32[32,1152]{1,0:T(8,128)S(1)}, u32[]{:S(2)}, u32[]{:S(2)}) collective-permute-start(f32[32,1152]{1,0:T(8,128)S(1)} %get-tuple-element.67), channel_id=1, source_target_pairs={{0,4},{4,0},{8,12},{12,8},{1,5},{5,1},{9,13},{13,9},{2,6},{6,2},{1... | collective-permute-start | bytes 442376 | tf_op jit(solution)/shard_map/ppermute | solution.py:647
  11.2 6.5 %copy-start.1 = (bf16[1536,512]{1,0:T(8,128)(2,1)S(1)}, bf16[1536,512]{1,0:T(8,128)(2,1)}, u32[]{:S(2)}) copy-start(bf16[1536,512]{1,0:T(8,128)(2,1)} %refs_3_.4) | copy-start | bytes 4718596
  11.2 6.5 %copy-start.3 = (bf16[256,512]{1,0:T(8,128)(2,1)S(1)}, bf16[256,512]{1,0:T(8,128)(2,1)}, u32[]{:S(2)}) copy-start(bf16[256,512]{1,0:T(8,128)(2,1)} %refs_2_.3) | copy-start | bytes 786436
  11.2 6.5 %copy-start.7 = (f32[512]{0:T(512)S(1)}, f32[512]{0:T(512)}, u32[]{:S(2)}) copy-start(f32[512]{0:T(512)} %param.17) | copy-start | bytes 6148
  11.2 6.5 %copy-start.10 = (s32[256]{0:T(256)S(1)}, s32[256]{0:T(256)}, u32[]{:S(2)}) copy-start(s32[256]{0:T(256)} %param.15) | copy-start | bytes 3076
  11.8 14.9 %collective-permute-start.6 = (f32[16,1152]{1,0:T(8,128)S(1)}, f32[16,1152]{1,0:T(8,128)S(1)}, u32[]{:S(2)}, u32[]{:S(2)}) collective-permute-start(f32[16,1152]{1,0:T(8,128)S(1)} %bitcast.35), channel_id=1, source_target_pairs={{0,8},{4,12},{8,0},{12,4},{1,9},{5,13},{9,1},{13,5},{2,10},{6,14},... | collective-permute-start | bytes 221192 | tf_op jit(solution)/shard_map/ppermute | solution.py:647
  17.0 7.4 %collective-permute-start.3 = (bf16[256,512]{1,0:T(8,128)(2,1)S(1)}, bf16[256,512]{1,0:T(8,128)(2,1)S(1)}, u32[]{:S(2)}, u32[]{:S(2)}) collective-permute-start(bf16[256,512]{1,0:T(8,128)(2,1)S(1)} %collective-permute-done.1.refs_11_.refs_3_.refs_9_), channel_id=1, source_target_pairs={{0,1},{1,0},{2,3},{3,2},{4,5},{5,4},{6,7},{7,6},{8,9},{9,8},{10,11... | collective-permute-start | bytes 786440 | tf_op jit(solution)/shard_map/ppermute | solution.py:647
  24.9 4.9 %collective-permute-start.4 = (bf16[128,512]{1,0:T(8,128)(2,1)S(1)}, bf16[128,512]{1,0:T(8,128)(2,1)S(1)}, u32[]{:S(2)}, u32[]{:S(2)}) collective-permute-start(bf16[128,512]{1,0:T(8,128)(2,1)S(1)} %get-tuple-element.72), channel_id=1, source_target_pairs={{0,4},{4,8},{8,12},{12,0},{1,5},{5,9},{9,13},{13,1},{2,6},{6,10},{... | collective-permute-start | bytes 393224 | tf_op jit(solution)/shard_map/ppermute | solution.py:749
  25.0 4.9 %collective-permute-start.5 = (bf16[128,512]{1,0:T(8,128)(2,1)S(1)}, bf16[128,512]{1,0:T(8,128)(2,1)S(1)}, u32[]{:S(2)}, u32[]{:S(2)}) collective-permute-start(bf16[128,512]{1,0:T(8,128)(2,1)S(1)} %get-tuple-element.73), channel_id=1, source_target_pairs={{4,0},{8,4},{12,8},{0,12},{5,1},{9,5},{13,9},{1,13},{6,2},{10,6},{... | collective-permute-start | bytes 393224 | tf_op jit(solution)/shard_map/ppermute | solution.py:750
  26.7 15.4 %collective-permute-start.7 = (f32[16,1152]{1,0:T(8,128)S(1)}, f32[16,1152]{1,0:T(8,128)S(1)}, u32[]{:S(2)}, u32[]{:S(2)}) collective-permute-start(f32[16,1152]{1,0:T(8,128)S(1)} %get-tuple-element.81.refs_2_), channel_id=1, source_target_pairs={{0,2},{1,3},{2,0},{3,1},{4,6},{5,7},{6,4},{7,5},{8,10},{9,11},{10,... | collective-permute-start | bytes 221192 | tf_op jit(solution)/shard_map/ppermute | solution.py:647
  42.9 4.4 %collective-permute-start.8 = (bf16[128,512]{1,0:T(8,128)(2,1)S(1)}, bf16[128,512]{1,0:T(8,128)(2,1)S(1)}, u32[]{:S(2)}, u32[]{:S(2)}) collective-permute-start(bf16[128,512]{1,0:T(8,128)(2,1)S(1)} %get-tuple-element.83.refs_6_), channel_id=1, source_target_pairs={{0,4},{4,8},{8,12},{12,0},{1,5},{5,9},{9,13},{13,1},{2,6},{6,10},{... | collective-permute-start | bytes 393224 | tf_op jit(solution)/shard_map/ppermute | solution.py:771
  43.8 4.0 %collective-permute-start.9 = (bf16[128,512]{1,0:T(8,128)(2,1)S(1)}, bf16[128,512]{1,0:T(8,128)(2,1)S(1)}, u32[]{:S(2)}, u32[]{:S(2)}) collective-permute-start(bf16[128,512]{1,0:T(8,128)(2,1)S(1)} %get-tuple-element.84.refs_5_), channel_id=1, source_target_pairs={{4,0},{8,4},{12,8},{0,12},{5,1},{9,5},{13,9},{1,13},{6,2},{10,6},{... | collective-permute-start | bytes 393224 | tf_op jit(solution)/shard_map/ppermute | solution.py:770
  48.5 10.1 %collective-permute-start.12 = (bf16[304,512]{1,0:T(8,128)(2,1)S(1)}, bf16[304,512]{1,0:T(8,128)(2,1)S(1)}, u32[]{:S(2)}, u32[]{:S(2)}) collective-permute-start(bf16[304,512]{1,0:T(8,128)(2,1)S(1)} %get-tuple-element.101.refs_0_), channel_id=1, source_target_pairs={{0,1},{1,0},{2,3},{3,2},{4,5},{5,4},{6,7},{7,6},{8,9},{9,8},{10,11... | collective-permute-start | bytes 933896 | tf_op jit(solution)/shard_map/ppermute | solution.py:647
  54.6 4.0 %collective-permute-start.11 = (bf16[4,2,512,128]{3,2,1,0:T(8,128)(2,1)S(1)}, bf16[4,2,512,128]{3,2,1,0:T(8,128)(2,1)S(1)}, u32[]{:S(2)}, u32[]{:S(2)}) collective-permute-start(bf16[4,2,512,128]{3,2,1,0:T(8,128)(2,1)S(1)} %get-tuple-element.99), channel_id=1, source_target_pairs={{0,4},{4,0},{8,12},{12,8},{1,5},{5,1},{9,13},{13,9},{2,6},{6,2},{1... | collective-permute-start | bytes 3145736 | tf_op jit(solution)/shard_map/ppermute | solution.py:647
  59.3 14.9 %collective-permute-start.14 = (bf16[4,512,128]{2,1,0:T(8,128)(2,1)S(1)}, bf16[4,512,128]{2,1,0:T(8,128)(2,1)S(1)}, u32[]{:S(2)}, u32[]{:S(2)}) collective-permute-start(bf16[4,512,128]{2,1,0:T(8,128)(2,1)S(1)} %get-tuple-element.108), channel_id=1, source_target_pairs={{0,8},{4,12},{8,0},{12,4},{1,9},{5,13},{9,1},{13,5},{2,10},{6,14},... | collective-permute-start | bytes 1572872 | tf_op jit(solution)/shard_map/ppermute | solution.py:647
  61.0 13.2 %collective-permute-start.10 = (bf16[256,512]{1,0:T(8,128)(2,1)S(1)}, bf16[256,512]{1,0:T(8,128)(2,1)S(1)}, u32[]{:S(2)}, u32[]{:S(2)}) collective-permute-start(bf16[256,512]{1,0:T(8,128)(2,1)S(1)} %get-tuple-element.90), channel_id=1, source_target_pairs={{0,1},{1,0},{2,3},{3,2},{4,5},{5,4},{6,7},{7,6},{8,9},{9,8},{10,11... | collective-permute-start | bytes 786440 | tf_op jit(solution)/shard_map/ppermute | solution.py:647
  62.7 15.1 %collective-permute-start.13 = (bf16[256,512]{1,0:T(8,128)(2,1)S(1)}, bf16[256,512]{1,0:T(8,128)(2,1)S(1)}, u32[]{:S(2)}, u32[]{:S(2)}) collective-permute-start(bf16[256,512]{1,0:T(8,128)(2,1)S(1)} %get-tuple-element.106), channel_id=1, source_target_pairs={{0,2},{1,3},{2,0},{3,1},{4,6},{5,7},{6,4},{7,5},{8,10},{9,11},{10,... | collective-permute-start | bytes 786440 | tf_op jit(solution)/shard_map/ppermute | solution.py:647
  74.9 6.9 %collective-permute-start.18 = (bf16[2,512,128]{2,1,0:T(8,128)(2,1)S(1)}, bf16[2,512,128]{2,1,0:T(8,128)(2,1)S(1)}, u32[]{:S(2)}, u32[]{:S(2)}) collective-permute-start(bf16[2,512,128]{2,1,0:T(8,128)(2,1)S(1)} %get-tuple-element.115), channel_id=1, source_target_pairs={{0,1},{1,0},{2,3},{3,2},{4,5},{5,4},{6,7},{7,6},{8,9},{9,8},{10,11... | collective-permute-start | bytes 786440 | tf_op jit(solution)/shard_map/ppermute | solution.py:647
  75.8 9.6 %collective-permute-start.17 = (bf16[48,512]{1,0:T(8,128)(2,1)S(1)}, bf16[48,512]{1,0:T(8,128)(2,1)S(1)}, u32[]{:S(2)}, u32[]{:S(2)}) collective-permute-start(bf16[48,512]{1,0:T(8,128)(2,1)S(1)} %get-tuple-element.113.refs_6_), channel_id=1, source_target_pairs={{0,12},{4,8},{8,4},{12,0},{1,13},{5,9},{9,5},{13,1},{2,14},{6,10},... | collective-permute-start | bytes 147464 | tf_op jit(solution)/shard_map/ppermute | solution.py:647
  75.9 9.5 %collective-permute-start.16 = (bf16[48,512]{1,0:T(8,128)(2,1)S(1)}, bf16[48,512]{1,0:T(8,128)(2,1)S(1)}, u32[]{:S(2)}, u32[]{:S(2)}) collective-permute-start(bf16[48,512]{1,0:T(8,128)(2,1)S(1)} %get-tuple-element.113.refs_6_), channel_id=1, source_target_pairs={{0,8},{4,12},{8,0},{12,4},{1,9},{5,13},{9,1},{13,5},{2,10},{6,14},... | collective-permute-start | bytes 147464 | tf_op jit(solution)/shard_map/ppermute | solution.py:647
  77.2 8.2 %collective-permute-start.15 = (bf16[48,512]{1,0:T(8,128)(2,1)S(1)}, bf16[48,512]{1,0:T(8,128)(2,1)S(1)}, u32[]{:S(2)}, u32[]{:S(2)}) collective-permute-start(bf16[48,512]{1,0:T(8,128)(2,1)S(1)} %get-tuple-element.113.refs_6_), channel_id=1, source_target_pairs={{0,4},{4,0},{8,12},{12,8},{1,5},{5,1},{9,13},{13,9},{2,6},{6,2},{1... | collective-permute-start | bytes 147464 | tf_op jit(solution)/shard_map/ppermute | solution.py:647
  82.4 7.9 %collective-permute-start.19 = (bf16[1,512,128]{2,1,0:T(8,128)(2,1)S(1)}, bf16[1,512,128]{2,1,0:T(8,128)(2,1)S(1)}, u32[]{:S(2)}, u32[]{:S(2)}) collective-permute-start(bf16[1,512,128]{2,1,0:T(8,128)(2,1)S(1)} %get-tuple-element.122), channel_id=1, source_target_pairs={{0,2},{1,3},{2,0},{3,1},{4,6},{5,7},{6,4},{7,5},{8,10},{9,11},{10,... | collective-permute-start | bytes 393224 | tf_op jit(solution)/shard_map/ppermute | solution.py:647
  (9 other events, 20.0 us)
